TPU v7x, 32 devices: a whole 2x2x4 slice. The times are simulated.
32 devices in a mesh: dp: 4 (over y, x), ctx: 8 (over z, core).
Axes of the slice: x: 2, y: 2, z: 4, core: 2. Of those that a mesh axis runs over, the one named last changes fastest.
Arguments:
- queries: bfloat16 [2048, 1024], P('ctx'), may hold values from -12 to 12
- keys: bfloat16 [2048, 128], P('ctx'), may hold values from -5 to 5
- values: bfloat16 [2048, 128], P('ctx'), may hold values from -5 to 5
- out_grad: bfloat16 [2048, 1024], P('ctx'), may hold values from -5 to 5
- segment_ids: int32 [2048], replicated, may hold values from 0 to 3, never falling along the last dimension, each value on 1 to 1792 neighbouring positions
Outputs:
- attn_out: bfloat16 [2048, 1024], P('ctx', 'dp')
- grad_q: bfloat16 [2048, 1024], P('ctx', 'dp')
- grad_k: bfloat16 [2048, 128], P(('dp', 'ctx'))
- grad_v: bfloat16 [2048, 128], P(('dp', 'ctx'))
Inputs may be any that keep to these rules, and one draw needn't show every extreme that they name: `segment_ids`: document numbers never fall along the tokens; each document is a run of positions, the longest exactly 1792.
All inputs are finite; a program needn't handle non-finite values.
Results may differ from a plain program's by a relative error of at most 0.04.
Values may be sent and summed in bfloat16 or wider, within the bound.
No kernel may reach another device: no remote copies, remote signals or barrier semaphores. Data moves between devices by JAX's collectives and lax.ppermute only.
A program may use at most 64 MiB of HBM per device.

v0:
```python
import functools
import math

import jax
import jax.numpy as jnp
from jax import lax
from jax.experimental import pallas as pl
from jax.experimental.pallas import tpu as pltpu
from jax.sharding import PartitionSpec as P

NEG = -1e30
LOG2E = 1.4426950408889634
DOC_NUMBERS = 4
KEY_GROUPS = 2
MIB = 1024 * 1024


def place():
    dp_index, ctx_index = lax.axis_index("dp"), lax.axis_index("ctx")
    return dp_index // KEY_GROUPS, dp_index % KEY_GROUPS, ctx_index // 2, ctx_index % 2

NT = (((1,), (1,)), ((), ()))


def home_chip(spot, key_group, chip, chips):
    level = chips // 4
    flip = spot // level * (2 * level) + spot % level
    home = chip ^ flip
    return home ^ ((home // level % 2) ^ key_group) * level


def gather_rounds(chips):
    rounds = [{} for _ in range(2 if chips == 4 else chips - 1)]
    for core in range(2):
        if chips == 4:
            rounds[0][0, 1, core] = (1, 0)
            rounds[0][0, 2, core] = (0, 0)
            rounds[0][1, 2, core] = (1, 1)
            rounds[0][0, 3, core] = (core, 2)
            rounds[1][0, 3, core] = (0, 0)
            rounds[1][1, 3, core] = (1, 1)
            continue
        for flip, moves in enumerate(rounds, 1):
            for home in range(chips):
                group = home // (chips // 4) % 2
                if home ^ flip > home:
                    moves[group, home ^ flip, core] = (group, home)
    return rounds


def spread_rounds(chips):
    flips = list(range(2, chips)) + [1]
    return [{chip: chip ^ flip for chip in range(chips)} for flip in flips]


def mask_bias(seg_ref, rows, held):
    _, key_group, chip, core = place()
    seg = seg_ref[...]
    lines = rows // 128
    seg_own = seg_ref[pl.ds((chip * 2 + core) * lines, lines), :]
    start = jnp.zeros((lines, 128), jnp.int32)
    for number in range(1, DOC_NUMBERS):
        before = jnp.sum((seg < number).astype(jnp.float32), axis=(0, 1), keepdims=True)
        start = jnp.where(seg_own == number, before.astype(jnp.int32), start)
    start = jnp.concatenate([start[k : k + 1] for k in range(lines)], axis=1)
    query_pos = (chip * 2 + core) * rows + lax.broadcasted_iota(jnp.int32, (1, rows), 1)
    blocks = held // rows
    bias = []
    for block in range(blocks):
        home = home_chip(block // 2, key_group, chip, blocks) * 2 + (core ^ block % 2)
        key_pos = home * rows + lax.broadcasted_iota(jnp.int32, (rows, rows), 0)
        allowed = (key_pos >= start) & (key_pos <= query_pos)
        bias.append(jnp.where(allowed, 0.0, NEG))
    return bias


def load_kernel(k_hbm, v_hbm, kv_ref, sems):
    width = k_hbm.shape[1]
    copies = [
        pltpu.make_async_copy(k_hbm, kv_ref.at[:, :width], sems.at[0]),
        pltpu.make_async_copy(v_hbm, kv_ref.at[:, width:], sems.at[1]),
    ]
    for copy in copies:
        copy.start()
    for copy in copies:
        copy.wait()


def pick_kernel(*refs, choices):
    out_ref = refs[-1]
    _, key_group, chip, _ = place()
    spot = key_group * (len(choices) // 2) + chip
    for choice in sorted(set(choices)):
        wanted = functools.reduce(
            jnp.logical_or, [spot == k for k, c in enumerate(choices) if c == choice]
        )

        @pl.when(wanted)
        def _():
            out_ref[...] = jnp.zeros_like(out_ref) if choice < 0 else refs[choice][...]


def prep_kernel(
    seg_hbm, q_hbm, g_hbm, q_ref, g_ref, gt_ref, bias_ref, token_ref, seg_ref, sems, *, dims
):
    heads, rows, width, held, ctx_count = dims
    head_group = place()[0]
    seg_copy = pltpu.make_async_copy(seg_hbm, seg_ref, sems.at[2, 0])
    seg_copy.start()
    copies = []
    for head in range(heads):
        source = head_columns(head_group * heads + head, width)
        target = slice(head * width, (head + 1) * width)
        for k, (full, part) in enumerate(((g_hbm, g_ref), (q_hbm, q_ref))):
            copies.append(
                pltpu.make_async_copy(full.at[:, source], part.at[:, target], sems.at[k, head])
            )
            copies[-1].start()
    token_ref[...] = jnp.zeros_like(token_ref)
    seg_copy.wait()
    for k, block in enumerate(mask_bias(seg_ref, rows, held)):
        bias_ref[k * rows : (k + 1) * rows, :] = block
    for head in range(heads):
        cols = slice(head * width, (head + 1) * width)
        copies[2 * head].wait()
        gt_ref[cols, :] = g_ref[:, cols].astype(jnp.float32).T.astype(jnp.bfloat16)
    for head in range(heads):
        copies[2 * head + 1].wait()


def head_columns(head, width):
    return pl.ds(pl.multiple_of(head * width, width), width)


def scores_pass(q_ref, bias_ref, blocks, scores_ref, top_ref, *, dims, first):
    heads, rows, width, held, ctx_count = dims
    for head in range(heads):
        query = q_ref[:, head * width : (head + 1) * width]
        top = None
        for k, kv_ref in enumerate(blocks):
            bias = bias_ref[(first + k) * rows : (first + k + 1) * rows, :]
            raw = lax.dot_general(kv_ref[:, :width], query, NT, preferred_element_type=jnp.float32)
            scores = raw * (width**-0.5 * LOG2E) + bias
            scores_ref[head, k * rows : (k + 1) * rows, :] = scores
            here = jnp.max(scores, axis=0, keepdims=True)
            top = here if top is None else jnp.maximum(top, here)
        top_ref[head : head + 1, :] = top


def transpose_values(blocks, vt_ref, width):
    size = blocks[0].shape[0]
    for k, kv_ref in enumerate(blocks):
        vt = kv_ref[:, width:].astype(jnp.float32).T.astype(jnp.bfloat16)
        vt_ref[:, k * size : (k + 1) * size] = vt


def sums_pass(vt_ref, scores_ref, top, head):
    expd = jnp.exp2(scores_ref[head] - top)
    total = jnp.sum(expd, axis=0, keepdims=True)
    sums = jnp.dot(vt_ref[...], expd.astype(jnp.bfloat16), preferred_element_type=jnp.float32)
    return total, sums


def part_kernel(q_ref, bias_ref, *refs, dims):
    heads, rows, width, held, ctx_count = dims
    *blocks, scores_ref, stats_ref, sums_ref, vt_ref = refs
    transpose_values(blocks, vt_ref, width)
    scores_pass(q_ref, bias_ref, blocks, scores_ref, stats_ref, dims=dims, first=0)
    for head in range(heads):
        total, sums_ref[head] = sums_pass(
            vt_ref, scores_ref, stats_ref[head : head + 1, :], head
        )
        stats_ref[heads + head : heads + head + 1, :] = total


def forward_kernel(
    q_ref, gt_ref, bias_ref, kv_ref, part_ref, part_sums_ref, stats_ref, scores_ref, *refs, dims
):
    heads, rows, width, held, ctx_count = dims
    *outs, top_ref, vt_ref, sums_ref = refs
    pair = heads // KEY_GROUPS
    key_group = place()[1]
    transpose_values([kv_ref], vt_ref, width)
    scores_pass(q_ref, bias_ref, [kv_ref], scores_ref, top_ref, dims=dims, first=held // rows - 1)
    for head in range(heads):
        cols = slice(head * width, (head + 1) * width)
        before = part_ref[head : head + 1, :]
        top = jnp.maximum(top_ref[head : head + 1, :], before)
        share = jnp.exp2(before - top)
        total, accum = sums_pass(vt_ref, scores_ref, top, head)
        total = total + share * part_ref[heads + head : heads + head + 1, :]
        accum = accum + share * part_sums_ref[head]
        delta = jnp.sum(accum * gt_ref[cols, :].astype(jnp.float32), axis=0, keepdims=True)
        for row, value in enumerate((top, total, delta)):
            stats_ref[row * heads + head : row * heads + head + 1, :] = value
        sums_ref[cols, :] = accum.astype(jnp.bfloat16)
    for slot, out_ref in enumerate(outs):
        out_ref[...] = sums_ref[head_columns(key_group ^ slot, pair * width), :]


def dprobs_kernel(g_ref, *refs, dims):
    heads, rows, width, held, ctx_count = dims
    *blocks, dprobs_ref = refs
    for head in range(heads):
        grad = g_ref[:, head * width : (head + 1) * width]
        for part, ref in enumerate(blocks):
            dprobs_ref[head, part * rows : (part + 1) * rows, :] = lax.dot_general(
                ref[:, width:], grad, NT, preferred_element_type=jnp.float32
            )


def merged_stats(stats, heads):
    top = functools.reduce(jnp.maximum, [s[:heads] for s in stats])
    shares = [jnp.exp2(s[:heads] - top) for s in stats]
    total = sum(f * s[heads : 2 * heads] for f, s in zip(shares, stats))
    delta = sum(f * s[2 * heads :] for f, s in zip(shares, stats)) / total
    return top, shares, total, delta


def backward_kernel(q_ref, g_ref, *refs, dims, ahead):
    heads, rows, width, held, ctx_count = dims
    parts = held // rows
    blocks, scores, last_scores, refs = refs[:parts], refs[parts], refs[parts + 1], refs[parts + 2 :]
    dprobs_ref, refs = (refs[0], refs[1:]) if ahead else (None, refs)
    stats = refs[:KEY_GROUPS]
    ds_ref, keep_ref, send_ref, acc_ref = refs[KEY_GROUPS:]
    scale = width**-0.5
    top, _, total, delta = merged_stats([s[...] for s in stats], heads)
    lse = top + jnp.log2(total)
    for head in range(heads):
        cols = slice(head * width, (head + 1) * width)
        query, grad = q_ref[:, cols], g_ref[:, cols]
        for part, ref in enumerate(blocks):
            here = slice(part * rows, (part + 1) * rows)
            row = last_scores[head] if part == parts - 1 else scores[head, here, :]
            probs = jnp.exp2(row - lse[head : head + 1])
            if ahead:
                dprobs = dprobs_ref[head, here, :]
            else:
                dprobs = lax.dot_general(
                    ref[:, width:], grad, NT, preferred_element_type=jnp.float32
                )
            dscores = (probs * (dprobs - delta[head : head + 1])).astype(jnp.bfloat16)
            ds_ref[head, here, :] = dscores
            dv = jnp.dot(probs.astype(jnp.bfloat16), grad, preferred_element_type=jnp.float32)
            dk = jnp.dot(dscores, query, preferred_element_type=jnp.float32)
            if head == 0:
                acc_ref[here, :width] = dk
                acc_ref[here, width:] = dv
            else:
                acc_ref[here, :width] += dk
                acc_ref[here, width:] += dv
    head_group, key_group, chip, core = place()
    chips, piece = ctx_count // 2, rows // 4
    level = chips // 4
    for spot in range(2 * chips):
        here = slice(spot * piece, (spot + 1) * piece)
        target = chip ^ (spot % chips)
        group = head_group ^ (spot // chips)
        block = group * (ctx_count // 2) + key_group * (ctx_count // 4) + target // 2
        flip = block // 2 ^ chip
        slot = flip // (2 * level) * level + flip % level
        line = (slot * 2 + (block % 2 ^ core)) * rows
        for ref, side in ((keep_ref, core), (send_ref, 1 - core)):
            mine = pl.ds(pl.multiple_of(line + (target % 2 * 2 + side) * piece, piece), piece)
            ref[here, :width] = (acc_ref[mine, :width] * scale).astype(ref.dtype)
            ref[here, width:] = acc_ref[mine, width:].astype(ref.dtype)


def query_kernel(*refs, dims):
    heads, rows, width, held, ctx_count = dims
    parts = held // rows
    blocks, ds_ref, refs = refs[:parts], refs[parts], refs[parts + 2 :]
    outs, kt_ref = refs[:KEY_GROUPS], refs[KEY_GROUPS]
    pair = heads // KEY_GROUPS
    key_group = place()[1]
    scale = width**-0.5
    for part, ref in enumerate(blocks):
        here = slice(part * rows, (part + 1) * rows)
        kt_ref[:, here] = ref[:, :width].astype(jnp.float32).T.astype(jnp.bfloat16)
    for slot in range(KEY_GROUPS):
        for part in range(pair):
            head = (key_group ^ slot) * pair + part
            dq = jnp.dot(kt_ref[...], ds_ref[head], preferred_element_type=jnp.float32)
            outs[slot][part * width : (part + 1) * width, :] = (dq * scale).astype(jnp.bfloat16)


def join_kernel(keep_ref, got_ref, kept_ref, send_ref):
    half = kept_ref.shape[0]
    kept_ref[...] = keep_ref[:half, :] + got_ref[:half, :].astype(jnp.float32)
    send = keep_ref[half:, :] + got_ref[half:, :].astype(jnp.float32)
    send_ref[...] = send.astype(jnp.bfloat16)


def spread_kernel(keep_ref, got_ref, token_ref, own_ref, *outs, rounds):
    piece = own_ref.shape[0]
    chip = place()[2]
    own_ref[...] = keep_ref[:piece, :] + got_ref[:piece, :].astype(jnp.float32)
    for out_ref, moves in zip(outs, rounds):
        flip = 0
        for source, target in moves.items():
            flip = jnp.where(chip == source, source ^ target, flip)
        mine = pl.ds(pl.multiple_of(flip * piece, piece), piece)
        out_ref[...] = (keep_ref[mine, :] + got_ref[mine, :].astype(jnp.float32)).astype(
            jnp.bfloat16
        )


def add_kernel(first_ref, second_ref, out_ref):
    out_ref[...] = first_ref[...] + second_ref[...].astype(jnp.float32)


def finish_out_kernel(*refs, dims):
    heads, rows, width, held, ctx_count = dims
    stats, outs = refs[:KEY_GROUPS], refs[KEY_GROUPS : 2 * KEY_GROUPS]
    attn_ref, token_ref = refs[2 * KEY_GROUPS :]
    token_ref[...] = jnp.zeros_like(token_ref)
    pair = heads // KEY_GROUPS
    top, shares, total, _ = merged_stats([s[...] for s in stats], heads)
    own = place()[1] * pair
    row = lax.broadcasted_iota(jnp.int32, (heads, 1), 0)
    for part in range(pair):
        here = slice(part * width, (part + 1) * width)

        def pick(array):
            return jnp.sum(jnp.where(row == own + part, array, 0.0), axis=0, keepdims=True)

        joined = sum(o[here, :].astype(jnp.float32) * pick(f) for o, f in zip(outs, shares))
        attn_ref[:, here] = (joined / pick(total)).T.astype(jnp.bfloat16)


def finish_query_kernel(own_ref, got_ref, gq_ref, token_ref):
    total = own_ref[...].astype(jnp.float32) + got_ref[...].astype(jnp.float32)
    gq_ref[...] = total.T.astype(jnp.bfloat16)
    token_ref[...] = jnp.zeros_like(token_ref)


def finish_kernel(token_ref, *refs):
    *terms, gk_ref, gv_ref = refs
    width = gk_ref.shape[1]
    both = sum(r[...].astype(jnp.float32) for r in terms)
    gk_ref[...] = both[:, :width].astype(jnp.bfloat16)
    gv_ref[...] = both[:, width:].astype(jnp.bfloat16)


def on_device(queries, keys, values, out_grad, segment_ids):
    rows = queries.shape[0]
    width = keys.shape[1]
    seq = segment_ids.shape[0]
    dp_count, ctx_count = lax.axis_size("dp"), lax.axis_size("ctx")
    head_groups = dp_count // KEY_GROUPS
    heads = queries.shape[1] // width // head_groups
    pair = heads // KEY_GROUPS
    chips = ctx_count // 2
    held = rows * ctx_count // KEY_GROUPS
    piece = rows // dp_count
    dims = (heads, rows, width, held, ctx_count)
    seg = segment_ids.reshape(seq // 128, 128)
    params = pltpu.CompilerParams(
        vmem_limit_bytes=min(56 * MIB, 12 * MIB + 12 * 4 * held * rows)
    )
    vmem = pl.BlockSpec(memory_space=pltpu.VMEM)
    bf16, f32 = jnp.bfloat16, jnp.float32

    def call(kernel, outs, ins, name, scratch=(), work=0, **static):
        specs = [a[1] if isinstance(a, tuple) else vmem for a in ins]
        arrays = [a[0] if isinstance(a, tuple) else a for a in ins]
        return pl.pallas_call(
            functools.partial(kernel, **static),
            out_shape=[jax.ShapeDtypeStruct(*o) for o in outs],
            in_specs=specs,
            out_specs=[vmem] * len(outs),
            scratch_shapes=list(scratch),
            compiler_params=params,
            cost_estimate=pl.CostEstimate(
                flops=work * 2 * heads * rows * held * width,
                bytes_accessed=sum(math.prod(o[0]) * 2 for o in outs),
                transcendentals=0,
            ),
            name=name,
        )(*arrays)

    def in_hbm(array):
        return pltpu.with_memory_space_constraint(array, pltpu.HBM), pl.BlockSpec(
            memory_space=pltpu.HBM
        )

    def over_dp(array, flip):
        return lax.ppermute(array, "dp", [(d, d ^ flip) for d in range(dp_count)])

    def over_cores(array):
        return lax.ppermute(array, "ctx", [(c, c ^ 1) for c in range(ctx_count)])

    def gathered(array, moves):
        pairs = []
        for d in range(0, dp_count, KEY_GROUPS):
            for (group, chip, core), (source, home) in moves.items():
                start = (d + source) * ctx_count + home * 2 + core
                pairs.append((start, (d + group) * ctx_count + chip * 2 + core))
        return lax.ppermute(array, ("dp", "ctx"), pairs)

    def spread(array, moves):
        pairs = [(a * 2 + core, b * 2 + core) for a, b in moves.items() for core in range(2)]
        return lax.ppermute(array, "ctx", pairs)

    (own_kv,) = call(
        load_kernel,
        [((rows, 2 * width), bf16)],
        [in_hbm(keys), in_hbm(values)],
        "load",
        scratch=[pltpu.SemaphoreType.DMA((2,))],
    )
    query_v, grad_v, grad_t, bias, token = call(
        prep_kernel,
        [
            ((rows, heads * width), bf16),
            ((rows, heads * width), bf16),
            ((heads * width, rows), bf16),
            ((held, rows), f32),
            ((8, 128), f32),
        ],
        [in_hbm(seg), in_hbm(queries), in_hbm(out_grad)],
        "prepare",
        scratch=[pltpu.VMEM(seg.shape, seg.dtype), pltpu.SemaphoreType.DMA((3, heads))],
        work=1,
        dims=dims,
    )
    rounds = gather_rounds(chips)
    sent = [own_kv] + [gathered(own_kv, moves) for moves in rounds]
    blocks = []
    for spot in range(chips // 2):
        choices = []
        for group in range(KEY_GROUPS):
            for chip in range(chips):
                home = home_chip(spot, group, chip, chips)
                spot_key = (group, chip, 0)
                ways = [k for k, m in enumerate(rounds, 1) if m.get(spot_key, (0, -1))[1] == home]
                choices.append(0 if home == chip else ways[0] if home < chip else -1)
        used = sorted(set(choices) - {-1})
        (picked,) = call(
            pick_kernel,
            [((rows, 2 * width), bf16)],
            [sent[k] for k in used] + [token],
            "pick",
            choices=[used.index(c) if c >= 0 else -1 for c in choices],
        )
        blocks += [picked, over_cores(picked)]
    early = held - rows
    scores, part_stats, part_sums = call(
        part_kernel,
        [((heads, early, rows), f32), ((2 * heads, rows), f32), ((heads, width, rows), f32)],
        [query_v, bias] + blocks[:-1],
        "attend_most",
        scratch=[pltpu.VMEM((width, early), bf16)],
        work=2,
        dims=dims,
    )
    stats, last_scores, *outs = call(
        forward_kernel,
        [((3 * heads, rows), f32), ((heads, rows, rows), f32)]
        + [((pair * width, rows), bf16)] * KEY_GROUPS,
        [query_v, grad_t, bias, blocks[-1], part_stats, part_sums],
        "attend",
        scratch=[
            pltpu.VMEM((heads, rows), f32),
            pltpu.VMEM((width, rows), bf16),
            pltpu.VMEM((heads * width, rows), bf16),
        ],
        work=1,
        dims=dims,
    )
    all_stats = [stats, over_dp(stats, 1)]
    all_outs = [outs[0], over_dp(outs[1], 1)]
    ahead = 4 * heads * held * rows <= 8 * MIB
    dprobs = []
    if ahead:
        dprobs = call(
            dprobs_kernel,
            [((heads, held, rows), f32)],
            [grad_v] + blocks,
            "dprobs",
            work=1,
            dims=dims,
        )

    dscores, keep, send = call(
        backward_kernel,
        [
            ((heads, held, rows), bf16),
            ((held // 2, 2 * width), f32),
            ((held // 2, 2 * width), bf16),
        ],
        [query_v, grad_v] + blocks + [scores, last_scores] + list(dprobs) + all_stats,
        "differentiate",
        scratch=[pltpu.VMEM((held, 2 * width), f32)],
        work=4,
        dims=dims,
        ahead=ahead,
    )
    got = over_cores(send)
    attn_out, token = call(
        finish_out_kernel,
        [((rows, pair * width), bf16), ((8, 128), f32)],
        all_stats + all_outs,
        "finish_out",
        dims=dims,
    )
    quarter = held // 4
    keep, send = call(
        join_kernel,
        [((quarter, 2 * width), f32), ((quarter, 2 * width), bf16)],
        [keep, got],
        "join_cores",
    )
    dqs = call(
        query_kernel,
        [((pair * width, rows), bf16)] * KEY_GROUPS,
        blocks + [dscores, keep],
        "query_terms",
        scratch=[pltpu.VMEM((width, held), bf16)],
        work=1,
        dims=dims,
    )
    all_dqs = [dqs[0], over_dp(dqs[1], 1)]
    rounds = spread_rounds(chips)
    terms, *pieces = call(
        spread_kernel,
        [((piece, 2 * width), f32)] + [((piece, 2 * width), bf16)] * len(rounds),
        [keep, over_dp(send, 2), token],
        "join_heads",
        rounds=rounds,
    )
    grad_q, token = call(
        finish_query_kernel,
        [((rows, pair * width), bf16), ((8, 128), f32)],
        all_dqs,
        "finish_query",
    )
    got = [spread(p, moves) for p, moves in zip(pieces, rounds)]
    for array in got[:-1]:
        (terms,) = call(add_kernel, [((piece, 2 * width), f32)], [terms, array], "add_terms")
    grad_k, grad_values = call(
        finish_kernel, [((piece, width), bf16)] * 2, [token, terms, got[-1]], "finish"
    )
    return attn_out, grad_q, grad_k, grad_values


def solution(mesh):
    return jax.shard_map(
        on_device,
        mesh=mesh,
        in_specs=(P("ctx", None), P("ctx", None), P("ctx", None), P("ctx", None), P()),
        out_specs=(P("ctx", "dp"), P("ctx", "dp"), P(("dp", "ctx"), None), P(("dp", "ctx"), None)),
        check_vma=False,
    )
```

profile of v0, /device:TPU:0, one launch (start us, length us, event | category | flops | bytes accessed | tf_op | source)
XLA Modules:
  0.0 36.8 jit_solution(5961298758948291754)
XLA Ops:
  0.6 0.9 %load.1.refs_0_ = bf16[256,256]{1,0:T(8,128)(2,1)S(1)} custom-call(bf16[256,128]{1,0:T(8,128)(2,1)} %k_hbm.1, bf16[256,128]{1,0:T(8,128)(2,1)} %v_hbm.1), custom_call_target="tpu_custom_call" | custom-call | bytes 131072 | tf_op jit(solution)/shard_map/load/pallas_call | solution.py:368
  1.5 5.9 %collective-permute-start = (bf16[256,256]{1,0:T(8,128)(2,1)S(1)}, bf16[256,256]{1,0:T(8,128)(2,1)S(1)}, u32[]{:S(2)}, u32[]{:S(2)}) collective-permute-start(bf16[256,256]{1,0:T(8,128)(2,1)S(1)} %load.1.refs_0_), channel_id=1, source_target_pairs={{8,2},{0,4},{10,12},{4,6},{9,3},{1,5},{11,13},{13,7},{24,18},{16,2... | collective-permute-start | bytes 393224 | tf_op jit(solution)/shard_map/ppermute | solution.py:400
  7.5 2.3 %collective-permute-start.1 = (bf16[256,256]{1,0:T(8,128)(2,1)S(1)}, bf16[256,256]{1,0:T(8,128)(2,1)S(1)}, u32[]{:S(2)}, u32[]{:S(2)}) collective-permute-start(bf16[256,256]{1,0:T(8,128)(2,1)S(1)} %load.1.refs_0_), channel_id=1, source_target_pairs={{0,6},{10,14},{1,7},{11,15},{16,22},{26,30},{17,23},{27,31}} | collective-permute-start | bytes 393224 | tf_op jit(solution)/shard_map/ppermute | solution.py:400
  9.8 1.5 %prepare.1 = (bf16[256,512]{1,0:T(8,128)(2,1)S(1)}, bf16[256,512]{1,0:T(8,128)(2,1)S(1)}, bf16[512,256]{1,0:T(8,128)(2,1)S(1)}, f32[1024,256]{1,0:T(8,128)S(1)}, f32[8,128]{1,0:T(8,128)S(1)}) custom-call(s32[16,128]{1,0:T(8,128)} %bitcast.1, bf16[256,1024]{1,0:T(8,128)(2,1)} %q_hbm.1, bf16[256,1024]{1,0:T(8,128)(2,1)} %g_hbm.1), custom_call_target="tpu_custom_call" | custom-call | flops 268435456 | bytes 1312768 | tf_op jit(solution)/shard_map/prepare/pallas_call | solution.py:368
  11.3 0.0 collective-permute-done.refs_0_.refs_1_
  11.4 0.1 collective-permute-start.3
  11.4 1.6 %collective-permute-done.1.refs_1_ = bf16[256,256]{1,0:T(8,128)(2,1)S(1)} collective-permute-done((bf16[256,256]{1,0:T(8,128)(2,1)S(1)}, bf16[256,256]{1,0:T(8,128)(2,1)S(1)}, u32[]{:S(2)}, u32[]{:S(2)}) %collective-permute-start.1) | collective-permute-done | bytes 131104 | tf_op jit(solution)/shard_map/ppermute | solution.py:400
  13.0 0.1 collective-permute-start.2
  13.1 0.0 collective-permute-done.3.refs_1_
  13.1 1.2 %attend_most.1 = (f32[4,768,256]{2,1,0:T(8,128)S(1)}, f32[8,256]{1,0:T(8,128)S(1)}, f32[4,128,256]{2,1,0:T(8,128)S(1)}) custom-call(bf16[256,512]{1,0:T(8,128)(2,1)S(1)} %get-tuple-element.33.q_ref, f32[1024,256]{1,0:T(8,128)S(1)} %get-tuple-element.35.bias_ref, bf16[256,256]{1,0:T(8,128)(2,1)S(1)} %pick.3.refs_0_, ...), custom_call_target="tpu_custom_call" | custom-call | flops 536870912 | bytes 1839104 | tf_op jit(solution)/shard_map/attend_most/pallas_call | solution.py:368
  14.3 0.1 collective-permute-done.2.kv_ref.refs_3_
  14.5 0.7 %attend.1 = (f32[12,256]{1,0:T(8,128)S(1)}, f32[4,256,256]{2,1,0:T(8,128)S(1)}, bf16[256,256]{1,0:T(8,128)(2,1)S(1)}, bf16[256,256]{1,0:T(8,128)(2,1)S(1)}) custom-call(bf16[256,512]{1,0:T(8,128)(2,1)S(1)} %get-tuple-element.33.q_ref, bf16[512,256]{1,0:T(8,128)(2,1)S(1)} %get-tuple-element.34.gt_ref, f32[1024,256]{1,0:T(8,128)S(1)} %get-tuple-element.35.bias_ref, ...), custom_call_target="tpu_custom_call" | custom-call | flops 268435456 | bytes 792576 | tf_op jit(solution)/shard_map/attend/pallas_call | solution.py:368
  15.2 0.1 collective-permute-start.4
  15.2 0.7 %dprobs.1.refs_6_ = f32[4,1024,256]{2,1,0:T(8,128)S(1)} custom-call(bf16[256,512]{1,0:T(8,128)(2,1)S(1)} %get-tuple-element.43.g_ref, bf16[256,256]{1,0:T(8,128)(2,1)S(1)} %pick.3.refs_0_, bf16[256,256]{1,0:T(8,128)(2,1)S(1)} %collective-permute-done.3.refs_1_, bf16[256,256]{1,0:T(8,128)(2,1)S(1)} %pick.2.refs_2_, ...), custom_call_target="tpu_custom_call" | custom-call | flops 268435456 | bytes 2097152 | tf_op jit(solution)/shard_map/dprobs/pallas_call | solution.py:368
  16.0 3.0 %collective-permute-done.4.refs_1_.refs_8_ = f32[12,256]{1,0:T(8,128)S(1)} collective-permute-done((f32[12,256]{1,0:T(8,128)S(1)}, f32[12,256]{1,0:T(8,128)S(1)}, u32[]{:S(2)}, u32[]{:S(2)}) %collective-permute-start.4) | collective-permute-done | bytes 12320 | tf_op jit(solution)/shard_map/ppermute | solution.py:389
  19.0 1.6 %differentiate.1 = (bf16[4,1024,256]{2,1,0:T(8,128)(2,1)S(1)}, f32[512,256]{1,0:T(8,128)S(1)}, bf16[512,256]{1,0:T(8,128)(2,1)S(1)}) custom-call(bf16[256,512]{1,0:T(8,128)(2,1)S(1)} %get-tuple-element.33.q_ref, bf16[256,512]{1,0:T(8,128)(2,1)S(1)} %get-tuple-element.43.g_ref, bf16[256,256]{1,0:T(8,128)(2,1)S(1)} %pick.3.refs_0_, ...), custom_call_target="tpu_custom_call" | custom-call | flops 1073741824 | bytes 2621440 | tf_op jit(solution)/shard_map/differentiate/pallas_call | solution.py:368
  20.6 0.1 collective-permute-start.6
  20.7 0.1 collective-permute-start.5
  20.7 1.4 %collective-permute-done.6.got_ref = bf16[512,256]{1,0:T(8,128)(2,1)S(1)} collective-permute-done((bf16[512,256]{1,0:T(8,128)(2,1)S(1)}, bf16[512,256]{1,0:T(8,128)(2,1)S(1)}, u32[]{:S(2)}, u32[]{:S(2)}) %collective-permute-start.6) | collective-permute-done | bytes 262176 | tf_op jit(solution)/shard_map/ppermute | solution.py:392
  22.2 1.6 %collective-permute-start.8 = (bf16[256,256]{1,0:T(8,128)(2,1)S(1)}, bf16[256,256]{1,0:T(8,128)(2,1)S(1)}, u32[]{:S(2)}, u32[]{:S(2)}) collective-permute-start(bf16[256,256]{1,0:T(8,128)(2,1)S(1)} %get-tuple-element.54), channel_id=1, source_target_pairs={{0,16},{8,24},{16,0},{24,8},{1,17},{9,25},{17,1},{25,9},{2,18},{10... | collective-permute-start | bytes 393224 | tf_op jit(solution)/shard_map/ppermute | solution.py:389
  23.8 0.5 %query_terms.1 = (bf16[256,256]{1,0:T(8,128)(2,1)S(1)}, bf16[256,256]{1,0:T(8,128)(2,1)S(1)}) custom-call(bf16[256,256]{1,0:T(8,128)(2,1)S(1)} %pick.3.refs_0_, bf16[256,256]{1,0:T(8,128)(2,1)S(1)} %collective-permute-done.3.refs_1_, bf16[256,256]{1,0:T(8,128)(2,1)S(1)} %pick.2.refs_2_, bf16[256,256]{1,0:T(8,128)(2,1)S(1)} %collective-permute-done.2.kv_ref.refs_3_, ...), custom_call_target="tpu_custom_call" | custom-call | flops 268435456 | bytes 262144 | tf_op jit(solution)/shard_map/query_terms/pallas_call | solution.py:368
  24.3 0.6 %collective-permute-start.7 = (bf16[256,256]{1,0:T(8,128)(2,1)S(1)}, bf16[256,256]{1,0:T(8,128)(2,1)S(1)}, u32[]{:S(2)}, u32[]{:S(2)}) collective-permute-start(bf16[256,256]{1,0:T(8,128)(2,1)S(1)} %get-tuple-element.51), channel_id=1, source_target_pairs={{0,8},{8,0},{16,24},{24,16},{1,9},{9,1},{17,25},{25,17},{2,10},{10... | collective-permute-start | bytes 393224 | tf_op jit(solution)/shard_map/ppermute | solution.py:389
  24.9 1.6 %collective-permute-done.5.refs_3_ = bf16[256,256]{1,0:T(8,128)(2,1)S(1)} collective-permute-done((bf16[256,256]{1,0:T(8,128)(2,1)S(1)}, bf16[256,256]{1,0:T(8,128)(2,1)S(1)}, u32[]{:S(2)}, u32[]{:S(2)}) %collective-permute-start.5) | collective-permute-done | bytes 131104 | tf_op jit(solution)/shard_map/ppermute | solution.py:389
  26.6 0.8 %finish_out.1 = (bf16[256,256]{1,0:T(8,128)(2,1)}, f32[8,128]{1,0:T(8,128)S(1)}) custom-call(f32[12,256]{1,0:T(8,128)S(1)} %get-tuple-element.39.refs_0_.refs_7_, f32[12,256]{1,0:T(8,128)S(1)} %collective-permute-done.4.refs_1_.refs_8_, bf16[256,256]{1,0:T(8,128)(2,1)S(1)} %get-tuple-element.40.refs_2_, bf16[256,256]{1,0:T(8,128)(2,1)S(1)} %collective-permute-done.5.refs_3_), custom_call_target="tpu_custom_call" | custom-call | bytes 133120 | tf_op jit(solution)/shard_map/finish_out/pallas_call | solution.py:368
  27.4 0.4 %collective-permute-done.8.got_ref = bf16[256,256]{1,0:T(8,128)(2,1)S(1)} collective-permute-done((bf16[256,256]{1,0:T(8,128)(2,1)S(1)}, bf16[256,256]{1,0:T(8,128)(2,1)S(1)}, u32[]{:S(2)}, u32[]{:S(2)}) %collective-permute-start.8) | collective-permute-done | bytes 131104 | tf_op jit(solution)/shard_map/ppermute | solution.py:389
  27.9 2.3 %collective-permute-start.9 = (bf16[64,256]{1,0:T(8,128)(2,1)S(1)}, bf16[64,256]{1,0:T(8,128)(2,1)S(1)}, u32[]{:S(2)}, u32[]{:S(2)}) collective-permute-start(bf16[64,256]{1,0:T(8,128)(2,1)S(1)} %get-tuple-element.57), channel_id=1, source_target_pairs={{0,4},{1,5},{2,6},{3,7},{4,0},{5,1},{6,2},{7,3},{8,12},{9,13},{10,... | collective-permute-start | bytes 98312 | tf_op jit(solution)/shard_map/ppermute | solution.py:404
  30.1 2.1 %collective-permute-start.10 = (bf16[64,256]{1,0:T(8,128)(2,1)S(1)}, bf16[64,256]{1,0:T(8,128)(2,1)S(1)}, u32[]{:S(2)}, u32[]{:S(2)}) collective-permute-start(bf16[64,256]{1,0:T(8,128)(2,1)S(1)} %get-tuple-element.58), channel_id=1, source_target_pairs={{0,6},{1,7},{2,4},{3,5},{4,2},{5,3},{6,0},{7,1},{8,14},{9,15},{10,... | collective-permute-start | bytes 98312 | tf_op jit(solution)/shard_map/ppermute | solution.py:404
  32.3 0.5 %collective-permute-start.11 = (bf16[64,256]{1,0:T(8,128)(2,1)S(1)}, bf16[64,256]{1,0:T(8,128)(2,1)S(1)}, u32[]{:S(2)}, u32[]{:S(2)}) collective-permute-start(bf16[64,256]{1,0:T(8,128)(2,1)S(1)} %get-tuple-element.59), channel_id=1, source_target_pairs={{0,2},{1,3},{2,0},{3,1},{4,6},{5,7},{6,4},{7,5},{8,10},{9,11},{10,... | collective-permute-start | bytes 98312 | tf_op jit(solution)/shard_map/ppermute | solution.py:404
  32.8 0.0 collective-permute-done.7.got_ref
  32.8 0.8 %finish_query.1 = (bf16[256,256]{1,0:T(8,128)(2,1)}, f32[8,128]{1,0:T(8,128)S(1)}) custom-call(bf16[256,256]{1,0:T(8,128)(2,1)S(1)} %get-tuple-element.50.own_ref, bf16[256,256]{1,0:T(8,128)(2,1)S(1)} %collective-permute-done.7.got_ref), custom_call_target="tpu_custom_call" | custom-call | bytes 133120 | tf_op jit(solution)/shard_map/finish_query/pallas_call | solution.py:368
  33.5 0.0 collective-permute-done.9.second_ref
  33.6 2.3 %collective-permute-done.10.second_ref = bf16[64,256]{1,0:T(8,128)(2,1)S(1)} collective-permute-done((bf16[64,256]{1,0:T(8,128)(2,1)S(1)}, bf16[64,256]{1,0:T(8,128)(2,1)S(1)}, u32[]{:S(2)}, u32[]{:S(2)}) %collective-permute-start.10) | collective-permute-done | bytes 32800 | tf_op jit(solution)/shard_map/ppermute | solution.py:404
  35.9 0.3 collective-permute-done.11.refs_1_
  36.2 0.6 %finish.1 = (bf16[64,128]{1,0:T(8,128)(2,1)}, bf16[64,128]{1,0:T(8,128)(2,1)}) custom-call(f32[8,128]{1,0:T(8,128)S(1)} %get-tuple-element.53.token_ref, f32[64,256]{1,0:T(8,128)S(1)} %add_terms.3.refs_0_, bf16[64,256]{1,0:T(8,128)(2,1)S(1)} %collective-permute-done.11.refs_1_), custom_call_target="tpu_custom_call" | custom-call | bytes 32768 | tf_op jit(solution)/shard_map/finish/pallas_call | solution.py:368
  (6 shorter events, 0.2 us)
Async XLA Ops:
  1.5 9.8 %collective-permute-start = (bf16[256,256]{1,0:T(8,128)(2,1)S(1)}, bf16[256,256]{1,0:T(8,128)(2,1)S(1)}, u32[]{:S(2)}, u32[]{:S(2)}) collective-permute-start(bf16[256,256]{1,0:T(8,128)(2,1)S(1)} %load.1.refs_0_), channel_id=1, source_target_pairs={{8,2},{0,4},{10,12},{4,6},{9,3},{1,5},{11,13},{13,7},{24,18},{16,2... | collective-permute-start | bytes 393224 | tf_op jit(solution)/shard_map/ppermute | solution.py:400
  7.5 5.5 %collective-permute-start.1 = (bf16[256,256]{1,0:T(8,128)(2,1)S(1)}, bf16[256,256]{1,0:T(8,128)(2,1)S(1)}, u32[]{:S(2)}, u32[]{:S(2)}) collective-permute-start(bf16[256,256]{1,0:T(8,128)(2,1)S(1)} %load.1.refs_0_), channel_id=1, source_target_pairs={{0,6},{10,14},{1,7},{11,15},{16,22},{26,30},{17,23},{27,31}} | collective-permute-start | bytes 393224 | tf_op jit(solution)/shard_map/ppermute | solution.py:400
  11.4 1.8 %collective-permute-start.3 = (bf16[256,256]{1,0:T(8,128)(2,1)S(1)}, bf16[256,256]{1,0:T(8,128)(2,1)S(1)}, u32[]{:S(2)}, u32[]{:S(2)}) collective-permute-start(bf16[256,256]{1,0:T(8,128)(2,1)S(1)} %pick.3.refs_0_), channel_id=1, source_target_pairs={{0,1},{1,0},{2,3},{3,2},{4,5},{5,4},{6,7},{7,6},{8,9},{9,8},{10,11... | collective-permute-start | bytes 393224 | tf_op jit(solution)/shard_map/ppermute | solution.py:392
  13.0 1.4 %collective-permute-start.2 = (bf16[256,256]{1,0:T(8,128)(2,1)S(1)}, bf16[256,256]{1,0:T(8,128)(2,1)S(1)}, u32[]{:S(2)}, u32[]{:S(2)}) collective-permute-start(bf16[256,256]{1,0:T(8,128)(2,1)S(1)} %pick.2.refs_2_), channel_id=1, source_target_pairs={{0,1},{1,0},{2,3},{3,2},{4,5},{5,4},{6,7},{7,6},{8,9},{9,8},{10,11... | collective-permute-start | bytes 393224 | tf_op jit(solution)/shard_map/ppermute | solution.py:392
  15.2 3.8 %collective-permute-start.4 = (f32[12,256]{1,0:T(8,128)S(1)}, f32[12,256]{1,0:T(8,128)S(1)}, u32[]{:S(2)}, u32[]{:S(2)}) collective-permute-start(f32[12,256]{1,0:T(8,128)S(1)} %get-tuple-element.39.refs_0_.refs_7_), channel_id=1, source_target_pairs={{0,8},{8,0},{16,24},{24,16},{1,9},{9,1},{17,25},{25,17},{2,10},{10... | collective-permute-start | bytes 36872 | tf_op jit(solution)/shard_map/ppermute | solution.py:389
  20.6 1.6 %collective-permute-start.6 = (bf16[512,256]{1,0:T(8,128)(2,1)S(1)}, bf16[512,256]{1,0:T(8,128)(2,1)S(1)}, u32[]{:S(2)}, u32[]{:S(2)}) collective-permute-start(bf16[512,256]{1,0:T(8,128)(2,1)S(1)} %get-tuple-element.48), channel_id=1, source_target_pairs={{0,1},{1,0},{2,3},{3,2},{4,5},{5,4},{6,7},{7,6},{8,9},{9,8},{10,11... | collective-permute-start | bytes 786440 | tf_op jit(solution)/shard_map/ppermute | solution.py:392
  20.7 5.9 %collective-permute-start.5 = (bf16[256,256]{1,0:T(8,128)(2,1)S(1)}, bf16[256,256]{1,0:T(8,128)(2,1)S(1)}, u32[]{:S(2)}, u32[]{:S(2)}) collective-permute-start(bf16[256,256]{1,0:T(8,128)(2,1)S(1)} %get-tuple-element.41), channel_id=1, source_target_pairs={{0,8},{8,0},{16,24},{24,16},{1,9},{9,1},{17,25},{25,17},{2,10},{10... | collective-permute-start | bytes 393224 | tf_op jit(solution)/shard_map/ppermute | solution.py:389
  22.2 5.6 %collective-permute-start.8 = (bf16[256,256]{1,0:T(8,128)(2,1)S(1)}, bf16[256,256]{1,0:T(8,128)(2,1)S(1)}, u32[]{:S(2)}, u32[]{:S(2)}) collective-permute-start(bf16[256,256]{1,0:T(8,128)(2,1)S(1)} %get-tuple-element.54), channel_id=1, source_target_pairs={{0,16},{8,24},{16,0},{24,8},{1,17},{9,25},{17,1},{25,9},{2,18},{10... | collective-permute-start | bytes 393224 | tf_op jit(solution)/shard_map/ppermute | solution.py:389
  24.3 8.5 %collective-permute-start.7 = (bf16[256,256]{1,0:T(8,128)(2,1)S(1)}, bf16[256,256]{1,0:T(8,128)(2,1)S(1)}, u32[]{:S(2)}, u32[]{:S(2)}) collective-permute-start(bf16[256,256]{1,0:T(8,128)(2,1)S(1)} %get-tuple-element.51), channel_id=1, source_target_pairs={{0,8},{8,0},{16,24},{24,16},{1,9},{9,1},{17,25},{25,17},{2,10},{10... | collective-permute-start | bytes 393224 | tf_op jit(solution)/shard_map/ppermute | solution.py:389
  27.9 5.7 %collective-permute-start.9 = (bf16[64,256]{1,0:T(8,128)(2,1)S(1)}, bf16[64,256]{1,0:T(8,128)(2,1)S(1)}, u32[]{:S(2)}, u32[]{:S(2)}) collective-permute-start(bf16[64,256]{1,0:T(8,128)(2,1)S(1)} %get-tuple-element.57), channel_id=1, source_target_pairs={{0,4},{1,5},{2,6},{3,7},{4,0},{5,1},{6,2},{7,3},{8,12},{9,13},{10,... | collective-permute-start | bytes 98312 | tf_op jit(solution)/shard_map/ppermute | solution.py:404
  30.1 5.7 %collective-permute-start.10 = (bf16[64,256]{1,0:T(8,128)(2,1)S(1)}, bf16[64,256]{1,0:T(8,128)(2,1)S(1)}, u32[]{:S(2)}, u32[]{:S(2)}) collective-permute-start(bf16[64,256]{1,0:T(8,128)(2,1)S(1)} %get-tuple-element.58), channel_id=1, source_target_pairs={{0,6},{1,7},{2,4},{3,5},{4,2},{5,3},{6,0},{7,1},{8,14},{9,15},{10,... | collective-permute-start | bytes 98312 | tf_op jit(solution)/shard_map/ppermute | solution.py:404
  32.3 3.9 %collective-permute-start.11 = (bf16[64,256]{1,0:T(8,128)(2,1)S(1)}, bf16[64,256]{1,0:T(8,128)(2,1)S(1)}, u32[]{:S(2)}, u32[]{:S(2)}) collective-permute-start(bf16[64,256]{1,0:T(8,128)(2,1)S(1)} %get-tuple-element.59), channel_id=1, source_target_pairs={{0,2},{1,3},{2,0},{3,1},{4,6},{5,7},{6,4},{7,5},{8,10},{9,11},{10,... | collective-permute-start | bytes 98312 | tf_op jit(solution)/shard_map/ppermute | solution.py:404
where the time goes:
time: 37.1 us; the launch traced here: 36.8 us
  starting transfers between devices  15.7 us (42%)
  waiting for transfers between devices  10.9 us (29%)
  Pallas kernels  9.4 us (25%)
  between operations  0.79 us (2%)
    pallas_call x16, Pallas kernels, call(): pl.pallas_call(functools.partial(kernel, **static), out_shape=[jax.ShapeD...  9.4 us
    ppermute x2, starting transfers between devices, gathered(): return lax.ppermute(array, ('dp', 'ctx'), pairs)  8.25 us
    ppermute x4, waiting for transfers between devices, over_dp(): return lax.ppermute(array, 'dp', [(d, d ^ flip) for d in range(dp_count)])  5.1 us
    ppermute x3, starting transfers between devices, spread(): return lax.ppermute(array, 'ctx', pairs)  4.9 us
    ppermute x3, waiting for transfers between devices, spread(): return lax.ppermute(array, 'ctx', pairs)  2.66 us
    ppermute x4, starting transfers between devices, over_dp(): return lax.ppermute(array, 'dp', [(d, d ^ flip) for d in range(dp_count)])  2.37 us
    ppermute x3, waiting for transfers between devices, over_cores(): return lax.ppermute(array, 'ctx', [(c, c ^ 1) for c in range(ctx_count)])  1.58 us
    ppermute x2, waiting for transfers between devices, gathered(): return lax.ppermute(array, ('dp', 'ctx'), pairs)  1.58 us
  transfers between devices with their start and end apart: 12, of which 8 were waited for; matrix products, arithmetic and copies ran while one was open for 0% of the time, Pallas kernels for 15%

commit v1 on v0

--- a/solution.py
+++ b/solution.py
@@ -65,21 +65,36 @@
     start = jnp.concatenate([start[k : k + 1] for k in range(lines)], axis=1)
     query_pos = (chip * 2 + core) * rows + lax.broadcasted_iota(jnp.int32, (1, rows), 1)
     blocks = held // rows
+    size = rows // 4
+    line = lax.broadcasted_iota(jnp.int32, (rows, rows), 0)
+    place_of = line // size
+    row = (place_of % 2 * 2 + place_of // 2) * size + line % size
     bias = []
     for block in range(blocks):
         home = home_chip(block // 2, key_group, chip, blocks) * 2 + (core ^ block % 2)
-        key_pos = home * rows + lax.broadcasted_iota(jnp.int32, (rows, rows), 0)
+        key_pos = home * rows + row
         allowed = (key_pos >= start) & (key_pos <= query_pos)
         bias.append(jnp.where(allowed, 0.0, NEG))
     return bias
 
 
-def load_kernel(k_hbm, v_hbm, kv_ref, sems):
-    width = k_hbm.shape[1]
-    copies = [
-        pltpu.make_async_copy(k_hbm, kv_ref.at[:, :width], sems.at[0]),
-        pltpu.make_async_copy(v_hbm, kv_ref.at[:, width:], sems.at[1]),
-    ]
+def row_order(pieces):
+    return list(range(0, pieces, 2)) + list(range(1, pieces, 2))
+
+
+def load_kernel(k_hbm, v_hbm, kv_ref, sems, *, pieces):
+    rows, width = k_hbm.shape
+    size = rows // pieces
+    copies = []
+    for spot, piece in enumerate(row_order(pieces)):
+        source, target = (slice(k * size, (k + 1) * size) for k in (piece, spot))
+        for k, array in enumerate((k_hbm, v_hbm)):
+            columns = slice(k * width, (k + 1) * width)
+            copies.append(
+                pltpu.make_async_copy(
+                    array.at[source, :], kv_ref.at[target, columns], sems.at[k, spot]
+                )
+            )
     for copy in copies:
         copy.start()
     for copy in copies:
@@ -217,13 +232,19 @@
     return top, shares, total, delta
 
 
-def backward_kernel(q_ref, g_ref, *refs, dims, ahead):
-    heads, rows, width, held, ctx_count = dims
-    parts = held // rows
+def core_rows(base, side, half):
+    return pl.ds(pl.multiple_of(base + side * half, half), half)
+
+
+def backward_kernel(q_ref, g_ref, *refs, dims, ahead, own):
+    heads, rows, width, held, ctx_count = dims
+    parts, half = held // rows, rows // 2
     blocks, scores, last_scores, refs = refs[:parts], refs[parts], refs[parts + 1], refs[parts + 2 :]
     dprobs_ref, refs = (refs[0], refs[1:]) if ahead else (None, refs)
     stats = refs[:KEY_GROUPS]
-    ds_ref, keep_ref, send_ref, acc_ref = refs[KEY_GROUPS:]
+    ds_ref, terms_ref, acc_ref = refs[-3:]
+    head_group, key_group, chip, core = place()
+    side = core if own else 1 - core
     scale = width**-0.5
     top, _, total, delta = merged_stats([s[...] for s in stats], heads)
     lse = top + jnp.log2(total)
@@ -231,16 +252,20 @@
         cols = slice(head * width, (head + 1) * width)
         query, grad = q_ref[:, cols], g_ref[:, cols]
         for part, ref in enumerate(blocks):
-            here = slice(part * rows, (part + 1) * rows)
-            row = last_scores[head] if part == parts - 1 else scores[head, here, :]
+            held_rows, block_rows = core_rows(part * rows, side, half), core_rows(0, side, half)
+            if part == parts - 1:
+                row = last_scores[head, block_rows, :]
+            else:
+                row = scores[head, held_rows, :]
             probs = jnp.exp2(row - lse[head : head + 1])
             if ahead:
-                dprobs = dprobs_ref[head, here, :]
+                dprobs = dprobs_ref[head, held_rows, :]
             else:
                 dprobs = lax.dot_general(
-                    ref[:, width:], grad, NT, preferred_element_type=jnp.float32
+                    ref[block_rows, width:], grad, NT, preferred_element_type=jnp.float32
                 )
             dscores = (probs * (dprobs - delta[head : head + 1])).astype(jnp.bfloat16)
+            here = slice(part * half, (part + 1) * half)
             ds_ref[head, here, :] = dscores
             dv = jnp.dot(probs.astype(jnp.bfloat16), grad, preferred_element_type=jnp.float32)
             dk = jnp.dot(dscores, query, preferred_element_type=jnp.float32)
@@ -250,7 +275,6 @@
             else:
                 acc_ref[here, :width] += dk
                 acc_ref[here, width:] += dv
-    head_group, key_group, chip, core = place()
     chips, piece = ctx_count // 2, rows // 4
     level = chips // 4
     for spot in range(2 * chips):
@@ -260,28 +284,31 @@
         block = group * (ctx_count // 2) + key_group * (ctx_count // 4) + target // 2
         flip = block // 2 ^ chip
         slot = flip // (2 * level) * level + flip % level
-        line = (slot * 2 + (block % 2 ^ core)) * rows
-        for ref, side in ((keep_ref, core), (send_ref, 1 - core)):
-            mine = pl.ds(pl.multiple_of(line + (target % 2 * 2 + side) * piece, piece), piece)
-            ref[here, :width] = (acc_ref[mine, :width] * scale).astype(ref.dtype)
-            ref[here, width:] = acc_ref[mine, width:].astype(ref.dtype)
+        line = (slot * 2 + (block % 2 ^ core)) * half + target % 2 * piece
+        mine = pl.ds(pl.multiple_of(line, piece), piece)
+        terms_ref[here, :width] = (acc_ref[mine, :width] * scale).astype(terms_ref.dtype)
+        terms_ref[here, width:] = acc_ref[mine, width:].astype(terms_ref.dtype)
 
 
 def query_kernel(*refs, dims):
     heads, rows, width, held, ctx_count = dims
-    parts = held // rows
-    blocks, ds_ref, refs = refs[:parts], refs[parts], refs[parts + 2 :]
-    outs, kt_ref = refs[:KEY_GROUPS], refs[KEY_GROUPS]
+    parts, half = held // rows, rows // 2
+    blocks, dscores, refs = refs[:parts], refs[parts : parts + 2], refs[parts + 3 :]
+    outs, kts = refs[:KEY_GROUPS], refs[KEY_GROUPS:]
     pair = heads // KEY_GROUPS
-    key_group = place()[1]
+    _, key_group, _, core = place()
     scale = width**-0.5
-    for part, ref in enumerate(blocks):
-        here = slice(part * rows, (part + 1) * rows)
-        kt_ref[:, here] = ref[:, :width].astype(jnp.float32).T.astype(jnp.bfloat16)
+    for kt_ref, side in zip(kts, (core, 1 - core)):
+        for part, ref in enumerate(blocks):
+            keys = ref[core_rows(0, side, half), :width].astype(jnp.float32)
+            kt_ref[:, part * half : (part + 1) * half] = keys.T.astype(jnp.bfloat16)
     for slot in range(KEY_GROUPS):
         for part in range(pair):
             head = (key_group ^ slot) * pair + part
-            dq = jnp.dot(kt_ref[...], ds_ref[head], preferred_element_type=jnp.float32)
+            dq = sum(
+                jnp.dot(kt_ref[...], ds_ref[head], preferred_element_type=jnp.float32)
+                for kt_ref, ds_ref in zip(kts, dscores)
+            )
             outs[slot][part * width : (part + 1) * width, :] = (dq * scale).astype(jnp.bfloat16)
 
 
@@ -408,7 +435,8 @@
         [((rows, 2 * width), bf16)],
         [in_hbm(keys), in_hbm(values)],
         "load",
-        scratch=[pltpu.SemaphoreType.DMA((2,))],
+        scratch=[pltpu.SemaphoreType.DMA((2, dp_count))],
+        pieces=dp_count,
     )
     query_v, grad_v, grad_t, bias, token = call(
         prep_kernel,
@@ -483,21 +511,24 @@
             dims=dims,
         )
 
-    dscores, keep, send = call(
-        backward_kernel,
-        [
-            ((heads, held, rows), bf16),
-            ((held // 2, 2 * width), f32),
-            ((held // 2, 2 * width), bf16),
-        ],
-        [query_v, grad_v] + blocks + [scores, last_scores] + list(dprobs) + all_stats,
-        "differentiate",
-        scratch=[pltpu.VMEM((held, 2 * width), f32)],
-        work=4,
-        dims=dims,
-        ahead=ahead,
-    )
+    inputs = [query_v, grad_v] + blocks + [scores, last_scores] + list(dprobs) + all_stats
+
+    def differentiate(own, dtype, after):
+        return call(
+            backward_kernel,
+            [((heads, held // 2, rows), bf16), ((held // 2, 2 * width), dtype)],
+            inputs + after,
+            "differentiate_own" if own else "differentiate_other",
+            scratch=[pltpu.VMEM((held // 2, 2 * width), f32)],
+            work=2,
+            dims=dims,
+            ahead=ahead,
+            own=own,
+        )
+
+    other_scores, send = differentiate(False, bf16, [])
     got = over_cores(send)
+    own_scores, keep = differentiate(True, f32, [other_scores])
     attn_out, token = call(
         finish_out_kernel,
         [((rows, pair * width), bf16), ((8, 128), f32)],
@@ -515,9 +546,9 @@
     dqs = call(
         query_kernel,
         [((pair * width, rows), bf16)] * KEY_GROUPS,
-        blocks + [dscores, keep],
+        blocks + [own_scores, other_scores, keep],
         "query_terms",
-        scratch=[pltpu.VMEM((width, held), bf16)],
+        scratch=[pltpu.VMEM((width, held // 2), bf16)] * 2,
         work=1,
         dims=dims,
     )

time: 37.1 us -> 37.2 us (level)
  waiting for transfers between devices: 10.9 us -> 9.33 us
  starting transfers between devices: 15.7 us -> 16.8 us
  Pallas kernels: 9.4 us -> 9.79 us
    ppermute x4, waiting for transfers between devices: 5.1 us -> 4.13 us  [over_dp(): return lax.ppermute(array, 'dp', [(d, d ^ flip) for d in range(dp_count)])]
    ppermute x3, waiting for transfers between devices: 1.58 us -> 0.62 us  [over_cores(): return lax.ppermute(array, 'ctx', [(c, c ^ 1) for c in range(ctx_count)])]
    ppermute x4, starting transfers between devices: 2.37 us -> 3.31 us  [over_dp(): return lax.ppermute(array, 'dp', [(d, d ^ flip) for d in range(dp_count)])]
    pallas_call x16 -> x17, Pallas kernels: 9.4 us -> 9.79 us  [call(): pl.pallas_call(functools.partial(kernel, **static), out_shape=[jax.ShapeD...]
  transfers between devices with their start and end apart: 12 -> 12, of which waited for: 8 -> 7; matrix products, arithmetic and copies ran while one was open for 0% -> 0% of each run, Pallas kernels for 15% -> 18%
where the time goes in v1:
time: 37.2 us; the launch traced here: 36.7 us
  starting transfers between devices  16.8 us (45%)
  Pallas kernels  9.79 us (26%)
  waiting for transfers between devices  9.33 us (25%)
  between operations  0.81 us (2%)
    pallas_call x17, Pallas kernels, call(): pl.pallas_call(functools.partial(kernel, **static), out_shape=[jax.ShapeD...  9.79 us
    ppermute x2, starting transfers between devices, gathered(): return lax.ppermute(array, ('dp', 'ctx'), pairs)  8.25 us
    ppermute x3, starting transfers between devices, spread(): return lax.ppermute(array, 'ctx', pairs)  5.03 us
    ppermute x4, waiting for transfers between devices, over_dp(): return lax.ppermute(array, 'dp', [(d, d ^ flip) for d in range(dp_count)])  4.13 us
    ppermute x4, starting transfers between devices, over_dp(): return lax.ppermute(array, 'dp', [(d, d ^ flip) for d in range(dp_count)])  3.31 us
    ppermute x3, waiting for transfers between devices, spread(): return lax.ppermute(array, 'ctx', pairs)  3 us
    ppermute x2, waiting for transfers between devices, gathered(): return lax.ppermute(array, ('dp', 'ctx'), pairs)  1.57 us
  transfers between devices with their start and end apart: 12, of which 7 were waited for; matrix products, arithmetic and copies ran while one was open for 0% of the time, Pallas kernels for 18%

profile of v1, /device:TPU:0, one launch (start us, length us, event | category | flops | bytes accessed | tf_op | source)
XLA Modules:
  0.0 36.7 jit_solution(8011715109875468261)
XLA Ops:
  0.6 0.9 %load.1.refs_0_ = bf16[256,256]{1,0:T(8,128)(2,1)S(1)} custom-call(bf16[256,128]{1,0:T(8,128)(2,1)} %k_hbm.1, bf16[256,128]{1,0:T(8,128)(2,1)} %v_hbm.1), custom_call_target="tpu_custom_call" | custom-call | bytes 131072 | tf_op jit(solution)/shard_map/load/pallas_call | solution.py:395
  1.5 5.9 %collective-permute-start = (bf16[256,256]{1,0:T(8,128)(2,1)S(1)}, bf16[256,256]{1,0:T(8,128)(2,1)S(1)}, u32[]{:S(2)}, u32[]{:S(2)}) collective-permute-start(bf16[256,256]{1,0:T(8,128)(2,1)S(1)} %load.1.refs_0_), channel_id=1, source_target_pairs={{8,2},{0,4},{10,12},{4,6},{9,3},{1,5},{11,13},{13,7},{24,18},{16,2... | collective-permute-start | bytes 393224 | tf_op jit(solution)/shard_map/ppermute | solution.py:427
  7.5 2.3 %collective-permute-start.1 = (bf16[256,256]{1,0:T(8,128)(2,1)S(1)}, bf16[256,256]{1,0:T(8,128)(2,1)S(1)}, u32[]{:S(2)}, u32[]{:S(2)}) collective-permute-start(bf16[256,256]{1,0:T(8,128)(2,1)S(1)} %load.1.refs_0_), channel_id=1, source_target_pairs={{0,6},{10,14},{1,7},{11,15},{16,22},{26,30},{17,23},{27,31}} | collective-permute-start | bytes 393224 | tf_op jit(solution)/shard_map/ppermute | solution.py:427
  9.8 1.5 %prepare.1 = (bf16[256,512]{1,0:T(8,128)(2,1)S(1)}, bf16[256,512]{1,0:T(8,128)(2,1)S(1)}, bf16[512,256]{1,0:T(8,128)(2,1)S(1)}, f32[1024,256]{1,0:T(8,128)S(1)}, f32[8,128]{1,0:T(8,128)S(1)}) custom-call(s32[16,128]{1,0:T(8,128)} %bitcast.1, bf16[256,1024]{1,0:T(8,128)(2,1)} %q_hbm.1, bf16[256,1024]{1,0:T(8,128)(2,1)} %g_hbm.1), custom_call_target="tpu_custom_call" | custom-call | flops 268435456 | bytes 1312768 | tf_op jit(solution)/shard_map/prepare/pallas_call | solution.py:395
  11.3 0.0 collective-permute-done.refs_0_.refs_1_
  11.4 0.1 collective-permute-start.3
  11.5 1.6 %collective-permute-done.1.refs_1_ = bf16[256,256]{1,0:T(8,128)(2,1)S(1)} collective-permute-done((bf16[256,256]{1,0:T(8,128)(2,1)S(1)}, bf16[256,256]{1,0:T(8,128)(2,1)S(1)}, u32[]{:S(2)}, u32[]{:S(2)}) %collective-permute-start.1) | collective-permute-done | bytes 131104 | tf_op jit(solution)/shard_map/ppermute | solution.py:427
  13.1 0.1 collective-permute-start.2
  13.1 0.0 collective-permute-done.3.refs_1_
  13.2 1.2 %attend_most.1 = (f32[4,768,256]{2,1,0:T(8,128)S(1)}, f32[8,256]{1,0:T(8,128)S(1)}, f32[4,128,256]{2,1,0:T(8,128)S(1)}) custom-call(bf16[256,512]{1,0:T(8,128)(2,1)S(1)} %get-tuple-element.34.q_ref, f32[1024,256]{1,0:T(8,128)S(1)} %get-tuple-element.36.bias_ref, bf16[256,256]{1,0:T(8,128)(2,1)S(1)} %pick.3.refs_0_, ...), custom_call_target="tpu_custom_call" | custom-call | flops 536870912 | bytes 1839104 | tf_op jit(solution)/shard_map/attend_most/pallas_call | solution.py:395
  14.3 0.1 collective-permute-done.2.kv_ref.refs_3_
  14.5 0.7 %attend.1 = (f32[12,256]{1,0:T(8,128)S(1)}, f32[4,256,256]{2,1,0:T(8,128)S(1)}, bf16[256,256]{1,0:T(8,128)(2,1)S(1)}, bf16[256,256]{1,0:T(8,128)(2,1)S(1)}) custom-call(bf16[256,512]{1,0:T(8,128)(2,1)S(1)} %get-tuple-element.34.q_ref, bf16[512,256]{1,0:T(8,128)(2,1)S(1)} %get-tuple-element.35.gt_ref, f32[1024,256]{1,0:T(8,128)S(1)} %get-tuple-element.36.bias_ref, ...), custom_call_target="tpu_custom_call" | custom-call | flops 268435456 | bytes 792576 | tf_op jit(solution)/shard_map/attend/pallas_call | solution.py:395
  15.2 0.1 collective-permute-start.4
  15.3 0.7 %dprobs.1.refs_6_ = f32[4,1024,256]{2,1,0:T(8,128)S(1)} custom-call(bf16[256,512]{1,0:T(8,128)(2,1)S(1)} %get-tuple-element.44.g_ref, bf16[256,256]{1,0:T(8,128)(2,1)S(1)} %pick.3.refs_0_, bf16[256,256]{1,0:T(8,128)(2,1)S(1)} %collective-permute-done.3.refs_1_, bf16[256,256]{1,0:T(8,128)(2,1)S(1)} %pick.2.refs_2_, ...), custom_call_target="tpu_custom_call" | custom-call | flops 268435456 | bytes 2097152 | tf_op jit(solution)/shard_map/dprobs/pallas_call | solution.py:395
  16.0 3.0 %collective-permute-done.4.refs_1_.refs_8_ = f32[12,256]{1,0:T(8,128)S(1)} collective-permute-done((f32[12,256]{1,0:T(8,128)S(1)}, f32[12,256]{1,0:T(8,128)S(1)}, u32[]{:S(2)}, u32[]{:S(2)}) %collective-permute-start.4) | collective-permute-done | bytes 12320 | tf_op jit(solution)/shard_map/ppermute | solution.py:416
  19.0 1.0 %differentiate_other.1 = (bf16[4,512,256]{2,1,0:T(8,128)(2,1)S(1)}, bf16[512,256]{1,0:T(8,128)(2,1)S(1)}) custom-call(bf16[256,512]{1,0:T(8,128)(2,1)S(1)} %get-tuple-element.34.q_ref, bf16[256,512]{1,0:T(8,128)(2,1)S(1)} %get-tuple-element.44.g_ref, bf16[256,256]{1,0:T(8,128)(2,1)S(1)} %pick.3.refs_0_, bf16[256,256]{1,0:T(8,128)(2,1)S(1)} %collective-permute-done.3.refs_1_, ...), custom_call_target="tpu_custom_call" | custom-call | flops 536870912 | bytes 1310720 | tf_op jit(solution)/shard_map/differentiate_other/pallas_call | solution.py:395
  20.0 0.1 collective-permute-start.6
  20.0 0.1 collective-permute-start.5
  20.1 0.9 %differentiate_own.1 = (bf16[4,512,256]{2,1,0:T(8,128)(2,1)S(1)}, f32[512,256]{1,0:T(8,128)S(1)}) custom-call(bf16[256,512]{1,0:T(8,128)(2,1)S(1)} %get-tuple-element.34.q_ref, bf16[256,512]{1,0:T(8,128)(2,1)S(1)} %get-tuple-element.44.g_ref, bf16[256,256]{1,0:T(8,128)(2,1)S(1)} %pick.3.refs_0_, bf16[256,256]{1,0:T(8,128)(2,1)S(1)} %collective-permute-done.3.refs_1_, ...), custom_call_target="tpu_custom_call" | custom-call | flops 536870912 | bytes 1310720 | tf_op jit(solution)/shard_map/differentiate_own/pallas_call | solution.py:395
  21.1 0.5 %collective-permute-done.6.got_ref = bf16[512,256]{1,0:T(8,128)(2,1)S(1)} collective-permute-done((bf16[512,256]{1,0:T(8,128)(2,1)S(1)}, bf16[512,256]{1,0:T(8,128)(2,1)S(1)}, u32[]{:S(2)}, u32[]{:S(2)}) %collective-permute-start.6) | collective-permute-done | bytes 262176 | tf_op jit(solution)/shard_map/ppermute | solution.py:419
  21.6 0.1 join_cores.1
  21.6 1.6 %collective-permute-start.8 = (bf16[256,256]{1,0:T(8,128)(2,1)S(1)}, bf16[256,256]{1,0:T(8,128)(2,1)S(1)}, u32[]{:S(2)}, u32[]{:S(2)}) collective-permute-start(bf16[256,256]{1,0:T(8,128)(2,1)S(1)} %get-tuple-element.56), channel_id=1, source_target_pairs={{0,16},{8,24},{16,0},{24,8},{1,17},{9,25},{17,1},{25,9},{2,18},{10... | collective-permute-start | bytes 393224 | tf_op jit(solution)/shard_map/ppermute | solution.py:416
  23.2 0.5 %query_terms.1 = (bf16[256,256]{1,0:T(8,128)(2,1)S(1)}, bf16[256,256]{1,0:T(8,128)(2,1)S(1)}) custom-call(bf16[256,256]{1,0:T(8,128)(2,1)S(1)} %pick.3.refs_0_, bf16[256,256]{1,0:T(8,128)(2,1)S(1)} %collective-permute-done.3.refs_1_, bf16[256,256]{1,0:T(8,128)(2,1)S(1)} %pick.2.refs_2_, bf16[256,256]{1,0:T(8,128)(2,1)S(1)} %collective-permute-done.2.kv_ref.refs_3_, ...), custom_call_target="tpu_custom_call" | custom-call | flops 268435456 | bytes 262144 | tf_op jit(solution)/shard_map/query_terms/pallas_call | solution.py:395
  23.7 1.6 %collective-permute-start.7 = (bf16[256,256]{1,0:T(8,128)(2,1)S(1)}, bf16[256,256]{1,0:T(8,128)(2,1)S(1)}, u32[]{:S(2)}, u32[]{:S(2)}) collective-permute-start(bf16[256,256]{1,0:T(8,128)(2,1)S(1)} %get-tuple-element.53), channel_id=1, source_target_pairs={{0,8},{8,0},{16,24},{24,16},{1,9},{9,1},{17,25},{25,17},{2,10},{10... | collective-permute-start | bytes 393224 | tf_op jit(solution)/shard_map/ppermute | solution.py:416
  25.3 0.6 %collective-permute-done.5.refs_3_ = bf16[256,256]{1,0:T(8,128)(2,1)S(1)} collective-permute-done((bf16[256,256]{1,0:T(8,128)(2,1)S(1)}, bf16[256,256]{1,0:T(8,128)(2,1)S(1)}, u32[]{:S(2)}, u32[]{:S(2)}) %collective-permute-start.5) | collective-permute-done | bytes 131104 | tf_op jit(solution)/shard_map/ppermute | solution.py:416
  26.0 0.8 %finish_out.1 = (bf16[256,256]{1,0:T(8,128)(2,1)}, f32[8,128]{1,0:T(8,128)S(1)}) custom-call(f32[12,256]{1,0:T(8,128)S(1)} %get-tuple-element.40.refs_0_.refs_7_, f32[12,256]{1,0:T(8,128)S(1)} %collective-permute-done.4.refs_1_.refs_8_, bf16[256,256]{1,0:T(8,128)(2,1)S(1)} %get-tuple-element.41.refs_2_, bf16[256,256]{1,0:T(8,128)(2,1)S(1)} %collective-permute-done.5.refs_3_), custom_call_target="tpu_custom_call" | custom-call | bytes 133120 | tf_op jit(solution)/shard_map/finish_out/pallas_call | solution.py:395
  26.8 0.5 %collective-permute-done.8.got_ref = bf16[256,256]{1,0:T(8,128)(2,1)S(1)} collective-permute-done((bf16[256,256]{1,0:T(8,128)(2,1)S(1)}, bf16[256,256]{1,0:T(8,128)(2,1)S(1)}, u32[]{:S(2)}, u32[]{:S(2)}) %collective-permute-start.8) | collective-permute-done | bytes 131104 | tf_op jit(solution)/shard_map/ppermute | solution.py:416
  27.3 3.1 %collective-permute-start.9 = (bf16[64,256]{1,0:T(8,128)(2,1)S(1)}, bf16[64,256]{1,0:T(8,128)(2,1)S(1)}, u32[]{:S(2)}, u32[]{:S(2)}) collective-permute-start(bf16[64,256]{1,0:T(8,128)(2,1)S(1)} %get-tuple-element.59), channel_id=1, source_target_pairs={{0,4},{1,5},{2,6},{3,7},{4,0},{5,1},{6,2},{7,3},{8,12},{9,13},{10,... | collective-permute-start | bytes 98312 | tf_op jit(solution)/shard_map/ppermute | solution.py:431
  30.4 1.5 %collective-permute-start.10 = (bf16[64,256]{1,0:T(8,128)(2,1)S(1)}, bf16[64,256]{1,0:T(8,128)(2,1)S(1)}, u32[]{:S(2)}, u32[]{:S(2)}) collective-permute-start(bf16[64,256]{1,0:T(8,128)(2,1)S(1)} %get-tuple-element.60), channel_id=1, source_target_pairs={{0,6},{1,7},{2,4},{3,5},{4,2},{5,3},{6,0},{7,1},{8,14},{9,15},{10,... | collective-permute-start | bytes 98312 | tf_op jit(solution)/shard_map/ppermute | solution.py:431
  31.8 0.5 %collective-permute-start.11 = (bf16[64,256]{1,0:T(8,128)(2,1)S(1)}, bf16[64,256]{1,0:T(8,128)(2,1)S(1)}, u32[]{:S(2)}, u32[]{:S(2)}) collective-permute-start(bf16[64,256]{1,0:T(8,128)(2,1)S(1)} %get-tuple-element.61), channel_id=1, source_target_pairs={{0,2},{1,3},{2,0},{3,1},{4,6},{5,7},{6,4},{7,5},{8,10},{9,11},{10,... | collective-permute-start | bytes 98312 | tf_op jit(solution)/shard_map/ppermute | solution.py:431
  32.3 0.0 collective-permute-done.7.got_ref
  32.3 0.8 %finish_query.1 = (bf16[256,256]{1,0:T(8,128)(2,1)}, f32[8,128]{1,0:T(8,128)S(1)}) custom-call(bf16[256,256]{1,0:T(8,128)(2,1)S(1)} %get-tuple-element.52.own_ref, bf16[256,256]{1,0:T(8,128)(2,1)S(1)} %collective-permute-done.7.got_ref), custom_call_target="tpu_custom_call" | custom-call | bytes 133120 | tf_op jit(solution)/shard_map/finish_query/pallas_call | solution.py:395
  33.1 0.0 collective-permute-done.9.second_ref
  33.1 3.0 %collective-permute-done.10.second_ref = bf16[64,256]{1,0:T(8,128)(2,1)S(1)} collective-permute-done((bf16[64,256]{1,0:T(8,128)(2,1)S(1)}, bf16[64,256]{1,0:T(8,128)(2,1)S(1)}, u32[]{:S(2)}, u32[]{:S(2)}) %collective-permute-start.10) | collective-permute-done | bytes 32800 | tf_op jit(solution)/shard_map/ppermute | solution.py:431
  36.1 0.0 collective-permute-done.11.refs_1_
  36.1 0.6 %finish.1 = (bf16[64,128]{1,0:T(8,128)(2,1)}, bf16[64,128]{1,0:T(8,128)(2,1)}) custom-call(f32[8,128]{1,0:T(8,128)S(1)} %get-tuple-element.55.token_ref, f32[64,256]{1,0:T(8,128)S(1)} %add_terms.3.refs_0_, bf16[64,256]{1,0:T(8,128)(2,1)S(1)} %collective-permute-done.11.refs_1_), custom_call_target="tpu_custom_call" | custom-call | bytes 32768 | tf_op jit(solution)/shard_map/finish/pallas_call | solution.py:395
  (5 shorter events, 0.1 us)
Async XLA Ops:
  1.5 9.8 %collective-permute-start = (bf16[256,256]{1,0:T(8,128)(2,1)S(1)}, bf16[256,256]{1,0:T(8,128)(2,1)S(1)}, u32[]{:S(2)}, u32[]{:S(2)}) collective-permute-start(bf16[256,256]{1,0:T(8,128)(2,1)S(1)} %load.1.refs_0_), channel_id=1, source_target_pairs={{8,2},{0,4},{10,12},{4,6},{9,3},{1,5},{11,13},{13,7},{24,18},{16,2... | collective-permute-start | bytes 393224 | tf_op jit(solution)/shard_map/ppermute | solution.py:427
  7.5 5.5 %collective-permute-start.1 = (bf16[256,256]{1,0:T(8,128)(2,1)S(1)}, bf16[256,256]{1,0:T(8,128)(2,1)S(1)}, u32[]{:S(2)}, u32[]{:S(2)}) collective-permute-start(bf16[256,256]{1,0:T(8,128)(2,1)S(1)} %load.1.refs_0_), channel_id=1, source_target_pairs={{0,6},{10,14},{1,7},{11,15},{16,22},{26,30},{17,23},{27,31}} | collective-permute-start | bytes 393224 | tf_op jit(solution)/shard_map/ppermute | solution.py:427
  11.4 1.8 %collective-permute-start.3 = (bf16[256,256]{1,0:T(8,128)(2,1)S(1)}, bf16[256,256]{1,0:T(8,128)(2,1)S(1)}, u32[]{:S(2)}, u32[]{:S(2)}) collective-permute-start(bf16[256,256]{1,0:T(8,128)(2,1)S(1)} %pick.3.refs_0_), channel_id=1, source_target_pairs={{0,1},{1,0},{2,3},{3,2},{4,5},{5,4},{6,7},{7,6},{8,9},{9,8},{10,11... | collective-permute-start | bytes 393224 | tf_op jit(solution)/shard_map/ppermute | solution.py:419
  13.1 1.4 %collective-permute-start.2 = (bf16[256,256]{1,0:T(8,128)(2,1)S(1)}, bf16[256,256]{1,0:T(8,128)(2,1)S(1)}, u32[]{:S(2)}, u32[]{:S(2)}) collective-permute-start(bf16[256,256]{1,0:T(8,128)(2,1)S(1)} %pick.2.refs_2_), channel_id=1, source_target_pairs={{0,1},{1,0},{2,3},{3,2},{4,5},{5,4},{6,7},{7,6},{8,9},{9,8},{10,11... | collective-permute-start | bytes 393224 | tf_op jit(solution)/shard_map/ppermute | solution.py:419
  15.2 3.8 %collective-permute-start.4 = (f32[12,256]{1,0:T(8,128)S(1)}, f32[12,256]{1,0:T(8,128)S(1)}, u32[]{:S(2)}, u32[]{:S(2)}) collective-permute-start(f32[12,256]{1,0:T(8,128)S(1)} %get-tuple-element.40.refs_0_.refs_7_), channel_id=1, source_target_pairs={{0,8},{8,0},{16,24},{24,16},{1,9},{9,1},{17,25},{25,17},{2,10},{10... | collective-permute-start | bytes 36872 | tf_op jit(solution)/shard_map/ppermute | solution.py:416
  20.0 1.6 %collective-permute-start.6 = (bf16[512,256]{1,0:T(8,128)(2,1)S(1)}, bf16[512,256]{1,0:T(8,128)(2,1)S(1)}, u32[]{:S(2)}, u32[]{:S(2)}) collective-permute-start(bf16[512,256]{1,0:T(8,128)(2,1)S(1)} %get-tuple-element.50), channel_id=1, source_target_pairs={{0,1},{1,0},{2,3},{3,2},{4,5},{5,4},{6,7},{7,6},{8,9},{9,8},{10,11... | collective-permute-start | bytes 786440 | tf_op jit(solution)/shard_map/ppermute | solution.py:419
  20.0 5.9 %collective-permute-start.5 = (bf16[256,256]{1,0:T(8,128)(2,1)S(1)}, bf16[256,256]{1,0:T(8,128)(2,1)S(1)}, u32[]{:S(2)}, u32[]{:S(2)}) collective-permute-start(bf16[256,256]{1,0:T(8,128)(2,1)S(1)} %get-tuple-element.42), channel_id=1, source_target_pairs={{0,8},{8,0},{16,24},{24,16},{1,9},{9,1},{17,25},{25,17},{2,10},{10... | collective-permute-start | bytes 393224 | tf_op jit(solution)/shard_map/ppermute | solution.py:416
  21.6 5.6 %collective-permute-start.8 = (bf16[256,256]{1,0:T(8,128)(2,1)S(1)}, bf16[256,256]{1,0:T(8,128)(2,1)S(1)}, u32[]{:S(2)}, u32[]{:S(2)}) collective-permute-start(bf16[256,256]{1,0:T(8,128)(2,1)S(1)} %get-tuple-element.56), channel_id=1, source_target_pairs={{0,16},{8,24},{16,0},{24,8},{1,17},{9,25},{17,1},{25,9},{2,18},{10... | collective-permute-start | bytes 393224 | tf_op jit(solution)/shard_map/ppermute | solution.py:416
  23.7 8.6 %collective-permute-start.7 = (bf16[256,256]{1,0:T(8,128)(2,1)S(1)}, bf16[256,256]{1,0:T(8,128)(2,1)S(1)}, u32[]{:S(2)}, u32[]{:S(2)}) collective-permute-start(bf16[256,256]{1,0:T(8,128)(2,1)S(1)} %get-tuple-element.53), channel_id=1, source_target_pairs={{0,8},{8,0},{16,24},{24,16},{1,9},{9,1},{17,25},{25,17},{2,10},{10... | collective-permute-start | bytes 393224 | tf_op jit(solution)/shard_map/ppermute | solution.py:416
  27.3 5.8 %collective-permute-start.9 = (bf16[64,256]{1,0:T(8,128)(2,1)S(1)}, bf16[64,256]{1,0:T(8,128)(2,1)S(1)}, u32[]{:S(2)}, u32[]{:S(2)}) collective-permute-start(bf16[64,256]{1,0:T(8,128)(2,1)S(1)} %get-tuple-element.59), channel_id=1, source_target_pairs={{0,4},{1,5},{2,6},{3,7},{4,0},{5,1},{6,2},{7,3},{8,12},{9,13},{10,... | collective-permute-start | bytes 98312 | tf_op jit(solution)/shard_map/ppermute | solution.py:431
  30.4 5.7 %collective-permute-start.10 = (bf16[64,256]{1,0:T(8,128)(2,1)S(1)}, bf16[64,256]{1,0:T(8,128)(2,1)S(1)}, u32[]{:S(2)}, u32[]{:S(2)}) collective-permute-start(bf16[64,256]{1,0:T(8,128)(2,1)S(1)} %get-tuple-element.60), channel_id=1, source_target_pairs={{0,6},{1,7},{2,4},{3,5},{4,2},{5,3},{6,0},{7,1},{8,14},{9,15},{10,... | collective-permute-start | bytes 98312 | tf_op jit(solution)/shard_map/ppermute | solution.py:431
  31.8 4.3 %collective-permute-start.11 = (bf16[64,256]{1,0:T(8,128)(2,1)S(1)}, bf16[64,256]{1,0:T(8,128)(2,1)S(1)}, u32[]{:S(2)}, u32[]{:S(2)}) collective-permute-start(bf16[64,256]{1,0:T(8,128)(2,1)S(1)} %get-tuple-element.61), channel_id=1, source_target_pairs={{0,2},{1,3},{2,0},{3,1},{4,6},{5,7},{6,4},{7,5},{8,10},{9,11},{10,... | collective-permute-start | bytes 98312 | tf_op jit(solution)/shard_map/ppermute | solution.py:431

commit v2 on v1

--- a/solution.py
+++ b/solution.py
@@ -242,17 +242,21 @@
     blocks, scores, last_scores, refs = refs[:parts], refs[parts], refs[parts + 1], refs[parts + 2 :]
     dprobs_ref, refs = (refs[0], refs[1:]) if ahead else (None, refs)
     stats = refs[:KEY_GROUPS]
-    ds_ref, terms_ref, acc_ref = refs[-3:]
+    ds_ref, terms_ref, acc_ref, queries_ref, grads_ref = refs[-5:]
     head_group, key_group, chip, core = place()
     side = core if own else 1 - core
     scale = width**-0.5
     top, _, total, delta = merged_stats([s[...] for s in stats], heads)
     lse = top + jnp.log2(total)
     for head in range(heads):
-        cols = slice(head * width, (head + 1) * width)
-        query, grad = q_ref[:, cols], g_ref[:, cols]
-        for part, ref in enumerate(blocks):
-            held_rows, block_rows = core_rows(part * rows, side, half), core_rows(0, side, half)
+        cols, here = (slice(head * size, (head + 1) * size) for size in (width, rows))
+        queries_ref[here, :] = q_ref[:, cols]
+        grads_ref[here, :] = g_ref[:, cols]
+    for part, ref in enumerate(blocks):
+        held_rows, block_rows = core_rows(part * rows, side, half), core_rows(0, side, half)
+        here = slice(part * half, (part + 1) * half)
+        all_probs, all_scores = [], []
+        for head in range(heads):
             if part == parts - 1:
                 row = last_scores[head, block_rows, :]
             else:
@@ -262,19 +266,22 @@
                 dprobs = dprobs_ref[head, held_rows, :]
             else:
                 dprobs = lax.dot_general(
-                    ref[block_rows, width:], grad, NT, preferred_element_type=jnp.float32
+                    ref[block_rows, width:],
+                    g_ref[:, head * width : (head + 1) * width],
+                    NT,
+                    preferred_element_type=jnp.float32,
                 )
             dscores = (probs * (dprobs - delta[head : head + 1])).astype(jnp.bfloat16)
-            here = slice(part * half, (part + 1) * half)
             ds_ref[head, here, :] = dscores
-            dv = jnp.dot(probs.astype(jnp.bfloat16), grad, preferred_element_type=jnp.float32)
-            dk = jnp.dot(dscores, query, preferred_element_type=jnp.float32)
-            if head == 0:
-                acc_ref[here, :width] = dk
-                acc_ref[here, width:] = dv
-            else:
-                acc_ref[here, :width] += dk
-                acc_ref[here, width:] += dv
+            all_probs.append(probs.astype(jnp.bfloat16))
+            all_scores.append(dscores)
+        for columns, factors, stacked in (
+            (slice(0, width), all_scores, queries_ref),
+            (slice(width, 2 * width), all_probs, grads_ref),
+        ):
+            acc_ref[here, columns] = jnp.dot(
+                jnp.concatenate(factors, axis=1), stacked[...], preferred_element_type=jnp.float32
+            )
     chips, piece = ctx_count // 2, rows // 4
     level = chips // 4
     for spot in range(2 * chips):
@@ -519,7 +526,8 @@
             [((heads, held // 2, rows), bf16), ((held // 2, 2 * width), dtype)],
             inputs + after,
             "differentiate_own" if own else "differentiate_other",
-            scratch=[pltpu.VMEM((held // 2, 2 * width), f32)],
+            scratch=[pltpu.VMEM((held // 2, 2 * width), f32)]
+            + [pltpu.VMEM((heads * rows, width), bf16)] * 2,
             work=2,
             dims=dims,
             ahead=ahead,

time: 37.2 us -> 37.3 us (level)
  no operation moved by 1% of the time
where the time goes in v2:
time: 37.3 us; the launch traced here: 36.9 us
  starting transfers between devices  17 us (46%)
  Pallas kernels  9.93 us (27%)
  waiting for transfers between devices  9.18 us (25%)
  between operations  0.81 us (2%)
    pallas_call x17, Pallas kernels, call(): pl.pallas_call(functools.partial(kernel, **static), out_shape=[jax.ShapeD...  9.93 us
    ppermute x2, starting transfers between devices, gathered(): return lax.ppermute(array, ('dp', 'ctx'), pairs)  8.25 us
    ppermute x3, starting transfers between devices, spread(): return lax.ppermute(array, 'ctx', pairs)  5.11 us
    ppermute x4, waiting for transfers between devices, over_dp(): return lax.ppermute(array, 'dp', [(d, d ^ flip) for d in range(dp_count)])  4.06 us
    ppermute x4, starting transfers between devices, over_dp(): return lax.ppermute(array, 'dp', [(d, d ^ flip) for d in range(dp_count)])  3.38 us
    ppermute x3, waiting for transfers between devices, spread(): return lax.ppermute(array, 'ctx', pairs)  3 us
    ppermute x2, waiting for transfers between devices, gathered(): return lax.ppermute(array, ('dp', 'ctx'), pairs)  1.57 us
  transfers between devices with their start and end apart: 12, of which 7 were waited for; matrix products, arithmetic and copies ran while one was open for 0% of the time, Pallas kernels for 18%

profile of v2, /device:TPU:0, one launch (start us, length us, event | category | flops | bytes accessed | tf_op | source)
XLA Modules:
  0.0 36.9 jit_solution(14608452633899191393)
XLA Ops:
  0.6 0.9 %load.1.refs_0_ = bf16[256,256]{1,0:T(8,128)(2,1)S(1)} custom-call(bf16[256,128]{1,0:T(8,128)(2,1)} %k_hbm.1, bf16[256,128]{1,0:T(8,128)(2,1)} %v_hbm.1), custom_call_target="tpu_custom_call" | custom-call | bytes 131072 | tf_op jit(solution)/shard_map/load/pallas_call | solution.py:402
  1.5 5.9 %collective-permute-start = (bf16[256,256]{1,0:T(8,128)(2,1)S(1)}, bf16[256,256]{1,0:T(8,128)(2,1)S(1)}, u32[]{:S(2)}, u32[]{:S(2)}) collective-permute-start(bf16[256,256]{1,0:T(8,128)(2,1)S(1)} %load.1.refs_0_), channel_id=1, source_target_pairs={{8,2},{0,4},{10,12},{4,6},{9,3},{1,5},{11,13},{13,7},{24,18},{16,2... | collective-permute-start | bytes 393224 | tf_op jit(solution)/shard_map/ppermute | solution.py:434
  7.5 2.3 %collective-permute-start.1 = (bf16[256,256]{1,0:T(8,128)(2,1)S(1)}, bf16[256,256]{1,0:T(8,128)(2,1)S(1)}, u32[]{:S(2)}, u32[]{:S(2)}) collective-permute-start(bf16[256,256]{1,0:T(8,128)(2,1)S(1)} %load.1.refs_0_), channel_id=1, source_target_pairs={{0,6},{10,14},{1,7},{11,15},{16,22},{26,30},{17,23},{27,31}} | collective-permute-start | bytes 393224 | tf_op jit(solution)/shard_map/ppermute | solution.py:434
  9.8 1.5 %prepare.1 = (bf16[256,512]{1,0:T(8,128)(2,1)S(1)}, bf16[256,512]{1,0:T(8,128)(2,1)S(1)}, bf16[512,256]{1,0:T(8,128)(2,1)S(1)}, f32[1024,256]{1,0:T(8,128)S(1)}, f32[8,128]{1,0:T(8,128)S(1)}) custom-call(s32[16,128]{1,0:T(8,128)} %bitcast.1, bf16[256,1024]{1,0:T(8,128)(2,1)} %q_hbm.1, bf16[256,1024]{1,0:T(8,128)(2,1)} %g_hbm.1), custom_call_target="tpu_custom_call" | custom-call | flops 268435456 | bytes 1312768 | tf_op jit(solution)/shard_map/prepare/pallas_call | solution.py:402
  11.3 0.0 collective-permute-done.refs_0_.refs_1_
  11.4 0.1 collective-permute-start.3
  11.5 1.6 %collective-permute-done.1.refs_1_ = bf16[256,256]{1,0:T(8,128)(2,1)S(1)} collective-permute-done((bf16[256,256]{1,0:T(8,128)(2,1)S(1)}, bf16[256,256]{1,0:T(8,128)(2,1)S(1)}, u32[]{:S(2)}, u32[]{:S(2)}) %collective-permute-start.1) | collective-permute-done | bytes 131104 | tf_op jit(solution)/shard_map/ppermute | solution.py:434
  13.1 0.1 collective-permute-start.2
  13.1 0.0 collective-permute-done.3.refs_1_
  13.2 1.2 %attend_most.1 = (f32[4,768,256]{2,1,0:T(8,128)S(1)}, f32[8,256]{1,0:T(8,128)S(1)}, f32[4,128,256]{2,1,0:T(8,128)S(1)}) custom-call(bf16[256,512]{1,0:T(8,128)(2,1)S(1)} %get-tuple-element.34.q_ref, f32[1024,256]{1,0:T(8,128)S(1)} %get-tuple-element.36.bias_ref, bf16[256,256]{1,0:T(8,128)(2,1)S(1)} %pick.3.refs_0_, ...), custom_call_target="tpu_custom_call" | custom-call | flops 536870912 | bytes 1839104 | tf_op jit(solution)/shard_map/attend_most/pallas_call | solution.py:402
  14.3 0.1 collective-permute-done.2.kv_ref.refs_3_
  14.5 0.7 %attend.1 = (f32[12,256]{1,0:T(8,128)S(1)}, f32[4,256,256]{2,1,0:T(8,128)S(1)}, bf16[256,256]{1,0:T(8,128)(2,1)S(1)}, bf16[256,256]{1,0:T(8,128)(2,1)S(1)}) custom-call(bf16[256,512]{1,0:T(8,128)(2,1)S(1)} %get-tuple-element.34.q_ref, bf16[512,256]{1,0:T(8,128)(2,1)S(1)} %get-tuple-element.35.gt_ref, f32[1024,256]{1,0:T(8,128)S(1)} %get-tuple-element.36.bias_ref, ...), custom_call_target="tpu_custom_call" | custom-call | flops 268435456 | bytes 792576 | tf_op jit(solution)/shard_map/attend/pallas_call | solution.py:402
  15.2 0.1 collective-permute-start.4
  15.3 0.7 %dprobs.1.refs_6_ = f32[4,1024,256]{2,1,0:T(8,128)S(1)} custom-call(bf16[256,512]{1,0:T(8,128)(2,1)S(1)} %get-tuple-element.44.g_ref, bf16[256,256]{1,0:T(8,128)(2,1)S(1)} %pick.3.refs_0_, bf16[256,256]{1,0:T(8,128)(2,1)S(1)} %collective-permute-done.3.refs_1_, bf16[256,256]{1,0:T(8,128)(2,1)S(1)} %pick.2.refs_2_, ...), custom_call_target="tpu_custom_call" | custom-call | flops 268435456 | bytes 2097152 | tf_op jit(solution)/shard_map/dprobs/pallas_call | solution.py:402
  16.0 3.0 %collective-permute-done.4.refs_1_.refs_8_ = f32[12,256]{1,0:T(8,128)S(1)} collective-permute-done((f32[12,256]{1,0:T(8,128)S(1)}, f32[12,256]{1,0:T(8,128)S(1)}, u32[]{:S(2)}, u32[]{:S(2)}) %collective-permute-start.4) | collective-permute-done | bytes 12320 | tf_op jit(solution)/shard_map/ppermute | solution.py:423
  19.0 1.0 %differentiate_other.1 = (bf16[4,512,256]{2,1,0:T(8,128)(2,1)S(1)}, bf16[512,256]{1,0:T(8,128)(2,1)S(1)}) custom-call(bf16[256,512]{1,0:T(8,128)(2,1)S(1)} %get-tuple-element.34.q_ref, bf16[256,512]{1,0:T(8,128)(2,1)S(1)} %get-tuple-element.44.g_ref, bf16[256,256]{1,0:T(8,128)(2,1)S(1)} %pick.3.refs_0_, bf16[256,256]{1,0:T(8,128)(2,1)S(1)} %collective-permute-done.3.refs_1_, ...), custom_call_target="tpu_custom_call" | custom-call | flops 536870912 | bytes 1310720 | tf_op jit(solution)/shard_map/differentiate_other/pallas_call | solution.py:402
  20.0 0.1 collective-permute-start.6
  20.1 0.1 collective-permute-start.5
  20.2 1.0 %differentiate_own.1 = (bf16[4,512,256]{2,1,0:T(8,128)(2,1)S(1)}, f32[512,256]{1,0:T(8,128)S(1)}) custom-call(bf16[256,512]{1,0:T(8,128)(2,1)S(1)} %get-tuple-element.34.q_ref, bf16[256,512]{1,0:T(8,128)(2,1)S(1)} %get-tuple-element.44.g_ref, bf16[256,256]{1,0:T(8,128)(2,1)S(1)} %pick.3.refs_0_, bf16[256,256]{1,0:T(8,128)(2,1)S(1)} %collective-permute-done.3.refs_1_, ...), custom_call_target="tpu_custom_call" | custom-call | flops 536870912 | bytes 1310720 | tf_op jit(solution)/shard_map/differentiate_own/pallas_call | solution.py:402
  21.2 0.4 %collective-permute-done.6.got_ref = bf16[512,256]{1,0:T(8,128)(2,1)S(1)} collective-permute-done((bf16[512,256]{1,0:T(8,128)(2,1)S(1)}, bf16[512,256]{1,0:T(8,128)(2,1)S(1)}, u32[]{:S(2)}, u32[]{:S(2)}) %collective-permute-start.6) | collective-permute-done | bytes 262176 | tf_op jit(solution)/shard_map/ppermute | solution.py:426
  21.6 0.1 join_cores.1
  21.7 1.6 %collective-permute-start.8 = (bf16[256,256]{1,0:T(8,128)(2,1)S(1)}, bf16[256,256]{1,0:T(8,128)(2,1)S(1)}, u32[]{:S(2)}, u32[]{:S(2)}) collective-permute-start(bf16[256,256]{1,0:T(8,128)(2,1)S(1)} %get-tuple-element.56), channel_id=1, source_target_pairs={{0,16},{8,24},{16,0},{24,8},{1,17},{9,25},{17,1},{25,9},{2,18},{10... | collective-permute-start | bytes 393224 | tf_op jit(solution)/shard_map/ppermute | solution.py:423
  23.3 0.5 %query_terms.1 = (bf16[256,256]{1,0:T(8,128)(2,1)S(1)}, bf16[256,256]{1,0:T(8,128)(2,1)S(1)}) custom-call(bf16[256,256]{1,0:T(8,128)(2,1)S(1)} %pick.3.refs_0_, bf16[256,256]{1,0:T(8,128)(2,1)S(1)} %collective-permute-done.3.refs_1_, bf16[256,256]{1,0:T(8,128)(2,1)S(1)} %pick.2.refs_2_, bf16[256,256]{1,0:T(8,128)(2,1)S(1)} %collective-permute-done.2.kv_ref.refs_3_, ...), custom_call_target="tpu_custom_call" | custom-call | flops 268435456 | bytes 262144 | tf_op jit(solution)/shard_map/query_terms/pallas_call | solution.py:402
  23.8 1.7 %collective-permute-start.7 = (bf16[256,256]{1,0:T(8,128)(2,1)S(1)}, bf16[256,256]{1,0:T(8,128)(2,1)S(1)}, u32[]{:S(2)}, u32[]{:S(2)}) collective-permute-start(bf16[256,256]{1,0:T(8,128)(2,1)S(1)} %get-tuple-element.53), channel_id=1, source_target_pairs={{0,8},{8,0},{16,24},{24,16},{1,9},{9,1},{17,25},{25,17},{2,10},{10... | collective-permute-start | bytes 393224 | tf_op jit(solution)/shard_map/ppermute | solution.py:423
  25.5 0.6 %collective-permute-done.5.refs_3_ = bf16[256,256]{1,0:T(8,128)(2,1)S(1)} collective-permute-done((bf16[256,256]{1,0:T(8,128)(2,1)S(1)}, bf16[256,256]{1,0:T(8,128)(2,1)S(1)}, u32[]{:S(2)}, u32[]{:S(2)}) %collective-permute-start.5) | collective-permute-done | bytes 131104 | tf_op jit(solution)/shard_map/ppermute | solution.py:423
  26.0 0.8 %finish_out.1 = (bf16[256,256]{1,0:T(8,128)(2,1)}, f32[8,128]{1,0:T(8,128)S(1)}) custom-call(f32[12,256]{1,0:T(8,128)S(1)} %get-tuple-element.40.refs_0_.refs_7_, f32[12,256]{1,0:T(8,128)S(1)} %collective-permute-done.4.refs_1_.refs_8_, bf16[256,256]{1,0:T(8,128)(2,1)S(1)} %get-tuple-element.41.refs_2_, bf16[256,256]{1,0:T(8,128)(2,1)S(1)} %collective-permute-done.5.refs_3_), custom_call_target="tpu_custom_call" | custom-call | bytes 133120 | tf_op jit(solution)/shard_map/finish_out/pallas_call | solution.py:402
  26.8 0.5 %collective-permute-done.8.got_ref = bf16[256,256]{1,0:T(8,128)(2,1)S(1)} collective-permute-done((bf16[256,256]{1,0:T(8,128)(2,1)S(1)}, bf16[256,256]{1,0:T(8,128)(2,1)S(1)}, u32[]{:S(2)}, u32[]{:S(2)}) %collective-permute-start.8) | collective-permute-done | bytes 131104 | tf_op jit(solution)/shard_map/ppermute | solution.py:423
  27.3 3.2 %collective-permute-start.9 = (bf16[64,256]{1,0:T(8,128)(2,1)S(1)}, bf16[64,256]{1,0:T(8,128)(2,1)S(1)}, u32[]{:S(2)}, u32[]{:S(2)}) collective-permute-start(bf16[64,256]{1,0:T(8,128)(2,1)S(1)} %get-tuple-element.59), channel_id=1, source_target_pairs={{0,4},{1,5},{2,6},{3,7},{4,0},{5,1},{6,2},{7,3},{8,12},{9,13},{10,... | collective-permute-start | bytes 98312 | tf_op jit(solution)/shard_map/ppermute | solution.py:438
  30.5 1.5 %collective-permute-start.10 = (bf16[64,256]{1,0:T(8,128)(2,1)S(1)}, bf16[64,256]{1,0:T(8,128)(2,1)S(1)}, u32[]{:S(2)}, u32[]{:S(2)}) collective-permute-start(bf16[64,256]{1,0:T(8,128)(2,1)S(1)} %get-tuple-element.60), channel_id=1, source_target_pairs={{0,6},{1,7},{2,4},{3,5},{4,2},{5,3},{6,0},{7,1},{8,14},{9,15},{10,... | collective-permute-start | bytes 98312 | tf_op jit(solution)/shard_map/ppermute | solution.py:438
  32.0 0.5 %collective-permute-start.11 = (bf16[64,256]{1,0:T(8,128)(2,1)S(1)}, bf16[64,256]{1,0:T(8,128)(2,1)S(1)}, u32[]{:S(2)}, u32[]{:S(2)}) collective-permute-start(bf16[64,256]{1,0:T(8,128)(2,1)S(1)} %get-tuple-element.61), channel_id=1, source_target_pairs={{0,2},{1,3},{2,0},{3,1},{4,6},{5,7},{6,4},{7,5},{8,10},{9,11},{10,... | collective-permute-start | bytes 98312 | tf_op jit(solution)/shard_map/ppermute | solution.py:438
  32.5 0.0 collective-permute-done.7.got_ref
  32.5 0.8 %finish_query.1 = (bf16[256,256]{1,0:T(8,128)(2,1)}, f32[8,128]{1,0:T(8,128)S(1)}) custom-call(bf16[256,256]{1,0:T(8,128)(2,1)S(1)} %get-tuple-element.52.own_ref, bf16[256,256]{1,0:T(8,128)(2,1)S(1)} %collective-permute-done.7.got_ref), custom_call_target="tpu_custom_call" | custom-call | bytes 133120 | tf_op jit(solution)/shard_map/finish_query/pallas_call | solution.py:402
  33.2 0.0 collective-permute-done.9.second_ref
  33.2 3.0 %collective-permute-done.10.second_ref = bf16[64,256]{1,0:T(8,128)(2,1)S(1)} collective-permute-done((bf16[64,256]{1,0:T(8,128)(2,1)S(1)}, bf16[64,256]{1,0:T(8,128)(2,1)S(1)}, u32[]{:S(2)}, u32[]{:S(2)}) %collective-permute-start.10) | collective-permute-done | bytes 32800 | tf_op jit(solution)/shard_map/ppermute | solution.py:438
  36.2 0.0 collective-permute-done.11.refs_1_
  36.3 0.6 %finish.1 = (bf16[64,128]{1,0:T(8,128)(2,1)}, bf16[64,128]{1,0:T(8,128)(2,1)}) custom-call(f32[8,128]{1,0:T(8,128)S(1)} %get-tuple-element.55.token_ref, f32[64,256]{1,0:T(8,128)S(1)} %add_terms.3.refs_0_, bf16[64,256]{1,0:T(8,128)(2,1)S(1)} %collective-permute-done.11.refs_1_), custom_call_target="tpu_custom_call" | custom-call | bytes 32768 | tf_op jit(solution)/shard_map/finish/pallas_call | solution.py:402
  (5 shorter events, 0.1 us)
Async XLA Ops:
  1.5 9.8 %collective-permute-start = (bf16[256,256]{1,0:T(8,128)(2,1)S(1)}, bf16[256,256]{1,0:T(8,128)(2,1)S(1)}, u32[]{:S(2)}, u32[]{:S(2)}) collective-permute-start(bf16[256,256]{1,0:T(8,128)(2,1)S(1)} %load.1.refs_0_), channel_id=1, source_target_pairs={{8,2},{0,4},{10,12},{4,6},{9,3},{1,5},{11,13},{13,7},{24,18},{16,2... | collective-permute-start | bytes 393224 | tf_op jit(solution)/shard_map/ppermute | solution.py:434
  7.5 5.5 %collective-permute-start.1 = (bf16[256,256]{1,0:T(8,128)(2,1)S(1)}, bf16[256,256]{1,0:T(8,128)(2,1)S(1)}, u32[]{:S(2)}, u32[]{:S(2)}) collective-permute-start(bf16[256,256]{1,0:T(8,128)(2,1)S(1)} %load.1.refs_0_), channel_id=1, source_target_pairs={{0,6},{10,14},{1,7},{11,15},{16,22},{26,30},{17,23},{27,31}} | collective-permute-start | bytes 393224 | tf_op jit(solution)/shard_map/ppermute | solution.py:434
  11.4 1.8 %collective-permute-start.3 = (bf16[256,256]{1,0:T(8,128)(2,1)S(1)}, bf16[256,256]{1,0:T(8,128)(2,1)S(1)}, u32[]{:S(2)}, u32[]{:S(2)}) collective-permute-start(bf16[256,256]{1,0:T(8,128)(2,1)S(1)} %pick.3.refs_0_), channel_id=1, source_target_pairs={{0,1},{1,0},{2,3},{3,2},{4,5},{5,4},{6,7},{7,6},{8,9},{9,8},{10,11... | collective-permute-start | bytes 393224 | tf_op jit(solution)/shard_map/ppermute | solution.py:426
  13.1 1.4 %collective-permute-start.2 = (bf16[256,256]{1,0:T(8,128)(2,1)S(1)}, bf16[256,256]{1,0:T(8,128)(2,1)S(1)}, u32[]{:S(2)}, u32[]{:S(2)}) collective-permute-start(bf16[256,256]{1,0:T(8,128)(2,1)S(1)} %pick.2.refs_2_), channel_id=1, source_target_pairs={{0,1},{1,0},{2,3},{3,2},{4,5},{5,4},{6,7},{7,6},{8,9},{9,8},{10,11... | collective-permute-start | bytes 393224 | tf_op jit(solution)/shard_map/ppermute | solution.py:426
  15.2 3.8 %collective-permute-start.4 = (f32[12,256]{1,0:T(8,128)S(1)}, f32[12,256]{1,0:T(8,128)S(1)}, u32[]{:S(2)}, u32[]{:S(2)}) collective-permute-start(f32[12,256]{1,0:T(8,128)S(1)} %get-tuple-element.40.refs_0_.refs_7_), channel_id=1, source_target_pairs={{0,8},{8,0},{16,24},{24,16},{1,9},{9,1},{17,25},{25,17},{2,10},{10... | collective-permute-start | bytes 36872 | tf_op jit(solution)/shard_map/ppermute | solution.py:423
  20.0 1.6 %collective-permute-start.6 = (bf16[512,256]{1,0:T(8,128)(2,1)S(1)}, bf16[512,256]{1,0:T(8,128)(2,1)S(1)}, u32[]{:S(2)}, u32[]{:S(2)}) collective-permute-start(bf16[512,256]{1,0:T(8,128)(2,1)S(1)} %get-tuple-element.50), channel_id=1, source_target_pairs={{0,1},{1,0},{2,3},{3,2},{4,5},{5,4},{6,7},{7,6},{8,9},{9,8},{10,11... | collective-permute-start | bytes 786440 | tf_op jit(solution)/shard_map/ppermute | solution.py:426
  20.1 5.9 %collective-permute-start.5 = (bf16[256,256]{1,0:T(8,128)(2,1)S(1)}, bf16[256,256]{1,0:T(8,128)(2,1)S(1)}, u32[]{:S(2)}, u32[]{:S(2)}) collective-permute-start(bf16[256,256]{1,0:T(8,128)(2,1)S(1)} %get-tuple-element.42), channel_id=1, source_target_pairs={{0,8},{8,0},{16,24},{24,16},{1,9},{9,1},{17,25},{25,17},{2,10},{10... | collective-permute-start | bytes 393224 | tf_op jit(solution)/shard_map/ppermute | solution.py:423
  21.7 5.6 %collective-permute-start.8 = (bf16[256,256]{1,0:T(8,128)(2,1)S(1)}, bf16[256,256]{1,0:T(8,128)(2,1)S(1)}, u32[]{:S(2)}, u32[]{:S(2)}) collective-permute-start(bf16[256,256]{1,0:T(8,128)(2,1)S(1)} %get-tuple-element.56), channel_id=1, source_target_pairs={{0,16},{8,24},{16,0},{24,8},{1,17},{9,25},{17,1},{25,9},{2,18},{10... | collective-permute-start | bytes 393224 | tf_op jit(solution)/shard_map/ppermute | solution.py:423
  23.8 8.7 %collective-permute-start.7 = (bf16[256,256]{1,0:T(8,128)(2,1)S(1)}, bf16[256,256]{1,0:T(8,128)(2,1)S(1)}, u32[]{:S(2)}, u32[]{:S(2)}) collective-permute-start(bf16[256,256]{1,0:T(8,128)(2,1)S(1)} %get-tuple-element.53), channel_id=1, source_target_pairs={{0,8},{8,0},{16,24},{24,16},{1,9},{9,1},{17,25},{25,17},{2,10},{10... | collective-permute-start | bytes 393224 | tf_op jit(solution)/shard_map/ppermute | solution.py:423
  27.3 5.9 %collective-permute-start.9 = (bf16[64,256]{1,0:T(8,128)(2,1)S(1)}, bf16[64,256]{1,0:T(8,128)(2,1)S(1)}, u32[]{:S(2)}, u32[]{:S(2)}) collective-permute-start(bf16[64,256]{1,0:T(8,128)(2,1)S(1)} %get-tuple-element.59), channel_id=1, source_target_pairs={{0,4},{1,5},{2,6},{3,7},{4,0},{5,1},{6,2},{7,3},{8,12},{9,13},{10,... | collective-permute-start | bytes 98312 | tf_op jit(solution)/shard_map/ppermute | solution.py:438
  30.5 5.7 %collective-permute-start.10 = (bf16[64,256]{1,0:T(8,128)(2,1)S(1)}, bf16[64,256]{1,0:T(8,128)(2,1)S(1)}, u32[]{:S(2)}, u32[]{:S(2)}) collective-permute-start(bf16[64,256]{1,0:T(8,128)(2,1)S(1)} %get-tuple-element.60), channel_id=1, source_target_pairs={{0,6},{1,7},{2,4},{3,5},{4,2},{5,3},{6,0},{7,1},{8,14},{9,15},{10,... | collective-permute-start | bytes 98312 | tf_op jit(solution)/shard_map/ppermute | solution.py:438
  32.0 4.3 %collective-permute-start.11 = (bf16[64,256]{1,0:T(8,128)(2,1)S(1)}, bf16[64,256]{1,0:T(8,128)(2,1)S(1)}, u32[]{:S(2)}, u32[]{:S(2)}) collective-permute-start(bf16[64,256]{1,0:T(8,128)(2,1)S(1)} %get-tuple-element.61), channel_id=1, source_target_pairs={{0,2},{1,3},{2,0},{3,1},{4,6},{5,7},{6,4},{7,5},{8,10},{9,11},{10,... | collective-permute-start | bytes 98312 | tf_op jit(solution)/shard_map/ppermute | solution.py:438

commit v3 on v1

--- a/solution.py
+++ b/solution.py
@@ -49,8 +49,7 @@
 
 
 def spread_rounds(chips):
-    flips = list(range(2, chips)) + [1]
-    return [{chip: chip ^ flip for chip in range(chips)} for flip in flips]
+    return [{chip: (chip + step) % chips for chip in range(chips)} for step in range(1, chips)]
 
 
 def mask_bias(seg_ref, rows, held):

time: 37.2 us -> 37.3 us (level)
  starting transfers between devices: 16.8 us -> 17.8 us
  waiting for transfers between devices: 9.33 us -> 8.47 us
    ppermute x3, starting transfers between devices: 5.03 us -> 5.99 us  [spread(): return lax.ppermute(array, 'ctx', pairs)]
    ppermute x3, waiting for transfers between devices: 3 us -> 2.15 us  [spread(): return lax.ppermute(array, 'ctx', pairs)]
  transfers between devices with their start and end apart: 12 -> 12, of which waited for: 7 -> 8; matrix products, arithmetic and copies ran while one was open for 0% -> 0% of each run, Pallas kernels for 18% -> 18%
where the time goes in v3:
time: 37.3 us; the launch traced here: 36.8 us
  starting transfers between devices  17.8 us (48%)
  Pallas kernels  9.79 us (26%)
  waiting for transfers between devices  8.47 us (23%)
  between operations  0.8 us (2%)
    pallas_call x17, Pallas kernels, call(): pl.pallas_call(functools.partial(kernel, **static), out_shape=[jax.ShapeD...  9.79 us
    ppermute x2, starting transfers between devices, gathered(): return lax.ppermute(array, ('dp', 'ctx'), pairs)  8.25 us
    ppermute x3, starting transfers between devices, spread(): return lax.ppermute(array, 'ctx', pairs)  5.99 us
    ppermute x4, waiting for transfers between devices, over_dp(): return lax.ppermute(array, 'dp', [(d, d ^ flip) for d in range(dp_count)])  4.13 us
    ppermute x4, starting transfers between devices, over_dp(): return lax.ppermute(array, 'dp', [(d, d ^ flip) for d in range(dp_count)])  3.31 us
    ppermute x3, waiting for transfers between devices, spread(): return lax.ppermute(array, 'ctx', pairs)  2.15 us
    ppermute x2, waiting for transfers between devices, gathered(): return lax.ppermute(array, ('dp', 'ctx'), pairs)  1.57 us
  transfers between devices with their start and end apart: 12, of which 8 were waited for; matrix products, arithmetic and copies ran while one was open for 0% of the time, Pallas kernels for 18%

profile of v3, /device:TPU:0, one launch (start us, length us, event | category | flops | bytes accessed | tf_op | source)
XLA Modules:
  0.0 36.8 jit_solution(18386088576183447876)
XLA Ops:
  0.6 0.9 %load.1.refs_0_ = bf16[256,256]{1,0:T(8,128)(2,1)S(1)} custom-call(bf16[256,128]{1,0:T(8,128)(2,1)} %k_hbm.1, bf16[256,128]{1,0:T(8,128)(2,1)} %v_hbm.1), custom_call_target="tpu_custom_call" | custom-call | bytes 131072 | tf_op jit(solution)/shard_map/load/pallas_call | solution.py:394
  1.5 5.9 %collective-permute-start = (bf16[256,256]{1,0:T(8,128)(2,1)S(1)}, bf16[256,256]{1,0:T(8,128)(2,1)S(1)}, u32[]{:S(2)}, u32[]{:S(2)}) collective-permute-start(bf16[256,256]{1,0:T(8,128)(2,1)S(1)} %load.1.refs_0_), channel_id=1, source_target_pairs={{8,2},{0,4},{10,12},{4,6},{9,3},{1,5},{11,13},{13,7},{24,18},{16,2... | collective-permute-start | bytes 393224 | tf_op jit(solution)/shard_map/ppermute | solution.py:426
  7.5 2.3 %collective-permute-start.1 = (bf16[256,256]{1,0:T(8,128)(2,1)S(1)}, bf16[256,256]{1,0:T(8,128)(2,1)S(1)}, u32[]{:S(2)}, u32[]{:S(2)}) collective-permute-start(bf16[256,256]{1,0:T(8,128)(2,1)S(1)} %load.1.refs_0_), channel_id=1, source_target_pairs={{0,6},{10,14},{1,7},{11,15},{16,22},{26,30},{17,23},{27,31}} | collective-permute-start | bytes 393224 | tf_op jit(solution)/shard_map/ppermute | solution.py:426
  9.8 1.5 %prepare.1 = (bf16[256,512]{1,0:T(8,128)(2,1)S(1)}, bf16[256,512]{1,0:T(8,128)(2,1)S(1)}, bf16[512,256]{1,0:T(8,128)(2,1)S(1)}, f32[1024,256]{1,0:T(8,128)S(1)}, f32[8,128]{1,0:T(8,128)S(1)}) custom-call(s32[16,128]{1,0:T(8,128)} %bitcast.1, bf16[256,1024]{1,0:T(8,128)(2,1)} %q_hbm.1, bf16[256,1024]{1,0:T(8,128)(2,1)} %g_hbm.1), custom_call_target="tpu_custom_call" | custom-call | flops 268435456 | bytes 1312768 | tf_op jit(solution)/shard_map/prepare/pallas_call | solution.py:394
  11.3 0.0 collective-permute-done.refs_0_.refs_1_
  11.4 0.1 collective-permute-start.3
  11.5 1.6 %collective-permute-done.1.refs_1_ = bf16[256,256]{1,0:T(8,128)(2,1)S(1)} collective-permute-done((bf16[256,256]{1,0:T(8,128)(2,1)S(1)}, bf16[256,256]{1,0:T(8,128)(2,1)S(1)}, u32[]{:S(2)}, u32[]{:S(2)}) %collective-permute-start.1) | collective-permute-done | bytes 131104 | tf_op jit(solution)/shard_map/ppermute | solution.py:426
  13.1 0.1 collective-permute-start.2
  13.1 0.0 collective-permute-done.3.refs_1_
  13.2 1.2 %attend_most.1 = (f32[4,768,256]{2,1,0:T(8,128)S(1)}, f32[8,256]{1,0:T(8,128)S(1)}, f32[4,128,256]{2,1,0:T(8,128)S(1)}) custom-call(bf16[256,512]{1,0:T(8,128)(2,1)S(1)} %get-tuple-element.34.q_ref, f32[1024,256]{1,0:T(8,128)S(1)} %get-tuple-element.36.bias_ref, bf16[256,256]{1,0:T(8,128)(2,1)S(1)} %pick.3.refs_0_, ...), custom_call_target="tpu_custom_call" | custom-call | flops 536870912 | bytes 1839104 | tf_op jit(solution)/shard_map/attend_most/pallas_call | solution.py:394
  14.3 0.1 collective-permute-done.2.kv_ref.refs_3_
  14.5 0.7 %attend.1 = (f32[12,256]{1,0:T(8,128)S(1)}, f32[4,256,256]{2,1,0:T(8,128)S(1)}, bf16[256,256]{1,0:T(8,128)(2,1)S(1)}, bf16[256,256]{1,0:T(8,128)(2,1)S(1)}) custom-call(bf16[256,512]{1,0:T(8,128)(2,1)S(1)} %get-tuple-element.34.q_ref, bf16[512,256]{1,0:T(8,128)(2,1)S(1)} %get-tuple-element.35.gt_ref, f32[1024,256]{1,0:T(8,128)S(1)} %get-tuple-element.36.bias_ref, ...), custom_call_target="tpu_custom_call" | custom-call | flops 268435456 | bytes 792576 | tf_op jit(solution)/shard_map/attend/pallas_call | solution.py:394
  15.2 0.1 collective-permute-start.4
  15.3 0.7 %dprobs.1.refs_6_ = f32[4,1024,256]{2,1,0:T(8,128)S(1)} custom-call(bf16[256,512]{1,0:T(8,128)(2,1)S(1)} %get-tuple-element.44.g_ref, bf16[256,256]{1,0:T(8,128)(2,1)S(1)} %pick.3.refs_0_, bf16[256,256]{1,0:T(8,128)(2,1)S(1)} %collective-permute-done.3.refs_1_, bf16[256,256]{1,0:T(8,128)(2,1)S(1)} %pick.2.refs_2_, ...), custom_call_target="tpu_custom_call" | custom-call | flops 268435456 | bytes 2097152 | tf_op jit(solution)/shard_map/dprobs/pallas_call | solution.py:394
  16.0 3.0 %collective-permute-done.4.refs_1_.refs_8_ = f32[12,256]{1,0:T(8,128)S(1)} collective-permute-done((f32[12,256]{1,0:T(8,128)S(1)}, f32[12,256]{1,0:T(8,128)S(1)}, u32[]{:S(2)}, u32[]{:S(2)}) %collective-permute-start.4) | collective-permute-done | bytes 12320 | tf_op jit(solution)/shard_map/ppermute | solution.py:415
  19.0 1.0 %differentiate_other.1 = (bf16[4,512,256]{2,1,0:T(8,128)(2,1)S(1)}, bf16[512,256]{1,0:T(8,128)(2,1)S(1)}) custom-call(bf16[256,512]{1,0:T(8,128)(2,1)S(1)} %get-tuple-element.34.q_ref, bf16[256,512]{1,0:T(8,128)(2,1)S(1)} %get-tuple-element.44.g_ref, bf16[256,256]{1,0:T(8,128)(2,1)S(1)} %pick.3.refs_0_, bf16[256,256]{1,0:T(8,128)(2,1)S(1)} %collective-permute-done.3.refs_1_, ...), custom_call_target="tpu_custom_call" | custom-call | flops 536870912 | bytes 1310720 | tf_op jit(solution)/shard_map/differentiate_other/pallas_call | solution.py:394
  20.0 0.1 collective-permute-start.6
  20.0 0.1 collective-permute-start.5
  20.1 0.9 %differentiate_own.1 = (bf16[4,512,256]{2,1,0:T(8,128)(2,1)S(1)}, f32[512,256]{1,0:T(8,128)S(1)}) custom-call(bf16[256,512]{1,0:T(8,128)(2,1)S(1)} %get-tuple-element.34.q_ref, bf16[256,512]{1,0:T(8,128)(2,1)S(1)} %get-tuple-element.44.g_ref, bf16[256,256]{1,0:T(8,128)(2,1)S(1)} %pick.3.refs_0_, bf16[256,256]{1,0:T(8,128)(2,1)S(1)} %collective-permute-done.3.refs_1_, ...), custom_call_target="tpu_custom_call" | custom-call | flops 536870912 | bytes 1310720 | tf_op jit(solution)/shard_map/differentiate_own/pallas_call | solution.py:394
  21.1 0.5 %collective-permute-done.6.got_ref = bf16[512,256]{1,0:T(8,128)(2,1)S(1)} collective-permute-done((bf16[512,256]{1,0:T(8,128)(2,1)S(1)}, bf16[512,256]{1,0:T(8,128)(2,1)S(1)}, u32[]{:S(2)}, u32[]{:S(2)}) %collective-permute-start.6) | collective-permute-done | bytes 262176 | tf_op jit(solution)/shard_map/ppermute | solution.py:418
  21.6 0.1 join_cores.1
  21.6 1.6 %collective-permute-start.8 = (bf16[256,256]{1,0:T(8,128)(2,1)S(1)}, bf16[256,256]{1,0:T(8,128)(2,1)S(1)}, u32[]{:S(2)}, u32[]{:S(2)}) collective-permute-start(bf16[256,256]{1,0:T(8,128)(2,1)S(1)} %get-tuple-element.56), channel_id=1, source_target_pairs={{0,16},{8,24},{16,0},{24,8},{1,17},{9,25},{17,1},{25,9},{2,18},{10... | collective-permute-start | bytes 393224 | tf_op jit(solution)/shard_map/ppermute | solution.py:415
  23.2 0.5 %query_terms.1 = (bf16[256,256]{1,0:T(8,128)(2,1)S(1)}, bf16[256,256]{1,0:T(8,128)(2,1)S(1)}) custom-call(bf16[256,256]{1,0:T(8,128)(2,1)S(1)} %pick.3.refs_0_, bf16[256,256]{1,0:T(8,128)(2,1)S(1)} %collective-permute-done.3.refs_1_, bf16[256,256]{1,0:T(8,128)(2,1)S(1)} %pick.2.refs_2_, bf16[256,256]{1,0:T(8,128)(2,1)S(1)} %collective-permute-done.2.kv_ref.refs_3_, ...), custom_call_target="tpu_custom_call" | custom-call | flops 268435456 | bytes 262144 | tf_op jit(solution)/shard_map/query_terms/pallas_call | solution.py:394
  23.7 1.6 %collective-permute-start.7 = (bf16[256,256]{1,0:T(8,128)(2,1)S(1)}, bf16[256,256]{1,0:T(8,128)(2,1)S(1)}, u32[]{:S(2)}, u32[]{:S(2)}) collective-permute-start(bf16[256,256]{1,0:T(8,128)(2,1)S(1)} %get-tuple-element.53), channel_id=1, source_target_pairs={{0,8},{8,0},{16,24},{24,16},{1,9},{9,1},{17,25},{25,17},{2,10},{10... | collective-permute-start | bytes 393224 | tf_op jit(solution)/shard_map/ppermute | solution.py:415
  25.3 0.6 %collective-permute-done.5.refs_3_ = bf16[256,256]{1,0:T(8,128)(2,1)S(1)} collective-permute-done((bf16[256,256]{1,0:T(8,128)(2,1)S(1)}, bf16[256,256]{1,0:T(8,128)(2,1)S(1)}, u32[]{:S(2)}, u32[]{:S(2)}) %collective-permute-start.5) | collective-permute-done | bytes 131104 | tf_op jit(solution)/shard_map/ppermute | solution.py:415
  26.0 0.8 %finish_out.1 = (bf16[256,256]{1,0:T(8,128)(2,1)}, f32[8,128]{1,0:T(8,128)S(1)}) custom-call(f32[12,256]{1,0:T(8,128)S(1)} %get-tuple-element.40.refs_0_.refs_7_, f32[12,256]{1,0:T(8,128)S(1)} %collective-permute-done.4.refs_1_.refs_8_, bf16[256,256]{1,0:T(8,128)(2,1)S(1)} %get-tuple-element.41.refs_2_, bf16[256,256]{1,0:T(8,128)(2,1)S(1)} %collective-permute-done.5.refs_3_), custom_call_target="tpu_custom_call" | custom-call | bytes 133120 | tf_op jit(solution)/shard_map/finish_out/pallas_call | solution.py:394
  26.8 0.5 %collective-permute-done.8.got_ref = bf16[256,256]{1,0:T(8,128)(2,1)S(1)} collective-permute-done((bf16[256,256]{1,0:T(8,128)(2,1)S(1)}, bf16[256,256]{1,0:T(8,128)(2,1)S(1)}, u32[]{:S(2)}, u32[]{:S(2)}) %collective-permute-start.8) | collective-permute-done | bytes 131104 | tf_op jit(solution)/shard_map/ppermute | solution.py:415
  27.3 1.6 %collective-permute-start.9 = (bf16[64,256]{1,0:T(8,128)(2,1)S(1)}, bf16[64,256]{1,0:T(8,128)(2,1)S(1)}, u32[]{:S(2)}, u32[]{:S(2)}) collective-permute-start(bf16[64,256]{1,0:T(8,128)(2,1)S(1)} %get-tuple-element.59), channel_id=1, source_target_pairs={{0,2},{1,3},{2,4},{3,5},{4,6},{5,7},{6,0},{7,1},{8,10},{9,11},{10,... | collective-permute-start | bytes 98312 | tf_op jit(solution)/shard_map/ppermute | solution.py:430
  28.9 3.4 %collective-permute-start.10 = (bf16[64,256]{1,0:T(8,128)(2,1)S(1)}, bf16[64,256]{1,0:T(8,128)(2,1)S(1)}, u32[]{:S(2)}, u32[]{:S(2)}) collective-permute-start(bf16[64,256]{1,0:T(8,128)(2,1)S(1)} %get-tuple-element.60), channel_id=1, source_target_pairs={{0,4},{1,5},{2,6},{3,7},{4,0},{5,1},{6,2},{7,3},{8,12},{9,13},{10,... | collective-permute-start | bytes 98312 | tf_op jit(solution)/shard_map/ppermute | solution.py:430
  32.3 1.0 %collective-permute-start.11 = (bf16[64,256]{1,0:T(8,128)(2,1)S(1)}, bf16[64,256]{1,0:T(8,128)(2,1)S(1)}, u32[]{:S(2)}, u32[]{:S(2)}) collective-permute-start(bf16[64,256]{1,0:T(8,128)(2,1)S(1)} %get-tuple-element.61), channel_id=1, source_target_pairs={{0,6},{1,7},{2,0},{3,1},{4,2},{5,3},{6,4},{7,5},{8,14},{9,15},{10,... | collective-permute-start | bytes 98312 | tf_op jit(solution)/shard_map/ppermute | solution.py:430
  33.3 0.0 collective-permute-done.7.got_ref
  33.3 0.8 %finish_query.1 = (bf16[256,256]{1,0:T(8,128)(2,1)}, f32[8,128]{1,0:T(8,128)S(1)}) custom-call(bf16[256,256]{1,0:T(8,128)(2,1)S(1)} %get-tuple-element.52.own_ref, bf16[256,256]{1,0:T(8,128)(2,1)S(1)} %collective-permute-done.7.got_ref), custom_call_target="tpu_custom_call" | custom-call | bytes 133120 | tf_op jit(solution)/shard_map/finish_query/pallas_call | solution.py:394
  34.0 0.0 collective-permute-done.9.second_ref
  34.0 0.3 collective-permute-done.10.second_ref
  34.4 1.8 %collective-permute-done.11.refs_1_ = bf16[64,256]{1,0:T(8,128)(2,1)S(1)} collective-permute-done((bf16[64,256]{1,0:T(8,128)(2,1)S(1)}, bf16[64,256]{1,0:T(8,128)(2,1)S(1)}, u32[]{:S(2)}, u32[]{:S(2)}) %collective-permute-start.11) | collective-permute-done | bytes 32800 | tf_op jit(solution)/shard_map/ppermute | solution.py:430
  36.2 0.6 %finish.1 = (bf16[64,128]{1,0:T(8,128)(2,1)}, bf16[64,128]{1,0:T(8,128)(2,1)}) custom-call(f32[8,128]{1,0:T(8,128)S(1)} %get-tuple-element.55.token_ref, f32[64,256]{1,0:T(8,128)S(1)} %add_terms.3.refs_0_, bf16[64,256]{1,0:T(8,128)(2,1)S(1)} %collective-permute-done.11.refs_1_), custom_call_target="tpu_custom_call" | custom-call | bytes 32768 | tf_op jit(solution)/shard_map/finish/pallas_call | solution.py:394
  (5 shorter events, 0.1 us)
Async XLA Ops:
  1.5 9.8 %collective-permute-start = (bf16[256,256]{1,0:T(8,128)(2,1)S(1)}, bf16[256,256]{1,0:T(8,128)(2,1)S(1)}, u32[]{:S(2)}, u32[]{:S(2)}) collective-permute-start(bf16[256,256]{1,0:T(8,128)(2,1)S(1)} %load.1.refs_0_), channel_id=1, source_target_pairs={{8,2},{0,4},{10,12},{4,6},{9,3},{1,5},{11,13},{13,7},{24,18},{16,2... | collective-permute-start | bytes 393224 | tf_op jit(solution)/shard_map/ppermute | solution.py:426
  7.5 5.5 %collective-permute-start.1 = (bf16[256,256]{1,0:T(8,128)(2,1)S(1)}, bf16[256,256]{1,0:T(8,128)(2,1)S(1)}, u32[]{:S(2)}, u32[]{:S(2)}) collective-permute-start(bf16[256,256]{1,0:T(8,128)(2,1)S(1)} %load.1.refs_0_), channel_id=1, source_target_pairs={{0,6},{10,14},{1,7},{11,15},{16,22},{26,30},{17,23},{27,31}} | collective-permute-start | bytes 393224 | tf_op jit(solution)/shard_map/ppermute | solution.py:426
  11.4 1.8 %collective-permute-start.3 = (bf16[256,256]{1,0:T(8,128)(2,1)S(1)}, bf16[256,256]{1,0:T(8,128)(2,1)S(1)}, u32[]{:S(2)}, u32[]{:S(2)}) collective-permute-start(bf16[256,256]{1,0:T(8,128)(2,1)S(1)} %pick.3.refs_0_), channel_id=1, source_target_pairs={{0,1},{1,0},{2,3},{3,2},{4,5},{5,4},{6,7},{7,6},{8,9},{9,8},{10,11... | collective-permute-start | bytes 393224 | tf_op jit(solution)/shard_map/ppermute | solution.py:418
  13.1 1.4 %collective-permute-start.2 = (bf16[256,256]{1,0:T(8,128)(2,1)S(1)}, bf16[256,256]{1,0:T(8,128)(2,1)S(1)}, u32[]{:S(2)}, u32[]{:S(2)}) collective-permute-start(bf16[256,256]{1,0:T(8,128)(2,1)S(1)} %pick.2.refs_2_), channel_id=1, source_target_pairs={{0,1},{1,0},{2,3},{3,2},{4,5},{5,4},{6,7},{7,6},{8,9},{9,8},{10,11... | collective-permute-start | bytes 393224 | tf_op jit(solution)/shard_map/ppermute | solution.py:418
  15.2 3.8 %collective-permute-start.4 = (f32[12,256]{1,0:T(8,128)S(1)}, f32[12,256]{1,0:T(8,128)S(1)}, u32[]{:S(2)}, u32[]{:S(2)}) collective-permute-start(f32[12,256]{1,0:T(8,128)S(1)} %get-tuple-element.40.refs_0_.refs_7_), channel_id=1, source_target_pairs={{0,8},{8,0},{16,24},{24,16},{1,9},{9,1},{17,25},{25,17},{2,10},{10... | collective-permute-start | bytes 36872 | tf_op jit(solution)/shard_map/ppermute | solution.py:415
  20.0 1.6 %collective-permute-start.6 = (bf16[512,256]{1,0:T(8,128)(2,1)S(1)}, bf16[512,256]{1,0:T(8,128)(2,1)S(1)}, u32[]{:S(2)}, u32[]{:S(2)}) collective-permute-start(bf16[512,256]{1,0:T(8,128)(2,1)S(1)} %get-tuple-element.50), channel_id=1, source_target_pairs={{0,1},{1,0},{2,3},{3,2},{4,5},{5,4},{6,7},{7,6},{8,9},{9,8},{10,11... | collective-permute-start | bytes 786440 | tf_op jit(solution)/shard_map/ppermute | solution.py:418
  20.0 5.9 %collective-permute-start.5 = (bf16[256,256]{1,0:T(8,128)(2,1)S(1)}, bf16[256,256]{1,0:T(8,128)(2,1)S(1)}, u32[]{:S(2)}, u32[]{:S(2)}) collective-permute-start(bf16[256,256]{1,0:T(8,128)(2,1)S(1)} %get-tuple-element.42), channel_id=1, source_target_pairs={{0,8},{8,0},{16,24},{24,16},{1,9},{9,1},{17,25},{25,17},{2,10},{10... | collective-permute-start | bytes 393224 | tf_op jit(solution)/shard_map/ppermute | solution.py:415
  21.6 5.6 %collective-permute-start.8 = (bf16[256,256]{1,0:T(8,128)(2,1)S(1)}, bf16[256,256]{1,0:T(8,128)(2,1)S(1)}, u32[]{:S(2)}, u32[]{:S(2)}) collective-permute-start(bf16[256,256]{1,0:T(8,128)(2,1)S(1)} %get-tuple-element.56), channel_id=1, source_target_pairs={{0,16},{8,24},{16,0},{24,8},{1,17},{9,25},{17,1},{25,9},{2,18},{10... | collective-permute-start | bytes 393224 | tf_op jit(solution)/shard_map/ppermute | solution.py:415
  23.7 9.5 %collective-permute-start.7 = (bf16[256,256]{1,0:T(8,128)(2,1)S(1)}, bf16[256,256]{1,0:T(8,128)(2,1)S(1)}, u32[]{:S(2)}, u32[]{:S(2)}) collective-permute-start(bf16[256,256]{1,0:T(8,128)(2,1)S(1)} %get-tuple-element.53), channel_id=1, source_target_pairs={{0,8},{8,0},{16,24},{24,16},{1,9},{9,1},{17,25},{25,17},{2,10},{10... | collective-permute-start | bytes 393224 | tf_op jit(solution)/shard_map/ppermute | solution.py:415
  27.3 6.8 %collective-permute-start.9 = (bf16[64,256]{1,0:T(8,128)(2,1)S(1)}, bf16[64,256]{1,0:T(8,128)(2,1)S(1)}, u32[]{:S(2)}, u32[]{:S(2)}) collective-permute-start(bf16[64,256]{1,0:T(8,128)(2,1)S(1)} %get-tuple-element.59), channel_id=1, source_target_pairs={{0,2},{1,3},{2,4},{3,5},{4,6},{5,7},{6,0},{7,1},{8,10},{9,11},{10,... | collective-permute-start | bytes 98312 | tf_op jit(solution)/shard_map/ppermute | solution.py:430
  28.9 5.4 %collective-permute-start.10 = (bf16[64,256]{1,0:T(8,128)(2,1)S(1)}, bf16[64,256]{1,0:T(8,128)(2,1)S(1)}, u32[]{:S(2)}, u32[]{:S(2)}) collective-permute-start(bf16[64,256]{1,0:T(8,128)(2,1)S(1)} %get-tuple-element.60), channel_id=1, source_target_pairs={{0,4},{1,5},{2,6},{3,7},{4,0},{5,1},{6,2},{7,3},{8,12},{9,13},{10,... | collective-permute-start | bytes 98312 | tf_op jit(solution)/shard_map/ppermute | solution.py:430
  32.3 3.9 %collective-permute-start.11 = (bf16[64,256]{1,0:T(8,128)(2,1)S(1)}, bf16[64,256]{1,0:T(8,128)(2,1)S(1)}, u32[]{:S(2)}, u32[]{:S(2)}) collective-permute-start(bf16[64,256]{1,0:T(8,128)(2,1)S(1)} %get-tuple-element.61), channel_id=1, source_target_pairs={{0,6},{1,7},{2,0},{3,1},{4,2},{5,3},{6,4},{7,5},{8,14},{9,15},{10,... | collective-permute-start | bytes 98312 | tf_op jit(solution)/shard_map/ppermute | solution.py:430

commit v4 on v1

--- a/solution.py
+++ b/solution.py
@@ -30,13 +30,13 @@
 
 
 def gather_rounds(chips):
-    rounds = [{} for _ in range(2 if chips == 4 else chips - 1)]
+    rounds = [{} for _ in range(1, chips)]
     for core in range(2):
         if chips == 4:
             rounds[0][0, 1, core] = (1, 0)
             rounds[0][0, 2, core] = (0, 0)
             rounds[0][1, 2, core] = (1, 1)
-            rounds[0][0, 3, core] = (core, 2)
+            rounds[2][0, 3, core] = (core, 2)
             rounds[1][0, 3, core] = (0, 0)
             rounds[1][1, 3, core] = (1, 1)
             continue
@@ -82,7 +82,8 @@
     return list(range(0, pieces, 2)) + list(range(1, pieces, 2))
 
 
-def load_kernel(k_hbm, v_hbm, kv_ref, sems, *, pieces):
+def load_kernel(k_hbm, v_hbm, *refs, pieces, chips):
+    kv_ref, sems = refs[-2:]
     rows, width = k_hbm.shape
     size = rows // pieces
     copies = []
@@ -95,10 +96,18 @@
                     array.at[source, :], kv_ref.at[target, columns], sems.at[k, spot]
                 )
             )
-    for copy in copies:
-        copy.start()
-    for copy in copies:
-        copy.wait()
+
+    def load():
+        for copy in copies:
+            copy.start()
+        for copy in copies:
+            copy.wait()
+
+    if chips:
+        chip = place()[2]
+        pl.when(functools.reduce(jnp.logical_or, [chip == c for c in chips]))(load)
+    else:
+        load()
 
 
 def pick_kernel(*refs, choices):
@@ -113,6 +122,10 @@
         @pl.when(wanted)
         def _():
             out_ref[...] = jnp.zeros_like(out_ref) if choice < 0 else refs[choice][...]
+
+
+def pass_kernel(array_ref, token_ref):
+    token_ref[...] = array_ref[:8, :128]
 
 
 def prep_kernel(
@@ -430,14 +443,22 @@
         pairs = [(a * 2 + core, b * 2 + core) for a, b in moves.items() for core in range(2)]
         return lax.ppermute(array, "ctx", pairs)
 
-    (own_kv,) = call(
-        load_kernel,
-        [((rows, 2 * width), bf16)],
-        [in_hbm(keys), in_hbm(values)],
-        "load",
-        scratch=[pltpu.SemaphoreType.DMA((2, dp_count))],
-        pieces=dp_count,
-    )
+    rounds = gather_rounds(chips)
+
+    def loaded(only, after):
+        (array,) = call(
+            load_kernel,
+            [((rows, 2 * width), bf16)],
+            [in_hbm(keys), in_hbm(values)] + after,
+            "load_first" if only else "load",
+            scratch=[pltpu.SemaphoreType.DMA((2, dp_count))],
+            pieces=dp_count,
+            chips=only,
+        )
+        return array
+
+    first_kv = loaded(sorted({home for _, home in rounds[0].values()}), [])
+    own_kv = loaded([], [first_kv])
     query_v, grad_v, grad_t, bias, token = call(
         prep_kernel,
         [
@@ -453,8 +474,9 @@
         work=1,
         dims=dims,
     )
-    rounds = gather_rounds(chips)
-    sent = [own_kv] + [gathered(own_kv, moves) for moves in rounds]
+    sent = [own_kv, gathered(first_kv, rounds[0])]
+    sent += [gathered(own_kv, moves) for moves in rounds[1:]]
+    first = call(pass_kernel, [((8, 128), bf16)], sent[1:2], "pass")
     blocks = []
     for spot in range(chips // 2):
         choices = []
@@ -468,7 +490,7 @@
         (picked,) = call(
             pick_kernel,
             [((rows, 2 * width), bf16)],
-            [sent[k] for k in used] + [token],
+            [sent[k] for k in used] + [token] + (list(first) if spot == 0 else []),
             "pick",
             choices=[used.index(c) if c >= 0 else -1 for c in choices],
         )

time: 37.2 us -> 37.1 us (level)
  Pallas kernels: 9.79 us -> 10.7 us
  waiting for transfers between devices: 9.33 us -> 8.46 us
    pallas_call x17 -> x19, Pallas kernels: 9.79 us -> 10.7 us  [call(): pl.pallas_call(functools.partial(kernel, **static), out_shape=[jax.ShapeD...]
    ppermute x2 -> x3, waiting for transfers between devices: 1.57 us -> 1.05 us  [gathered(): return lax.ppermute(array, ('dp', 'ctx'), pairs)]
    ppermute x2 -> x3, starting transfers between devices: 8.25 us -> 8.1 us  [gathered(): return lax.ppermute(array, ('dp', 'ctx'), pairs)]
  transfers between devices with their start and end apart: 12 -> 13, of which waited for: 7 -> 8; matrix products, arithmetic and copies ran while one was open for 0% -> 0% of each run, Pallas kernels for 18% -> 21%
where the time goes in v4:
time: 37.1 us; the launch traced here: 36.5 us
  starting transfers between devices  16.5 us (44%)
  Pallas kernels  10.7 us (29%)
  waiting for transfers between devices  8.46 us (23%)
  between operations  0.83 us (2%)
    pallas_call x19, Pallas kernels, call(): pl.pallas_call(functools.partial(kernel, **static), out_shape=[jax.ShapeD...  10.7 us
    ppermute x3, starting transfers between devices, gathered(): return lax.ppermute(array, ('dp', 'ctx'), pairs)  8.1 us
    ppermute x3, starting transfers between devices, spread(): return lax.ppermute(array, 'ctx', pairs)  4.88 us
    ppermute x4, waiting for transfers between devices, over_dp(): return lax.ppermute(array, 'dp', [(d, d ^ flip) for d in range(dp_count)])  4.1 us
    ppermute x4, starting transfers between devices, over_dp(): return lax.ppermute(array, 'dp', [(d, d ^ flip) for d in range(dp_count)])  3.33 us
    ppermute x3, waiting for transfers between devices, spread(): return lax.ppermute(array, 'ctx', pairs)  2.63 us
    ppermute x3, waiting for transfers between devices, gathered(): return lax.ppermute(array, ('dp', 'ctx'), pairs)  1.05 us
  transfers between devices with their start and end apart: 13, of which 8 were waited for; matrix products, arithmetic and copies ran while one was open for 0% of the time, Pallas kernels for 21%

profile of v4, /device:TPU:0, one launch (start us, length us, event | category | flops | bytes accessed | tf_op | source)
XLA Modules:
  0.0 36.5 jit_solution(1596249434741716476)
XLA Ops:
  0.6 0.9 %load_first.1.refs_0_ = bf16[256,256]{1,0:T(8,128)(2,1)S(1)} custom-call(bf16[256,128]{1,0:T(8,128)(2,1)} %k_hbm.3, bf16[256,128]{1,0:T(8,128)(2,1)} %v_hbm.3), custom_call_target="tpu_custom_call" | custom-call | bytes 131072 | tf_op jit(solution)/shard_map/load_first/pallas_call | solution.py:408
  1.6 5.1 %collective-permute-start = (bf16[256,256]{1,0:T(8,128)(2,1)S(1)}, bf16[256,256]{1,0:T(8,128)(2,1)S(1)}, u32[]{:S(2)}, u32[]{:S(2)}) collective-permute-start(bf16[256,256]{1,0:T(8,128)(2,1)S(1)} %load_first.1.refs_0_), channel_id=1, source_target_pairs={{8,2},{0,4},{10,12},{9,3},{1,5},{11,13},{24,18},{16,20},{26,28},{2... | collective-permute-start | bytes 393224 | tf_op jit(solution)/shard_map/ppermute | solution.py:440
  6.7 0.9 %load.1.refs_0_ = bf16[256,256]{1,0:T(8,128)(2,1)S(1)} custom-call(bf16[256,128]{1,0:T(8,128)(2,1)} %k_hbm.3, bf16[256,128]{1,0:T(8,128)(2,1)} %v_hbm.3, bf16[256,256]{1,0:T(8,128)(2,1)S(1)} %load_first.1.refs_0_), custom_call_target="tpu_custom_call" | custom-call | bytes 131072 | tf_op jit(solution)/shard_map/load/pallas_call | solution.py:408
  7.6 0.7 %collective-permute-start.3 = (bf16[256,256]{1,0:T(8,128)(2,1)S(1)}, bf16[256,256]{1,0:T(8,128)(2,1)S(1)}, u32[]{:S(2)}, u32[]{:S(2)}) collective-permute-start(bf16[256,256]{1,0:T(8,128)(2,1)S(1)} %load.1.refs_0_), channel_id=1, source_target_pairs={{4,6},{13,7},{20,22},{29,23}} | collective-permute-start | bytes 393224 | tf_op jit(solution)/shard_map/ppermute | solution.py:440
  8.3 2.3 %collective-permute-start.1 = (bf16[256,256]{1,0:T(8,128)(2,1)S(1)}, bf16[256,256]{1,0:T(8,128)(2,1)S(1)}, u32[]{:S(2)}, u32[]{:S(2)}) collective-permute-start(bf16[256,256]{1,0:T(8,128)(2,1)S(1)} %load.1.refs_0_), channel_id=1, source_target_pairs={{0,6},{10,14},{1,7},{11,15},{16,22},{26,30},{17,23},{27,31}} | collective-permute-start | bytes 393224 | tf_op jit(solution)/shard_map/ppermute | solution.py:440
  10.6 1.5 %prepare.1 = (bf16[256,512]{1,0:T(8,128)(2,1)S(1)}, bf16[256,512]{1,0:T(8,128)(2,1)S(1)}, bf16[512,256]{1,0:T(8,128)(2,1)S(1)}, f32[1024,256]{1,0:T(8,128)S(1)}, f32[8,128]{1,0:T(8,128)S(1)}) custom-call(s32[16,128]{1,0:T(8,128)} %bitcast.1, bf16[256,1024]{1,0:T(8,128)(2,1)} %q_hbm.1, bf16[256,1024]{1,0:T(8,128)(2,1)} %g_hbm.1), custom_call_target="tpu_custom_call" | custom-call | flops 268435456 | bytes 1312768 | tf_op jit(solution)/shard_map/prepare/pallas_call | solution.py:408
  12.1 0.0 collective-permute-done.refs_0_.array_ref.refs_1_
  12.1 0.0 collective-permute-done.3.refs_2_
  12.2 0.1 collective-permute-start.4
  12.3 1.0 %collective-permute-done.1.refs_1_ = bf16[256,256]{1,0:T(8,128)(2,1)S(1)} collective-permute-done((bf16[256,256]{1,0:T(8,128)(2,1)S(1)}, bf16[256,256]{1,0:T(8,128)(2,1)S(1)}, u32[]{:S(2)}, u32[]{:S(2)}) %collective-permute-start.1) | collective-permute-done | bytes 131104 | tf_op jit(solution)/shard_map/ppermute | solution.py:440
  13.4 0.1 collective-permute-start.2
  13.4 0.2 collective-permute-done.4.refs_1_
  13.6 1.2 %attend_most.1 = (f32[4,768,256]{2,1,0:T(8,128)S(1)}, f32[8,256]{1,0:T(8,128)S(1)}, f32[4,128,256]{2,1,0:T(8,128)S(1)}) custom-call(bf16[256,512]{1,0:T(8,128)(2,1)S(1)} %get-tuple-element.34.q_ref, f32[1024,256]{1,0:T(8,128)S(1)} %get-tuple-element.36.bias_ref, bf16[256,256]{1,0:T(8,128)(2,1)S(1)} %pick.3.refs_0_, ...), custom_call_target="tpu_custom_call" | custom-call | flops 536870912 | bytes 1839104 | tf_op jit(solution)/shard_map/attend_most/pallas_call | solution.py:408
  14.8 0.0 collective-permute-done.2.kv_ref.refs_3_
  14.8 0.7 %attend.1 = (f32[12,256]{1,0:T(8,128)S(1)}, f32[4,256,256]{2,1,0:T(8,128)S(1)}, bf16[256,256]{1,0:T(8,128)(2,1)S(1)}, bf16[256,256]{1,0:T(8,128)(2,1)S(1)}) custom-call(bf16[256,512]{1,0:T(8,128)(2,1)S(1)} %get-tuple-element.34.q_ref, bf16[512,256]{1,0:T(8,128)(2,1)S(1)} %get-tuple-element.35.gt_ref, f32[1024,256]{1,0:T(8,128)S(1)} %get-tuple-element.36.bias_ref, ...), custom_call_target="tpu_custom_call" | custom-call | flops 268435456 | bytes 792576 | tf_op jit(solution)/shard_map/attend/pallas_call | solution.py:408
  15.5 0.1 collective-permute-start.5
  15.6 0.7 %dprobs.1.refs_6_ = f32[4,1024,256]{2,1,0:T(8,128)S(1)} custom-call(bf16[256,512]{1,0:T(8,128)(2,1)S(1)} %get-tuple-element.44.g_ref, bf16[256,256]{1,0:T(8,128)(2,1)S(1)} %pick.3.refs_0_, bf16[256,256]{1,0:T(8,128)(2,1)S(1)} %collective-permute-done.4.refs_1_, bf16[256,256]{1,0:T(8,128)(2,1)S(1)} %pick.2.refs_2_, ...), custom_call_target="tpu_custom_call" | custom-call | flops 268435456 | bytes 2097152 | tf_op jit(solution)/shard_map/dprobs/pallas_call | solution.py:408
  16.3 3.0 %collective-permute-done.5.refs_1_.refs_8_ = f32[12,256]{1,0:T(8,128)S(1)} collective-permute-done((f32[12,256]{1,0:T(8,128)S(1)}, f32[12,256]{1,0:T(8,128)S(1)}, u32[]{:S(2)}, u32[]{:S(2)}) %collective-permute-start.5) | collective-permute-done | bytes 12320 | tf_op jit(solution)/shard_map/ppermute | solution.py:429
  19.3 1.0 %differentiate_other.1 = (bf16[4,512,256]{2,1,0:T(8,128)(2,1)S(1)}, bf16[512,256]{1,0:T(8,128)(2,1)S(1)}) custom-call(bf16[256,512]{1,0:T(8,128)(2,1)S(1)} %get-tuple-element.34.q_ref, bf16[256,512]{1,0:T(8,128)(2,1)S(1)} %get-tuple-element.44.g_ref, bf16[256,256]{1,0:T(8,128)(2,1)S(1)} %pick.3.refs_0_, bf16[256,256]{1,0:T(8,128)(2,1)S(1)} %collective-permute-done.4.refs_1_, ...), custom_call_target="tpu_custom_call" | custom-call | flops 536870912 | bytes 1310720 | tf_op jit(solution)/shard_map/differentiate_other/pallas_call | solution.py:408
  20.3 0.1 collective-permute-start.7
  20.4 0.1 collective-permute-start.6
  20.4 0.9 %differentiate_own.1 = (bf16[4,512,256]{2,1,0:T(8,128)(2,1)S(1)}, f32[512,256]{1,0:T(8,128)S(1)}) custom-call(bf16[256,512]{1,0:T(8,128)(2,1)S(1)} %get-tuple-element.34.q_ref, bf16[256,512]{1,0:T(8,128)(2,1)S(1)} %get-tuple-element.44.g_ref, bf16[256,256]{1,0:T(8,128)(2,1)S(1)} %pick.3.refs_0_, bf16[256,256]{1,0:T(8,128)(2,1)S(1)} %collective-permute-done.4.refs_1_, ...), custom_call_target="tpu_custom_call" | custom-call | flops 536870912 | bytes 1310720 | tf_op jit(solution)/shard_map/differentiate_own/pallas_call | solution.py:408
  21.4 0.5 %collective-permute-done.7.got_ref = bf16[512,256]{1,0:T(8,128)(2,1)S(1)} collective-permute-done((bf16[512,256]{1,0:T(8,128)(2,1)S(1)}, bf16[512,256]{1,0:T(8,128)(2,1)S(1)}, u32[]{:S(2)}, u32[]{:S(2)}) %collective-permute-start.7) | collective-permute-done | bytes 262176 | tf_op jit(solution)/shard_map/ppermute | solution.py:432
  21.9 0.1 join_cores.1
  22.0 1.6 %collective-permute-start.9 = (bf16[256,256]{1,0:T(8,128)(2,1)S(1)}, bf16[256,256]{1,0:T(8,128)(2,1)S(1)}, u32[]{:S(2)}, u32[]{:S(2)}) collective-permute-start(bf16[256,256]{1,0:T(8,128)(2,1)S(1)} %get-tuple-element.56), channel_id=1, source_target_pairs={{0,16},{8,24},{16,0},{24,8},{1,17},{9,25},{17,1},{25,9},{2,18},{10... | collective-permute-start | bytes 393224 | tf_op jit(solution)/shard_map/ppermute | solution.py:429
  23.5 0.5 %query_terms.1 = (bf16[256,256]{1,0:T(8,128)(2,1)S(1)}, bf16[256,256]{1,0:T(8,128)(2,1)S(1)}) custom-call(bf16[256,256]{1,0:T(8,128)(2,1)S(1)} %pick.3.refs_0_, bf16[256,256]{1,0:T(8,128)(2,1)S(1)} %collective-permute-done.4.refs_1_, bf16[256,256]{1,0:T(8,128)(2,1)S(1)} %pick.2.refs_2_, bf16[256,256]{1,0:T(8,128)(2,1)S(1)} %collective-permute-done.2.kv_ref.refs_3_, ...), custom_call_target="tpu_custom_call" | custom-call | flops 268435456 | bytes 262144 | tf_op jit(solution)/shard_map/query_terms/pallas_call | solution.py:408
  24.1 1.6 %collective-permute-start.8 = (bf16[256,256]{1,0:T(8,128)(2,1)S(1)}, bf16[256,256]{1,0:T(8,128)(2,1)S(1)}, u32[]{:S(2)}, u32[]{:S(2)}) collective-permute-start(bf16[256,256]{1,0:T(8,128)(2,1)S(1)} %get-tuple-element.53), channel_id=1, source_target_pairs={{0,8},{8,0},{16,24},{24,16},{1,9},{9,1},{17,25},{25,17},{2,10},{10... | collective-permute-start | bytes 393224 | tf_op jit(solution)/shard_map/ppermute | solution.py:429
  25.7 0.6 %collective-permute-done.6.refs_3_ = bf16[256,256]{1,0:T(8,128)(2,1)S(1)} collective-permute-done((bf16[256,256]{1,0:T(8,128)(2,1)S(1)}, bf16[256,256]{1,0:T(8,128)(2,1)S(1)}, u32[]{:S(2)}, u32[]{:S(2)}) %collective-permute-start.6) | collective-permute-done | bytes 131104 | tf_op jit(solution)/shard_map/ppermute | solution.py:429
  26.3 0.8 %finish_out.1 = (bf16[256,256]{1,0:T(8,128)(2,1)}, f32[8,128]{1,0:T(8,128)S(1)}) custom-call(f32[12,256]{1,0:T(8,128)S(1)} %get-tuple-element.40.refs_0_.refs_7_, f32[12,256]{1,0:T(8,128)S(1)} %collective-permute-done.5.refs_1_.refs_8_, bf16[256,256]{1,0:T(8,128)(2,1)S(1)} %get-tuple-element.41.refs_2_, bf16[256,256]{1,0:T(8,128)(2,1)S(1)} %collective-permute-done.6.refs_3_), custom_call_target="tpu_custom_call" | custom-call | bytes 133120 | tf_op jit(solution)/shard_map/finish_out/pallas_call | solution.py:408
  27.1 0.5 %collective-permute-done.9.got_ref = bf16[256,256]{1,0:T(8,128)(2,1)S(1)} collective-permute-done((bf16[256,256]{1,0:T(8,128)(2,1)S(1)}, bf16[256,256]{1,0:T(8,128)(2,1)S(1)}, u32[]{:S(2)}, u32[]{:S(2)}) %collective-permute-start.9) | collective-permute-done | bytes 131104 | tf_op jit(solution)/shard_map/ppermute | solution.py:429
  27.6 0.8 %collective-permute-start.10 = (bf16[64,256]{1,0:T(8,128)(2,1)S(1)}, bf16[64,256]{1,0:T(8,128)(2,1)S(1)}, u32[]{:S(2)}, u32[]{:S(2)}) collective-permute-start(bf16[64,256]{1,0:T(8,128)(2,1)S(1)} %get-tuple-element.59), channel_id=1, source_target_pairs={{0,4},{1,5},{2,6},{3,7},{4,0},{5,1},{6,2},{7,3},{8,12},{9,13},{10,... | collective-permute-start | bytes 98312 | tf_op jit(solution)/shard_map/ppermute | solution.py:444
  28.4 3.6 %collective-permute-start.11 = (bf16[64,256]{1,0:T(8,128)(2,1)S(1)}, bf16[64,256]{1,0:T(8,128)(2,1)S(1)}, u32[]{:S(2)}, u32[]{:S(2)}) collective-permute-start(bf16[64,256]{1,0:T(8,128)(2,1)S(1)} %get-tuple-element.60), channel_id=1, source_target_pairs={{0,6},{1,7},{2,4},{3,5},{4,2},{5,3},{6,0},{7,1},{8,14},{9,15},{10,... | collective-permute-start | bytes 98312 | tf_op jit(solution)/shard_map/ppermute | solution.py:444
  32.0 0.5 %collective-permute-start.12 = (bf16[64,256]{1,0:T(8,128)(2,1)S(1)}, bf16[64,256]{1,0:T(8,128)(2,1)S(1)}, u32[]{:S(2)}, u32[]{:S(2)}) collective-permute-start(bf16[64,256]{1,0:T(8,128)(2,1)S(1)} %get-tuple-element.61), channel_id=1, source_target_pairs={{0,2},{1,3},{2,0},{3,1},{4,6},{5,7},{6,4},{7,5},{8,10},{9,11},{10,... | collective-permute-start | bytes 98312 | tf_op jit(solution)/shard_map/ppermute | solution.py:444
  32.5 0.0 collective-permute-done.8.got_ref
  32.5 0.8 %finish_query.1 = (bf16[256,256]{1,0:T(8,128)(2,1)}, f32[8,128]{1,0:T(8,128)S(1)}) custom-call(bf16[256,256]{1,0:T(8,128)(2,1)S(1)} %get-tuple-element.52.own_ref, bf16[256,256]{1,0:T(8,128)(2,1)S(1)} %collective-permute-done.8.got_ref), custom_call_target="tpu_custom_call" | custom-call | bytes 133120 | tf_op jit(solution)/shard_map/finish_query/pallas_call | solution.py:408
  33.2 0.0 collective-permute-done.10.second_ref
  33.3 1.0 %collective-permute-done.11.second_ref = bf16[64,256]{1,0:T(8,128)(2,1)S(1)} collective-permute-done((bf16[64,256]{1,0:T(8,128)(2,1)S(1)}, bf16[64,256]{1,0:T(8,128)(2,1)S(1)}, u32[]{:S(2)}, u32[]{:S(2)}) %collective-permute-start.11) | collective-permute-done | bytes 32800 | tf_op jit(solution)/shard_map/ppermute | solution.py:444
  34.3 1.6 %collective-permute-done.12.refs_1_ = bf16[64,256]{1,0:T(8,128)(2,1)S(1)} collective-permute-done((bf16[64,256]{1,0:T(8,128)(2,1)S(1)}, bf16[64,256]{1,0:T(8,128)(2,1)S(1)}, u32[]{:S(2)}, u32[]{:S(2)}) %collective-permute-start.12) | collective-permute-done | bytes 32800 | tf_op jit(solution)/shard_map/ppermute | solution.py:444
  35.9 0.6 %finish.1 = (bf16[64,128]{1,0:T(8,128)(2,1)}, bf16[64,128]{1,0:T(8,128)(2,1)}) custom-call(f32[8,128]{1,0:T(8,128)S(1)} %get-tuple-element.55.token_ref, f32[64,256]{1,0:T(8,128)S(1)} %add_terms.3.refs_0_, bf16[64,256]{1,0:T(8,128)(2,1)S(1)} %collective-permute-done.12.refs_1_), custom_call_target="tpu_custom_call" | custom-call | bytes 32768 | tf_op jit(solution)/shard_map/finish/pallas_call | solution.py:408
  (6 shorter events, 0.1 us)
Async XLA Ops:
  1.6 10.6 %collective-permute-start = (bf16[256,256]{1,0:T(8,128)(2,1)S(1)}, bf16[256,256]{1,0:T(8,128)(2,1)S(1)}, u32[]{:S(2)}, u32[]{:S(2)}) collective-permute-start(bf16[256,256]{1,0:T(8,128)(2,1)S(1)} %load_first.1.refs_0_), channel_id=1, source_target_pairs={{8,2},{0,4},{10,12},{9,3},{1,5},{11,13},{24,18},{16,20},{26,28},{2... | collective-permute-start | bytes 393224 | tf_op jit(solution)/shard_map/ppermute | solution.py:440
  7.6 4.5 %collective-permute-start.3 = (bf16[256,256]{1,0:T(8,128)(2,1)S(1)}, bf16[256,256]{1,0:T(8,128)(2,1)S(1)}, u32[]{:S(2)}, u32[]{:S(2)}) collective-permute-start(bf16[256,256]{1,0:T(8,128)(2,1)S(1)} %load.1.refs_0_), channel_id=1, source_target_pairs={{4,6},{13,7},{20,22},{29,23}} | collective-permute-start | bytes 393224 | tf_op jit(solution)/shard_map/ppermute | solution.py:440
  8.3 5.0 %collective-permute-start.1 = (bf16[256,256]{1,0:T(8,128)(2,1)S(1)}, bf16[256,256]{1,0:T(8,128)(2,1)S(1)}, u32[]{:S(2)}, u32[]{:S(2)}) collective-permute-start(bf16[256,256]{1,0:T(8,128)(2,1)S(1)} %load.1.refs_0_), channel_id=1, source_target_pairs={{0,6},{10,14},{1,7},{11,15},{16,22},{26,30},{17,23},{27,31}} | collective-permute-start | bytes 393224 | tf_op jit(solution)/shard_map/ppermute | solution.py:440
  12.2 1.4 %collective-permute-start.4 = (bf16[256,256]{1,0:T(8,128)(2,1)S(1)}, bf16[256,256]{1,0:T(8,128)(2,1)S(1)}, u32[]{:S(2)}, u32[]{:S(2)}) collective-permute-start(bf16[256,256]{1,0:T(8,128)(2,1)S(1)} %pick.3.refs_0_), channel_id=1, source_target_pairs={{0,1},{1,0},{2,3},{3,2},{4,5},{5,4},{6,7},{7,6},{8,9},{9,8},{10,11... | collective-permute-start | bytes 393224 | tf_op jit(solution)/shard_map/ppermute | solution.py:432
  13.4 1.4 %collective-permute-start.2 = (bf16[256,256]{1,0:T(8,128)(2,1)S(1)}, bf16[256,256]{1,0:T(8,128)(2,1)S(1)}, u32[]{:S(2)}, u32[]{:S(2)}) collective-permute-start(bf16[256,256]{1,0:T(8,128)(2,1)S(1)} %pick.2.refs_2_), channel_id=1, source_target_pairs={{0,1},{1,0},{2,3},{3,2},{4,5},{5,4},{6,7},{7,6},{8,9},{9,8},{10,11... | collective-permute-start | bytes 393224 | tf_op jit(solution)/shard_map/ppermute | solution.py:432
  15.5 3.8 %collective-permute-start.5 = (f32[12,256]{1,0:T(8,128)S(1)}, f32[12,256]{1,0:T(8,128)S(1)}, u32[]{:S(2)}, u32[]{:S(2)}) collective-permute-start(f32[12,256]{1,0:T(8,128)S(1)} %get-tuple-element.40.refs_0_.refs_7_), channel_id=1, source_target_pairs={{0,8},{8,0},{16,24},{24,16},{1,9},{9,1},{17,25},{25,17},{2,10},{10... | collective-permute-start | bytes 36872 | tf_op jit(solution)/shard_map/ppermute | solution.py:429
  20.3 1.6 %collective-permute-start.7 = (bf16[512,256]{1,0:T(8,128)(2,1)S(1)}, bf16[512,256]{1,0:T(8,128)(2,1)S(1)}, u32[]{:S(2)}, u32[]{:S(2)}) collective-permute-start(bf16[512,256]{1,0:T(8,128)(2,1)S(1)} %get-tuple-element.50), channel_id=1, source_target_pairs={{0,1},{1,0},{2,3},{3,2},{4,5},{5,4},{6,7},{7,6},{8,9},{9,8},{10,11... | collective-permute-start | bytes 786440 | tf_op jit(solution)/shard_map/ppermute | solution.py:432
  20.4 5.9 %collective-permute-start.6 = (bf16[256,256]{1,0:T(8,128)(2,1)S(1)}, bf16[256,256]{1,0:T(8,128)(2,1)S(1)}, u32[]{:S(2)}, u32[]{:S(2)}) collective-permute-start(bf16[256,256]{1,0:T(8,128)(2,1)S(1)} %get-tuple-element.42), channel_id=1, source_target_pairs={{0,8},{8,0},{16,24},{24,16},{1,9},{9,1},{17,25},{25,17},{2,10},{10... | collective-permute-start | bytes 393224 | tf_op jit(solution)/shard_map/ppermute | solution.py:429
  22.0 5.6 %collective-permute-start.9 = (bf16[256,256]{1,0:T(8,128)(2,1)S(1)}, bf16[256,256]{1,0:T(8,128)(2,1)S(1)}, u32[]{:S(2)}, u32[]{:S(2)}) collective-permute-start(bf16[256,256]{1,0:T(8,128)(2,1)S(1)} %get-tuple-element.56), channel_id=1, source_target_pairs={{0,16},{8,24},{16,0},{24,8},{1,17},{9,25},{17,1},{25,9},{2,18},{10... | collective-permute-start | bytes 393224 | tf_op jit(solution)/shard_map/ppermute | solution.py:429
  24.1 8.4 %collective-permute-start.8 = (bf16[256,256]{1,0:T(8,128)(2,1)S(1)}, bf16[256,256]{1,0:T(8,128)(2,1)S(1)}, u32[]{:S(2)}, u32[]{:S(2)}) collective-permute-start(bf16[256,256]{1,0:T(8,128)(2,1)S(1)} %get-tuple-element.53), channel_id=1, source_target_pairs={{0,8},{8,0},{16,24},{24,16},{1,9},{9,1},{17,25},{25,17},{2,10},{10... | collective-permute-start | bytes 393224 | tf_op jit(solution)/shard_map/ppermute | solution.py:429
  27.6 5.7 %collective-permute-start.10 = (bf16[64,256]{1,0:T(8,128)(2,1)S(1)}, bf16[64,256]{1,0:T(8,128)(2,1)S(1)}, u32[]{:S(2)}, u32[]{:S(2)}) collective-permute-start(bf16[64,256]{1,0:T(8,128)(2,1)S(1)} %get-tuple-element.59), channel_id=1, source_target_pairs={{0,4},{1,5},{2,6},{3,7},{4,0},{5,1},{6,2},{7,3},{8,12},{9,13},{10,... | collective-permute-start | bytes 98312 | tf_op jit(solution)/shard_map/ppermute | solution.py:444
  28.4 5.9 %collective-permute-start.11 = (bf16[64,256]{1,0:T(8,128)(2,1)S(1)}, bf16[64,256]{1,0:T(8,128)(2,1)S(1)}, u32[]{:S(2)}, u32[]{:S(2)}) collective-permute-start(bf16[64,256]{1,0:T(8,128)(2,1)S(1)} %get-tuple-element.60), channel_id=1, source_target_pairs={{0,6},{1,7},{2,4},{3,5},{4,2},{5,3},{6,0},{7,1},{8,14},{9,15},{10,... | collective-permute-start | bytes 98312 | tf_op jit(solution)/shard_map/ppermute | solution.py:444
  32.0 3.9 %collective-permute-start.12 = (bf16[64,256]{1,0:T(8,128)(2,1)S(1)}, bf16[64,256]{1,0:T(8,128)(2,1)S(1)}, u32[]{:S(2)}, u32[]{:S(2)}) collective-permute-start(bf16[64,256]{1,0:T(8,128)(2,1)S(1)} %get-tuple-element.61), channel_id=1, source_target_pairs={{0,2},{1,3},{2,0},{3,1},{4,6},{5,7},{6,4},{7,5},{8,10},{9,11},{10,... | collective-permute-start | bytes 98312 | tf_op jit(solution)/shard_map/ppermute | solution.py:444

commit v5 on v4

--- a/solution.py
+++ b/solution.py
@@ -124,7 +124,7 @@
             out_ref[...] = jnp.zeros_like(out_ref) if choice < 0 else refs[choice][...]
 
 
-def pass_kernel(array_ref, token_ref):
+def pass_kernel(array_ref, after_ref, token_ref):
     token_ref[...] = array_ref[:8, :128]
 
 
@@ -474,9 +474,12 @@
         work=1,
         dims=dims,
     )
-    sent = [own_kv, gathered(first_kv, rounds[0])]
-    sent += [gathered(own_kv, moves) for moves in rounds[1:]]
-    first = call(pass_kernel, [((8, 128), bf16)], sent[1:2], "pass")
+    early = 2 if chips == 4 else 1
+    sent = [own_kv] + [gathered(first_kv, moves) for moves in rounds[:early]]
+    sent += [gathered(own_kv, moves) for moves in rounds[early:]]
+    first = [token]
+    for array in sent[1 : early + 1]:
+        first = call(pass_kernel, [((8, 128), bf16)], [array] + list(first), "pass")
     blocks = []
     for spot in range(chips // 2):
         choices = []

time: 37.1 us -> 38.4 us (1.035)
  starting transfers between devices: 16.5 us -> 17.4 us
  waiting for transfers between devices: 8.46 us -> 8.88 us
    ppermute x3, starting transfers between devices: 4.88 us -> 5.95 us  [spread(): return lax.ppermute(array, 'ctx', pairs)]
    ppermute x3, starting transfers between devices: 8.1 us -> 7.48 us  [gathered(): return lax.ppermute(array, ('dp', 'ctx'), pairs)]
    ppermute x3, waiting for transfers between devices: 0.67 us -> 1.24 us  [over_cores(): return lax.ppermute(array, 'ctx', [(c, c ^ 1) for c in range(ctx_count)])]
    ppermute x3, starting transfers between devices: 0.21 us -> 0.68 us  [over_cores(): return lax.ppermute(array, 'ctx', [(c, c ^ 1) for c in range(ctx_count)])]
    pallas_call x19 -> x20, Pallas kernels: 10.7 us -> 10.7 us  [call(): pl.pallas_call(functools.partial(kernel, **static), out_shape=[jax.ShapeD...]
  transfers between devices with their start and end apart: 13 -> 13, of which waited for: 8 -> 8; matrix products, arithmetic and copies ran while one was open for 0% -> 0% of each run, Pallas kernels for 21% -> 20%
where the time goes in v5:
time: 38.4 us; the launch traced here: 37.8 us
  starting transfers between devices  17.4 us (45%)
  Pallas kernels  10.7 us (28%)
  waiting for transfers between devices  8.88 us (23%)
  between operations  0.82 us (2%)
    pallas_call x20, Pallas kernels, call(): pl.pallas_call(functools.partial(kernel, **static), out_shape=[jax.ShapeD...  10.7 us
    ppermute x3, starting transfers between devices, gathered(): return lax.ppermute(array, ('dp', 'ctx'), pairs)  7.48 us
    ppermute x3, starting transfers between devices, spread(): return lax.ppermute(array, 'ctx', pairs)  5.95 us
    ppermute x4, waiting for transfers between devices, over_dp(): return lax.ppermute(array, 'dp', [(d, d ^ flip) for d in range(dp_count)])  4.12 us
    ppermute x4, starting transfers between devices, over_dp(): return lax.ppermute(array, 'dp', [(d, d ^ flip) for d in range(dp_count)])  3.31 us
    ppermute x3, waiting for transfers between devices, spread(): return lax.ppermute(array, 'ctx', pairs)  2.8 us
    ppermute x3, waiting for transfers between devices, over_cores(): return lax.ppermute(array, 'ctx', [(c, c ^ 1) for c in range(ctx_count)])  1.24 us
  transfers between devices with their start and end apart: 13, of which 8 were waited for; matrix products, arithmetic and copies ran while one was open for 0% of the time, Pallas kernels for 20%

profile of v5, /device:TPU:0, one launch (start us, length us, event | category | flops | bytes accessed | tf_op | source)
XLA Modules:
  0.0 37.8 jit_solution(10178474805176340547)
XLA Ops:
  0.6 0.9 %load_first.1.refs_0_ = bf16[256,256]{1,0:T(8,128)(2,1)S(1)} custom-call(bf16[256,128]{1,0:T(8,128)(2,1)} %k_hbm.3, bf16[256,128]{1,0:T(8,128)(2,1)} %v_hbm.3), custom_call_target="tpu_custom_call" | custom-call | bytes 131072 | tf_op jit(solution)/shard_map/load_first/pallas_call | solution.py:408
  1.6 5.1 %collective-permute-start = (bf16[256,256]{1,0:T(8,128)(2,1)S(1)}, bf16[256,256]{1,0:T(8,128)(2,1)S(1)}, u32[]{:S(2)}, u32[]{:S(2)}) collective-permute-start(bf16[256,256]{1,0:T(8,128)(2,1)S(1)} %load_first.1.refs_0_), channel_id=1, source_target_pairs={{8,2},{0,4},{10,12},{9,3},{1,5},{11,13},{24,18},{16,20},{26,28},{2... | collective-permute-start | bytes 393224 | tf_op jit(solution)/shard_map/ppermute | solution.py:440
  6.7 1.7 %collective-permute-start.1 = (bf16[256,256]{1,0:T(8,128)(2,1)S(1)}, bf16[256,256]{1,0:T(8,128)(2,1)S(1)}, u32[]{:S(2)}, u32[]{:S(2)}) collective-permute-start(bf16[256,256]{1,0:T(8,128)(2,1)S(1)} %load_first.1.refs_0_), channel_id=1, source_target_pairs={{0,6},{10,14},{1,7},{11,15},{16,22},{26,30},{17,23},{27,31}} | collective-permute-start | bytes 393224 | tf_op jit(solution)/shard_map/ppermute | solution.py:440
  8.4 0.9 %load.1.refs_0_ = bf16[256,256]{1,0:T(8,128)(2,1)S(1)} custom-call(bf16[256,128]{1,0:T(8,128)(2,1)} %k_hbm.3, bf16[256,128]{1,0:T(8,128)(2,1)} %v_hbm.3, bf16[256,256]{1,0:T(8,128)(2,1)S(1)} %load_first.1.refs_0_), custom_call_target="tpu_custom_call" | custom-call | bytes 131072 | tf_op jit(solution)/shard_map/load/pallas_call | solution.py:408
  9.3 0.7 %collective-permute-start.3 = (bf16[256,256]{1,0:T(8,128)(2,1)S(1)}, bf16[256,256]{1,0:T(8,128)(2,1)S(1)}, u32[]{:S(2)}, u32[]{:S(2)}) collective-permute-start(bf16[256,256]{1,0:T(8,128)(2,1)S(1)} %load.1.refs_0_), channel_id=1, source_target_pairs={{4,6},{13,7},{20,22},{29,23}} | collective-permute-start | bytes 393224 | tf_op jit(solution)/shard_map/ppermute | solution.py:440
  10.0 1.5 %prepare.1 = (bf16[256,512]{1,0:T(8,128)(2,1)S(1)}, bf16[256,512]{1,0:T(8,128)(2,1)S(1)}, bf16[512,256]{1,0:T(8,128)(2,1)S(1)}, f32[1024,256]{1,0:T(8,128)S(1)}, f32[8,128]{1,0:T(8,128)S(1)}) custom-call(s32[16,128]{1,0:T(8,128)} %bitcast.1, bf16[256,1024]{1,0:T(8,128)(2,1)} %q_hbm.1, bf16[256,1024]{1,0:T(8,128)(2,1)} %g_hbm.1), custom_call_target="tpu_custom_call" | custom-call | flops 268435456 | bytes 1312768 | tf_op jit(solution)/shard_map/prepare/pallas_call | solution.py:408
  11.5 0.0 collective-permute-done.refs_0_.array_ref.refs_1_
  11.5 0.7 %collective-permute-done.1.refs_1_.array_ref = bf16[256,256]{1,0:T(8,128)(2,1)S(1)} collective-permute-done((bf16[256,256]{1,0:T(8,128)(2,1)S(1)}, bf16[256,256]{1,0:T(8,128)(2,1)S(1)}, u32[]{:S(2)}, u32[]{:S(2)}) %collective-permute-start.1) | collective-permute-done | bytes 131104 | tf_op jit(solution)/shard_map/ppermute | solution.py:440
  12.2 0.0 collective-permute-done.3.refs_2_
  12.3 0.1 collective-permute-start.4
  12.4 0.5 %collective-permute-start.2 = (bf16[256,256]{1,0:T(8,128)(2,1)S(1)}, bf16[256,256]{1,0:T(8,128)(2,1)S(1)}, u32[]{:S(2)}, u32[]{:S(2)}) collective-permute-start(bf16[256,256]{1,0:T(8,128)(2,1)S(1)} %pick.2.refs_2_), channel_id=1, source_target_pairs={{0,1},{1,0},{2,3},{3,2},{4,5},{5,4},{6,7},{7,6},{8,9},{9,8},{10,11... | collective-permute-start | bytes 393224 | tf_op jit(solution)/shard_map/ppermute | solution.py:432
  12.9 0.7 %collective-permute-done.4.refs_1_ = bf16[256,256]{1,0:T(8,128)(2,1)S(1)} collective-permute-done((bf16[256,256]{1,0:T(8,128)(2,1)S(1)}, bf16[256,256]{1,0:T(8,128)(2,1)S(1)}, u32[]{:S(2)}, u32[]{:S(2)}) %collective-permute-start.4) | collective-permute-done | bytes 131104 | tf_op jit(solution)/shard_map/ppermute | solution.py:432
  13.7 1.2 %attend_most.1 = (f32[4,768,256]{2,1,0:T(8,128)S(1)}, f32[8,256]{1,0:T(8,128)S(1)}, f32[4,128,256]{2,1,0:T(8,128)S(1)}) custom-call(bf16[256,512]{1,0:T(8,128)(2,1)S(1)} %get-tuple-element.34.q_ref, f32[1024,256]{1,0:T(8,128)S(1)} %get-tuple-element.36.bias_ref, bf16[256,256]{1,0:T(8,128)(2,1)S(1)} %pick.3.refs_0_, ...), custom_call_target="tpu_custom_call" | custom-call | flops 536870912 | bytes 1839104 | tf_op jit(solution)/shard_map/attend_most/pallas_call | solution.py:408
  14.9 0.0 collective-permute-done.2.kv_ref.refs_3_
  14.9 0.7 %attend.1 = (f32[12,256]{1,0:T(8,128)S(1)}, f32[4,256,256]{2,1,0:T(8,128)S(1)}, bf16[256,256]{1,0:T(8,128)(2,1)S(1)}, bf16[256,256]{1,0:T(8,128)(2,1)S(1)}) custom-call(bf16[256,512]{1,0:T(8,128)(2,1)S(1)} %get-tuple-element.34.q_ref, bf16[512,256]{1,0:T(8,128)(2,1)S(1)} %get-tuple-element.35.gt_ref, f32[1024,256]{1,0:T(8,128)S(1)} %get-tuple-element.36.bias_ref, ...), custom_call_target="tpu_custom_call" | custom-call | flops 268435456 | bytes 792576 | tf_op jit(solution)/shard_map/attend/pallas_call | solution.py:408
  15.6 0.1 collective-permute-start.5
  15.7 0.7 %dprobs.1.refs_6_ = f32[4,1024,256]{2,1,0:T(8,128)S(1)} custom-call(bf16[256,512]{1,0:T(8,128)(2,1)S(1)} %get-tuple-element.44.g_ref, bf16[256,256]{1,0:T(8,128)(2,1)S(1)} %pick.3.refs_0_, bf16[256,256]{1,0:T(8,128)(2,1)S(1)} %collective-permute-done.4.refs_1_, bf16[256,256]{1,0:T(8,128)(2,1)S(1)} %pick.2.refs_2_, ...), custom_call_target="tpu_custom_call" | custom-call | flops 268435456 | bytes 2097152 | tf_op jit(solution)/shard_map/dprobs/pallas_call | solution.py:408
  16.4 3.0 %collective-permute-done.5.refs_1_.refs_8_ = f32[12,256]{1,0:T(8,128)S(1)} collective-permute-done((f32[12,256]{1,0:T(8,128)S(1)}, f32[12,256]{1,0:T(8,128)S(1)}, u32[]{:S(2)}, u32[]{:S(2)}) %collective-permute-start.5) | collective-permute-done | bytes 12320 | tf_op jit(solution)/shard_map/ppermute | solution.py:429
  19.4 1.0 %differentiate_other.1 = (bf16[4,512,256]{2,1,0:T(8,128)(2,1)S(1)}, bf16[512,256]{1,0:T(8,128)(2,1)S(1)}) custom-call(bf16[256,512]{1,0:T(8,128)(2,1)S(1)} %get-tuple-element.34.q_ref, bf16[256,512]{1,0:T(8,128)(2,1)S(1)} %get-tuple-element.44.g_ref, bf16[256,256]{1,0:T(8,128)(2,1)S(1)} %pick.3.refs_0_, bf16[256,256]{1,0:T(8,128)(2,1)S(1)} %collective-permute-done.4.refs_1_, ...), custom_call_target="tpu_custom_call" | custom-call | flops 536870912 | bytes 1310720 | tf_op jit(solution)/shard_map/differentiate_other/pallas_call | solution.py:408
  20.3 0.1 collective-permute-start.7
  20.4 0.1 collective-permute-start.6
  20.5 1.0 %differentiate_own.1 = (bf16[4,512,256]{2,1,0:T(8,128)(2,1)S(1)}, f32[512,256]{1,0:T(8,128)S(1)}) custom-call(bf16[256,512]{1,0:T(8,128)(2,1)S(1)} %get-tuple-element.34.q_ref, bf16[256,512]{1,0:T(8,128)(2,1)S(1)} %get-tuple-element.44.g_ref, bf16[256,256]{1,0:T(8,128)(2,1)S(1)} %pick.3.refs_0_, bf16[256,256]{1,0:T(8,128)(2,1)S(1)} %collective-permute-done.4.refs_1_, ...), custom_call_target="tpu_custom_call" | custom-call | flops 536870912 | bytes 1310720 | tf_op jit(solution)/shard_map/differentiate_own/pallas_call | solution.py:408
  21.5 0.5 %collective-permute-done.7.got_ref = bf16[512,256]{1,0:T(8,128)(2,1)S(1)} collective-permute-done((bf16[512,256]{1,0:T(8,128)(2,1)S(1)}, bf16[512,256]{1,0:T(8,128)(2,1)S(1)}, u32[]{:S(2)}, u32[]{:S(2)}) %collective-permute-start.7) | collective-permute-done | bytes 262176 | tf_op jit(solution)/shard_map/ppermute | solution.py:432
  21.9 0.1 join_cores.1
  22.0 1.6 %collective-permute-start.9 = (bf16[256,256]{1,0:T(8,128)(2,1)S(1)}, bf16[256,256]{1,0:T(8,128)(2,1)S(1)}, u32[]{:S(2)}, u32[]{:S(2)}) collective-permute-start(bf16[256,256]{1,0:T(8,128)(2,1)S(1)} %get-tuple-element.56), channel_id=1, source_target_pairs={{0,16},{8,24},{16,0},{24,8},{1,17},{9,25},{17,1},{25,9},{2,18},{10... | collective-permute-start | bytes 393224 | tf_op jit(solution)/shard_map/ppermute | solution.py:429
  23.6 0.5 %query_terms.1 = (bf16[256,256]{1,0:T(8,128)(2,1)S(1)}, bf16[256,256]{1,0:T(8,128)(2,1)S(1)}) custom-call(bf16[256,256]{1,0:T(8,128)(2,1)S(1)} %pick.3.refs_0_, bf16[256,256]{1,0:T(8,128)(2,1)S(1)} %collective-permute-done.4.refs_1_, bf16[256,256]{1,0:T(8,128)(2,1)S(1)} %pick.2.refs_2_, bf16[256,256]{1,0:T(8,128)(2,1)S(1)} %collective-permute-done.2.kv_ref.refs_3_, ...), custom_call_target="tpu_custom_call" | custom-call | flops 268435456 | bytes 262144 | tf_op jit(solution)/shard_map/query_terms/pallas_call | solution.py:408
  24.1 1.6 %collective-permute-start.8 = (bf16[256,256]{1,0:T(8,128)(2,1)S(1)}, bf16[256,256]{1,0:T(8,128)(2,1)S(1)}, u32[]{:S(2)}, u32[]{:S(2)}) collective-permute-start(bf16[256,256]{1,0:T(8,128)(2,1)S(1)} %get-tuple-element.53), channel_id=1, source_target_pairs={{0,8},{8,0},{16,24},{24,16},{1,9},{9,1},{17,25},{25,17},{2,10},{10... | collective-permute-start | bytes 393224 | tf_op jit(solution)/shard_map/ppermute | solution.py:429
  25.7 0.6 %collective-permute-done.6.refs_3_ = bf16[256,256]{1,0:T(8,128)(2,1)S(1)} collective-permute-done((bf16[256,256]{1,0:T(8,128)(2,1)S(1)}, bf16[256,256]{1,0:T(8,128)(2,1)S(1)}, u32[]{:S(2)}, u32[]{:S(2)}) %collective-permute-start.6) | collective-permute-done | bytes 131104 | tf_op jit(solution)/shard_map/ppermute | solution.py:429
  26.3 0.8 %finish_out.1 = (bf16[256,256]{1,0:T(8,128)(2,1)}, f32[8,128]{1,0:T(8,128)S(1)}) custom-call(f32[12,256]{1,0:T(8,128)S(1)} %get-tuple-element.40.refs_0_.refs_7_, f32[12,256]{1,0:T(8,128)S(1)} %collective-permute-done.5.refs_1_.refs_8_, bf16[256,256]{1,0:T(8,128)(2,1)S(1)} %get-tuple-element.41.refs_2_, bf16[256,256]{1,0:T(8,128)(2,1)S(1)} %collective-permute-done.6.refs_3_), custom_call_target="tpu_custom_call" | custom-call | bytes 133120 | tf_op jit(solution)/shard_map/finish_out/pallas_call | solution.py:408
  27.2 0.5 %collective-permute-done.9.got_ref = bf16[256,256]{1,0:T(8,128)(2,1)S(1)} collective-permute-done((bf16[256,256]{1,0:T(8,128)(2,1)S(1)}, bf16[256,256]{1,0:T(8,128)(2,1)S(1)}, u32[]{:S(2)}, u32[]{:S(2)}) %collective-permute-start.9) | collective-permute-done | bytes 131104 | tf_op jit(solution)/shard_map/ppermute | solution.py:429
  27.7 3.5 %collective-permute-start.10 = (bf16[64,256]{1,0:T(8,128)(2,1)S(1)}, bf16[64,256]{1,0:T(8,128)(2,1)S(1)}, u32[]{:S(2)}, u32[]{:S(2)}) collective-permute-start(bf16[64,256]{1,0:T(8,128)(2,1)S(1)} %get-tuple-element.59), channel_id=1, source_target_pairs={{0,4},{1,5},{2,6},{3,7},{4,0},{5,1},{6,2},{7,3},{8,12},{9,13},{10,... | collective-permute-start | bytes 98312 | tf_op jit(solution)/shard_map/ppermute | solution.py:444
  31.1 2.0 %collective-permute-start.11 = (bf16[64,256]{1,0:T(8,128)(2,1)S(1)}, bf16[64,256]{1,0:T(8,128)(2,1)S(1)}, u32[]{:S(2)}, u32[]{:S(2)}) collective-permute-start(bf16[64,256]{1,0:T(8,128)(2,1)S(1)} %get-tuple-element.60), channel_id=1, source_target_pairs={{0,6},{1,7},{2,4},{3,5},{4,2},{5,3},{6,0},{7,1},{8,14},{9,15},{10,... | collective-permute-start | bytes 98312 | tf_op jit(solution)/shard_map/ppermute | solution.py:444
  33.1 0.5 %collective-permute-start.12 = (bf16[64,256]{1,0:T(8,128)(2,1)S(1)}, bf16[64,256]{1,0:T(8,128)(2,1)S(1)}, u32[]{:S(2)}, u32[]{:S(2)}) collective-permute-start(bf16[64,256]{1,0:T(8,128)(2,1)S(1)} %get-tuple-element.61), channel_id=1, source_target_pairs={{0,2},{1,3},{2,0},{3,1},{4,6},{5,7},{6,4},{7,5},{8,10},{9,11},{10,... | collective-permute-start | bytes 98312 | tf_op jit(solution)/shard_map/ppermute | solution.py:444
  33.6 0.0 collective-permute-done.8.got_ref
  33.6 0.8 %finish_query.1 = (bf16[256,256]{1,0:T(8,128)(2,1)}, f32[8,128]{1,0:T(8,128)S(1)}) custom-call(bf16[256,256]{1,0:T(8,128)(2,1)S(1)} %get-tuple-element.52.own_ref, bf16[256,256]{1,0:T(8,128)(2,1)S(1)} %collective-permute-done.8.got_ref), custom_call_target="tpu_custom_call" | custom-call | bytes 133120 | tf_op jit(solution)/shard_map/finish_query/pallas_call | solution.py:408
  34.4 0.0 collective-permute-done.10.second_ref
  34.4 2.5 %collective-permute-done.11.second_ref = bf16[64,256]{1,0:T(8,128)(2,1)S(1)} collective-permute-done((bf16[64,256]{1,0:T(8,128)(2,1)S(1)}, bf16[64,256]{1,0:T(8,128)(2,1)S(1)}, u32[]{:S(2)}, u32[]{:S(2)}) %collective-permute-start.11) | collective-permute-done | bytes 32800 | tf_op jit(solution)/shard_map/ppermute | solution.py:444
  36.9 0.3 collective-permute-done.12.refs_1_
  37.2 0.6 %finish.1 = (bf16[64,128]{1,0:T(8,128)(2,1)}, bf16[64,128]{1,0:T(8,128)(2,1)}) custom-call(f32[8,128]{1,0:T(8,128)S(1)} %get-tuple-element.55.token_ref, f32[64,256]{1,0:T(8,128)S(1)} %add_terms.3.refs_0_, bf16[64,256]{1,0:T(8,128)(2,1)S(1)} %collective-permute-done.12.refs_1_), custom_call_target="tpu_custom_call" | custom-call | bytes 32768 | tf_op jit(solution)/shard_map/finish/pallas_call | solution.py:408
  (7 shorter events, 0.1 us)
Async XLA Ops:
  1.6 9.9 %collective-permute-start = (bf16[256,256]{1,0:T(8,128)(2,1)S(1)}, bf16[256,256]{1,0:T(8,128)(2,1)S(1)}, u32[]{:S(2)}, u32[]{:S(2)}) collective-permute-start(bf16[256,256]{1,0:T(8,128)(2,1)S(1)} %load_first.1.refs_0_), channel_id=1, source_target_pairs={{8,2},{0,4},{10,12},{9,3},{1,5},{11,13},{24,18},{16,20},{26,28},{2... | collective-permute-start | bytes 393224 | tf_op jit(solution)/shard_map/ppermute | solution.py:440
  6.7 5.5 %collective-permute-start.1 = (bf16[256,256]{1,0:T(8,128)(2,1)S(1)}, bf16[256,256]{1,0:T(8,128)(2,1)S(1)}, u32[]{:S(2)}, u32[]{:S(2)}) collective-permute-start(bf16[256,256]{1,0:T(8,128)(2,1)S(1)} %load_first.1.refs_0_), channel_id=1, source_target_pairs={{0,6},{10,14},{1,7},{11,15},{16,22},{26,30},{17,23},{27,31}} | collective-permute-start | bytes 393224 | tf_op jit(solution)/shard_map/ppermute | solution.py:440
  9.3 2.9 %collective-permute-start.3 = (bf16[256,256]{1,0:T(8,128)(2,1)S(1)}, bf16[256,256]{1,0:T(8,128)(2,1)S(1)}, u32[]{:S(2)}, u32[]{:S(2)}) collective-permute-start(bf16[256,256]{1,0:T(8,128)(2,1)S(1)} %load.1.refs_0_), channel_id=1, source_target_pairs={{4,6},{13,7},{20,22},{29,23}} | collective-permute-start | bytes 393224 | tf_op jit(solution)/shard_map/ppermute | solution.py:440
  12.3 1.4 %collective-permute-start.4 = (bf16[256,256]{1,0:T(8,128)(2,1)S(1)}, bf16[256,256]{1,0:T(8,128)(2,1)S(1)}, u32[]{:S(2)}, u32[]{:S(2)}) collective-permute-start(bf16[256,256]{1,0:T(8,128)(2,1)S(1)} %pick.3.refs_0_), channel_id=1, source_target_pairs={{0,1},{1,0},{2,3},{3,2},{4,5},{5,4},{6,7},{7,6},{8,9},{9,8},{10,11... | collective-permute-start | bytes 393224 | tf_op jit(solution)/shard_map/ppermute | solution.py:432
  12.4 2.5 %collective-permute-start.2 = (bf16[256,256]{1,0:T(8,128)(2,1)S(1)}, bf16[256,256]{1,0:T(8,128)(2,1)S(1)}, u32[]{:S(2)}, u32[]{:S(2)}) collective-permute-start(bf16[256,256]{1,0:T(8,128)(2,1)S(1)} %pick.2.refs_2_), channel_id=1, source_target_pairs={{0,1},{1,0},{2,3},{3,2},{4,5},{5,4},{6,7},{7,6},{8,9},{9,8},{10,11... | collective-permute-start | bytes 393224 | tf_op jit(solution)/shard_map/ppermute | solution.py:432
  15.6 3.8 %collective-permute-start.5 = (f32[12,256]{1,0:T(8,128)S(1)}, f32[12,256]{1,0:T(8,128)S(1)}, u32[]{:S(2)}, u32[]{:S(2)}) collective-permute-start(f32[12,256]{1,0:T(8,128)S(1)} %get-tuple-element.40.refs_0_.refs_7_), channel_id=1, source_target_pairs={{0,8},{8,0},{16,24},{24,16},{1,9},{9,1},{17,25},{25,17},{2,10},{10... | collective-permute-start | bytes 36872 | tf_op jit(solution)/shard_map/ppermute | solution.py:429
  20.3 1.6 %collective-permute-start.7 = (bf16[512,256]{1,0:T(8,128)(2,1)S(1)}, bf16[512,256]{1,0:T(8,128)(2,1)S(1)}, u32[]{:S(2)}, u32[]{:S(2)}) collective-permute-start(bf16[512,256]{1,0:T(8,128)(2,1)S(1)} %get-tuple-element.50), channel_id=1, source_target_pairs={{0,1},{1,0},{2,3},{3,2},{4,5},{5,4},{6,7},{7,6},{8,9},{9,8},{10,11... | collective-permute-start | bytes 786440 | tf_op jit(solution)/shard_map/ppermute | solution.py:432
  20.4 5.9 %collective-permute-start.6 = (bf16[256,256]{1,0:T(8,128)(2,1)S(1)}, bf16[256,256]{1,0:T(8,128)(2,1)S(1)}, u32[]{:S(2)}, u32[]{:S(2)}) collective-permute-start(bf16[256,256]{1,0:T(8,128)(2,1)S(1)} %get-tuple-element.42), channel_id=1, source_target_pairs={{0,8},{8,0},{16,24},{24,16},{1,9},{9,1},{17,25},{25,17},{2,10},{10... | collective-permute-start | bytes 393224 | tf_op jit(solution)/shard_map/ppermute | solution.py:429
  22.0 5.6 %collective-permute-start.9 = (bf16[256,256]{1,0:T(8,128)(2,1)S(1)}, bf16[256,256]{1,0:T(8,128)(2,1)S(1)}, u32[]{:S(2)}, u32[]{:S(2)}) collective-permute-start(bf16[256,256]{1,0:T(8,128)(2,1)S(1)} %get-tuple-element.56), channel_id=1, source_target_pairs={{0,16},{8,24},{16,0},{24,8},{1,17},{9,25},{17,1},{25,9},{2,18},{10... | collective-permute-start | bytes 393224 | tf_op jit(solution)/shard_map/ppermute | solution.py:429
  24.1 9.5 %collective-permute-start.8 = (bf16[256,256]{1,0:T(8,128)(2,1)S(1)}, bf16[256,256]{1,0:T(8,128)(2,1)S(1)}, u32[]{:S(2)}, u32[]{:S(2)}) collective-permute-start(bf16[256,256]{1,0:T(8,128)(2,1)S(1)} %get-tuple-element.53), channel_id=1, source_target_pairs={{0,8},{8,0},{16,24},{24,16},{1,9},{9,1},{17,25},{25,17},{2,10},{10... | collective-permute-start | bytes 393224 | tf_op jit(solution)/shard_map/ppermute | solution.py:429
  27.7 6.7 %collective-permute-start.10 = (bf16[64,256]{1,0:T(8,128)(2,1)S(1)}, bf16[64,256]{1,0:T(8,128)(2,1)S(1)}, u32[]{:S(2)}, u32[]{:S(2)}) collective-permute-start(bf16[64,256]{1,0:T(8,128)(2,1)S(1)} %get-tuple-element.59), channel_id=1, source_target_pairs={{0,4},{1,5},{2,6},{3,7},{4,0},{5,1},{6,2},{7,3},{8,12},{9,13},{10,... | collective-permute-start | bytes 98312 | tf_op jit(solution)/shard_map/ppermute | solution.py:444
  31.1 5.7 %collective-permute-start.11 = (bf16[64,256]{1,0:T(8,128)(2,1)S(1)}, bf16[64,256]{1,0:T(8,128)(2,1)S(1)}, u32[]{:S(2)}, u32[]{:S(2)}) collective-permute-start(bf16[64,256]{1,0:T(8,128)(2,1)S(1)} %get-tuple-element.60), channel_id=1, source_target_pairs={{0,6},{1,7},{2,4},{3,5},{4,2},{5,3},{6,0},{7,1},{8,14},{9,15},{10,... | collective-permute-start | bytes 98312 | tf_op jit(solution)/shard_map/ppermute | solution.py:444
  33.1 4.1 %collective-permute-start.12 = (bf16[64,256]{1,0:T(8,128)(2,1)S(1)}, bf16[64,256]{1,0:T(8,128)(2,1)S(1)}, u32[]{:S(2)}, u32[]{:S(2)}) collective-permute-start(bf16[64,256]{1,0:T(8,128)(2,1)S(1)} %get-tuple-element.61), channel_id=1, source_target_pairs={{0,2},{1,3},{2,0},{3,1},{4,6},{5,7},{6,4},{7,5},{8,10},{9,11},{10,... | collective-permute-start | bytes 98312 | tf_op jit(solution)/shard_map/ppermute | solution.py:444
